TPU v7x, 32 devices: a whole 2x2x4 slice. The times are simulated.
32 devices in a mesh: row: 8 (over z, x), col: 4 (over y, core).
Axes of the slice: x: 2, y: 2, z: 4, core: 2. Of those that a mesh axis runs over, the one named last changes fastest.
Arguments:
- panel: float32 [256, 16384], P('col', 'row'), may hold values from -6 to 6
- cauchy: float32 [256, 256], replicated, may hold values from -1 to 1
- refl_v: float32 [2, 128, 256, 128], P(None, 'row'), may hold values from -1 to 1
- block_start: int32 [2], replicated, may hold values from 0 to 127
Outputs:
- eigvec_out: float32 [256, 16384], P('col', 'row')
All inputs are finite; a program needn't handle non-finite values.
Results may differ from a plain program's by a relative error of at most 0.0003.
Values sent between devices are 32-bit elements; how exact they have to be, the bound alone decides.
No kernel may reach another device: no remote copies, remote signals or barrier semaphores. Data moves between devices by JAX's collectives and lax.ppermute only.
A program may use at most 128 MiB of HBM per device.

v0:
```python
import functools

import jax
import jax.numpy as jnp
from jax import lax
from jax.experimental import pallas as pl
from jax.experimental.pallas import tpu as pltpu
from jax.sharding import PartitionSpec as P

F32, BF16 = jnp.float32, jnp.bfloat16
VMEM = pl.BlockSpec(memory_space=pltpu.VMEM)
SMEM = pl.BlockSpec(memory_space=pltpu.SMEM)
NN = (((1,), (0,)), ((), ()))
NT = (((1,), (1,)), ((), ()))
TN = (((0,), (0,)), ((), ()))


def split(value):
    high = value.astype(BF16)
    return high, (value - high.astype(F32)).astype(BF16)


def dot(left, right, dims=NN):
    return lax.dot_general(left, right, dims, preferred_element_type=F32)


def wide(value):
    return jnp.concatenate(split(value), axis=1)


def tall(value):
    terms = [jnp.concatenate([term, term], axis=1) for term in split(value)]
    return jnp.concatenate(terms, axis=0)


def doubled(rows_high, rows_low):
    return jnp.concatenate([rows_high, rows_low], axis=0)


def folded(product):
    half = product.shape[0] // 2
    return product[:half] + product[half:]


def apply(left, high, low):
    if left.shape[1] <= 128:
        return folded(dot(tall(left), doubled(high, low)))
    left_high, left_low = split(left)
    return folded(dot(jnp.concatenate([left_high, left_low], axis=0), high)) + dot(left_high, low)


def times(left, right):
    return apply(left, *split(right))


def eye(rows, columns):
    shape = (rows, columns)
    return lax.broadcasted_iota(jnp.int32, shape, 0) == lax.broadcasted_iota(jnp.int32, shape, 1)


def upper_inverses(grams):
    spread = grams[0].shape[0]
    base = spread // 4
    diagonal = eye(spread, spread)
    above = lax.broadcasted_iota(jnp.int32, (spread, spread), 0) < lax.broadcasted_iota(
        jnp.int32, (spread, spread), 1
    )
    halves = [jnp.where(diagonal, 0.5 * gram, 0.0) for gram in grams]
    columns = [jnp.sum(half, axis=0, keepdims=True) for half in halves]
    scaled = [
        jnp.where(above, gram, 0.0) / jnp.sum(half, axis=1, keepdims=True)
        for gram, half in zip(grams, halves)
    ]

    def owner(size):
        return lax.broadcasted_iota(jnp.int32, (size, spread), 1) // size

    def compact(value, size, row=lambda block: block):
        owns = owner(size)
        result = value[row(0) * size : (row(0) + 1) * size]
        for block in range(1, spread // size):
            at = row(block) * size
            result = jnp.where(owns == block, value[at : at + size], result)
        return result

    def expanded(value, size, row=lambda block: block):
        owns = owner(size)
        masks = [(owns == block).astype(BF16) for block in range(spread // size)]
        terms = []
        for term in split(value):
            rows = [jnp.zeros_like(term)] * (spread // size)
            for block, mask in enumerate(masks):
                if row(block) is not None:
                    rows[row(block)] = term * mask
            terms.append(jnp.concatenate(rows, axis=0))
        return doubled(*terms)

    size = base
    unit = compact(diagonal.astype(F32), size)
    powers = [compact(value, size) for value in scaled]
    results = [unit - power for power in powers]
    rights = [expanded(power, size) for power in powers]
    powers = [folded(dot(tall(power), right)) for power, right in zip(powers, rights)]
    reach = 2
    while reach < size:
        reach *= 2
        rights = [expanded(power, size) for power in powers]
        if reach < size:
            lefts = [jnp.concatenate([r, p], axis=0) for r, p in zip(results, powers)]
        else:
            lefts = results
        products = [folded(dot(tall(left), right)) for left, right in zip(lefts, rights)]
        results = [result + product[:size] for result, product in zip(results, products)]
        if reach < size:
            powers = [product[size:] for product in products]
    while size < spread:
        odd = lax.rem(owner(size), 2) == 1
        edges = [
            jnp.where(odd, compact(value, size, lambda block: block & ~1), 0.0) for value in scaled
        ]
        rights = [expanded(result, size) for result in results]
        products = [folded(dot(tall(edge), right)) for edge, right in zip(edges, rights)]
        rights = [
            expanded(product, size, lambda block: block - 1 if block & 1 else None)
            for product in products
        ]
        products = [folded(dot(tall(result), right)) for result, right in zip(results, rights)]
        results = [
            jnp.concatenate(
                [jnp.where(odd, -product, result), jnp.where(odd, result, 0.0)], axis=0
            )
            for result, product in zip(results, products)
        ]
        size *= 2
    return [result / column for result, column in zip(results, columns)]


def reflect_kernel(
    run, sweep, last_slot, place, source,
    k_high, k_low, q_high, q_low, maps, reach, total, first, last, final,
):
    blocks, double, spread = source.shape[1:]
    limit = last_slot - place[0] * blocks
    pairs = [wide(source[sweep, b]) for b in range(blocks)]
    grams = [dot(pair, pair, TN) for pair in pairs]
    grams = [
        (g[:spread, :spread] + g[spread:, spread:]) + (g[:spread, spread:] + g[spread:, :spread])
        for g in grams
    ]
    triangles = upper_inverses(grams)
    unit = eye(double, double).astype(F32)
    scaled = []
    for b in range(blocks):
        high, low = split(triangles[b])
        right = jnp.concatenate(
            [jnp.concatenate([high, high], axis=1), jnp.concatenate([low, low], axis=1)], axis=0
        )
        product = dot(pairs[b], right, NT)
        scaled.append(product[:, :spread] + product[:, spread:])
    for b in range(blocks):
        product = folded(dot(tall(scaled[b]), pairs[b], NT))
        high, low = split(unit - jnp.where(b <= limit, product, 0.0))
        k_high[b] = high
        k_low[b] = low
    runs = blocks // run
    state, out = [None] * runs, [None] * runs
    for step in range(run):
        for j in range(runs):
            b = j * run + step
            high, low = k_high[b, :spread, :], k_low[b, :spread, :]
            if step == 0:
                both = high.astype(F32) + low.astype(F32)
            else:
                both = apply(state[j], high, low)
            state[j] = both[:, spread:]
            out[j] = both[:, :spread]
            high, low = split(out[j])
            q_high[j, :, step * spread : (step + 1) * spread] = high
            q_low[j, :, step * spread : (step + 1) * spread] = low
            if j == 0 and step < 2:
                first[:, step * spread : (step + 1) * spread] = out[j]
    so_far = state[0]
    for j in range(runs):
        maps[j] = state[j]
        if j:
            reach[j - 1] = so_far
            if j == runs - 1:
                last[...] = out[j]
                final[...] = times(so_far, out[j])
            so_far = times(so_far, state[j])
    total[...] = so_far


def reflect(place, refl_v, sweep, run):
    count, double, spread = refl_v.shape[1:]
    runs = count // run
    last_slot = lax.axis_size("row") * count - 3
    square = jax.ShapeDtypeStruct((spread, spread), F32)
    shapes = [
        jax.ShapeDtypeStruct((count, double, double), BF16),
        jax.ShapeDtypeStruct((count, double, double), BF16),
        jax.ShapeDtypeStruct((runs, spread, run * spread), BF16),
        jax.ShapeDtypeStruct((runs, spread, run * spread), BF16),
        jax.ShapeDtypeStruct((runs, spread, spread), F32),
        jax.ShapeDtypeStruct((runs - 1, spread, spread), F32),
        square,
        jax.ShapeDtypeStruct((spread, 2 * spread), F32),
        square,
        square,
    ]
    return pl.pallas_call(
        functools.partial(reflect_kernel, run, sweep, last_slot),
        out_shape=shapes,
        in_specs=[SMEM, VMEM],
        out_specs=[VMEM] * len(shapes),
        compiler_params=pltpu.CompilerParams(vmem_limit_bytes=16 << 20),
        cost_estimate=pl.CostEstimate(
            flops=count * 500_000_000, bytes_accessed=count * 400_000, transcendentals=0
        ),
    )(place, refl_v)


def merge_kernel(owners, place, cauchy, *refs):
    pieces, (merged, chosen) = refs[:-2], refs[-2:]
    rows, columns = pieces[0].shape
    mine = place[1]
    chosen[...] = rolled(cauchy[...], mine * rows)[:, : chosen.shape[1]]
    left = [
        chosen[pl.ds(pl.multiple_of((mine ^ owner) * rows, rows), rows), :rows] for owner in owners
    ]
    left_high, left_low = split(jnp.concatenate(left, axis=0))
    step = columns // 4
    for part in range(4):
        at = slice(part * step, (part + 1) * step)
        right_high, right_low = split(jnp.concatenate([piece[:, at] for piece in pieces], axis=0))
        merged[:, at] = dot(left_high, right_high, TN) + (
            dot(left_high, right_low, TN) + dot(left_low, right_high, TN)
        )


def shifted(array, by):
    devices = lax.axis_size("row")
    return lax.ppermute(array, "row", [(i, (i + by) % devices) for i in range(devices)])


def swapped(array, axis, distance):
    devices = lax.axis_size(axis)
    return lax.ppermute(array, axis, [(i, i ^ distance) for i in range(devices)])


def merge(place, panel, cauchy, ready):
    rows, columns = panel.shape
    count = lax.axis_size("col")
    pieces, owners = [panel], [0]
    distance = count // 2
    while distance:
        pieces += [swapped(piece, "col", distance) for piece in pieces]
        if owners == [0]:
            pieces[-1] = lax.optimization_barrier((pieces[-1], ready))[0]
        owners += [owner ^ distance for owner in owners]
        distance //= 2
    return whole_call(
        functools.partial(merge_kernel, owners), jax.ShapeDtypeStruct((rows, columns), F32),
        1_000_000_000, [place], [cauchy] + pieces,
        [pltpu.VMEM((cauchy.shape[0], 128 * pl.cdiv(rows, 128)), F32)],
    )


def rolled(value, left):
    width = value.shape[1]
    return pltpu.roll(value, lax.rem(width - left, width), 1)


def chain(first, aligned, k_high, k_low, maps, y_local, joins, state):
    slots, rows, spread = y_local.shape
    runs = maps.shape[0]
    run = slots // runs

    def segment(slot):
        return aligned[:, slot * spread : (slot + 1) * spread]

    carry = [jnp.zeros((rows, spread), F32)] * runs
    carry[0] = jnp.where(first, segment(0), 0.0)
    for step in range(run):
        for j in range(runs):
            slot = j * run + step
            fresh = jnp.concatenate([carry[j], segment(slot + 1)], axis=1)
            both = apply(fresh, k_high[slot], k_low[slot])
            y_local[slot] = both[:, :spread]
            carry[j] = both[:, spread:]
    so_far = carry[0]
    joins[0] = jnp.zeros_like(so_far)
    for j in range(1, runs):
        joins[j] = so_far
        so_far = times(so_far, maps[j]) + carry[j]
    state[...] = so_far


def first_kernel(place, start, k_high, k_low, maps, home, after, y_local, joins, state, head):
    slots, rows, spread = y_local.shape
    offset = start[0]
    head[...] = pltpu.roll(home[:, :spread], lax.rem(spread - offset, spread), 1)
    aligned = rolled(jnp.concatenate([home[...], after[: home.shape[0]]], axis=1), offset)
    chain(place[0] == 0, aligned, k_high, k_low, maps, y_local, joins, state)


def is_upper(place, level):
    return lax.rem(place[0] // (1 << level), 2) == 1


def join_maps_kernel(level, top, place, mine, other, *refs):
    upper = is_upper(place, level)
    if level:
        inner, refs = refs[0], refs[1:]
    if top:
        final, refs = refs[0], refs[1:]
    high, both, inside = refs[:3]
    low = jnp.where(upper, other[...], mine[...])
    high[...] = jnp.where(upper, mine[...], other[...])
    both[...] = times(low, high[...])
    if level:
        inside[...] = jnp.where(upper, times(low, inner[...]), inner[...])
    else:
        inside[...] = jnp.where(upper, low, eye(*low.shape).astype(F32))
    if top:
        refs[3][...] = jnp.where(
            is_upper(place, level + 1), times(inside[...], final[...]), 0.0
        )


def join_states_kernel(level, top, place, mine, other, high, *refs):
    upper = is_upper(place, level)
    if level:
        inner, before, refs = refs[0], refs[1], refs[2:]
    if top:
        tail, final, refs = refs[0], refs[1], refs[2:]
    low = jnp.where(upper, other[...], mine[...])
    refs[0][...] = times(low, high[...]) + jnp.where(upper, mine[...], other[...])
    if level:
        enters = before[...] + jnp.where(upper, times(low, inner[...]), 0.0)
    else:
        enters = jnp.where(upper, low, 0.0)
    refs[1][...] = enters
    if top:
        refs[2][...] = tail[...] + times(enters, final[...])


def join_maps(place, total, final=None):
    levels = lax.axis_size("row").bit_length() - 1
    square = jax.ShapeDtypeStruct(total.shape, F32)
    inside, found, seam = None, [], None
    for level in range(levels - 1):
        top = final is not None and level == levels - 2
        arrays = [total, swapped(total, "row", 1 << level)]
        arrays += ([inside] if level else []) + ([final] if top else [])
        high, total, inside, *seam = whole_call(
            functools.partial(join_maps_kernel, level, top), [square] * (4 if top else 3),
            100_000_000, [place], arrays,
        )
        found.append((high, inside))
    return found, seam


def join_states(place, state, maps, tail=None, final=None):
    levels = len(maps) + 1
    segment = jax.ShapeDtypeStruct(state.shape, F32)
    enters, moved = None, None
    for level in range(levels - 1):
        top = tail is not None and level == levels - 2
        arrays = [state, swapped(state, "row", 1 << level), maps[level][0]]
        arrays += [maps[level - 1][1], enters] if level else []
        arrays += [tail, final] if top else []
        state, enters, *moved = whole_call(
            functools.partial(join_states_kernel, level, top), [segment] * (3 if top else 2),
            50_000_000, [place], arrays,
        )
    return swapped(state, "row", 1 << (levels - 1)), enters, moved


def entering(levels, place, half, inner, before):
    enters = jnp.where(is_upper(place, levels - 1), half[...], 0.0)
    return enters, before[...] + times(enters, inner[...])


def settled(incoming, reach, joins, q_high, q_low, y_local, put):
    runs = joins.shape[0]
    spread = incoming.shape[1]
    run = q_high.shape[2] // spread
    for j in range(runs):
        enters = incoming if j == 0 else joins[j] + times(incoming, reach[j - 1])
        added = apply(enters, q_high[j], q_low[j])
        for step in range(run):
            slot = j * run + step
            put(slot, y_local[slot] + added[:, step * spread : (step + 1) * spread])


def second_kernel(
    levels, place, start, half, inner, before, k_high, k_low, maps, q_high, q_low, reach, joins_in,
    y_in, state_in, total_in, head, y_after, after, final,
    y_local, joins, state, head_out, tail, line,
):
    slots, rows, spread = y_local.shape
    incoming = entering(levels, place, half, inner, before)[1]

    def put(slot, value):
        line[:, (slot + 1) * spread : (slot + 2) * spread] = value

    line[:, :spread] = head[...]
    settled(incoming, reach, joins_in, q_high, q_low, y_in, put)
    leaving = times(incoming, total_in[...]) + state_in[...]
    added = times(leaving, after[rows:])
    for extra in range(2):
        put(slots + extra, y_after[extra] + added[:, extra * spread : (extra + 1) * spread])
    ahead = start[1] - start[0]
    head_out[...] = pltpu.roll(
        line[:, : 2 * spread], lax.rem(4 * spread - ahead, 2 * spread), 1
    )[:, :spread]
    chain(
        place[0] == 0, rolled(line[...], ahead + spread), k_high, k_low, maps, y_local, joins, state
    )
    tail[...] = y_local[slots - 1] + times(joins[joins.shape[0] - 1], final[...])


def final_kernel(
    levels, place, start, half, inner, before, q_high, q_low, reach, joins, y_local, head, tail,
    final, out, line,
):
    spread = head.shape[1]
    earlier, incoming = entering(levels, place, half, inner, before)

    def put(slot, value):
        line[:, (slot + 1) * spread : (slot + 2) * spread] = value

    line[:, :spread] = jnp.where(
        place[0] == 0, head[...], tail[...] + times(earlier, final[...])
    )
    settled(incoming, reach, joins, q_high, q_low, y_local, put)
    out[...] = rolled(line[...], spread - start[1])[:, : out.shape[1]]


def whole_call(kernel, shapes, flops, scalars, arrays, scratch=()):
    return pl.pallas_call(
        kernel,
        out_shape=shapes,
        in_specs=[SMEM] * len(scalars) + [VMEM] * len(arrays),
        out_specs=jax.tree.map(lambda shape: VMEM, shapes),
        scratch_shapes=list(scratch),
        compiler_params=pltpu.CompilerParams(vmem_limit_bytes=8 << 20),
        cost_estimate=pl.CostEstimate(
            flops=flops, bytes_accessed=4_000_000, transcendentals=0
        ),
    )(*scalars, *arrays)


def run_length(slots):
    return next(size for size in (4, 2, 1) if slots % size == 0 and slots // size > 1)


def shards(panel, cauchy, refl_v, block_start):
    rows, columns = panel.shape
    slots, _, spread = refl_v.shape[1:]
    run = run_length(slots)
    levels = lax.axis_size("row").bit_length() - 1
    place = jnp.stack([lax.axis_index("row"), lax.axis_index("col")]).astype(jnp.int32)
    scalars = [place, block_start]
    shape = functools.partial(jax.ShapeDtypeStruct, dtype=F32)
    segment = shape((rows, spread))
    chained = [shape((slots, rows, spread)), shape((slots // run, rows, spread)), segment]

    high1, low1, qh1, ql1, maps1, reach1, total1, first1, _, _ = reflect(place, refl_v, 0, run)
    groups1, _ = join_maps(place, total1)
    high2, low2, qh2, ql2, maps2, reach2, total2, _, last2, final2 = reflect(place, refl_v, 1, run)
    groups2, [seam2] = join_maps(place, total2, final2)
    seam2 = shifted(seam2, 1)

    merged = merge(place, panel, cauchy, total1)
    after = shifted(jnp.concatenate([merged[:, : 2 * spread], first1], axis=0), -1)
    y1, joins1, state1, head1 = whole_call(
        first_kernel, chained + [segment], 3_000_000_000, scalars,
        [high1, low1, maps1, merged, after],
    )
    y_after = shifted(y1[:2], -1)
    half1, enters1, _ = join_states(place, state1, groups1)
    y2, joins2, state2, head2, tail2 = whole_call(
        functools.partial(second_kernel, levels), chained + [segment, segment], 4_000_000_000,
        scalars,
        [half1, groups1[-1][1], enters1, high2, low2, maps2, qh1, ql1, reach1, joins1, y1, state1,
         total1, head1, y_after, after, last2],
        [pltpu.VMEM((rows, columns + 3 * spread), F32)],
    )
    half2, enters2, [tail2] = join_states(place, state2, groups2, tail2, final2)
    tail2 = shifted(tail2, 1)
    return whole_call(
        functools.partial(final_kernel, levels), shape((rows, columns)), 1_000_000_000, scalars,
        [half2, groups2[-1][1], enters2, qh2, ql2, reach2, joins2, y2, head2, tail2, seam2],
        [pltpu.VMEM((rows, columns + spread), F32)],
    )


def solution(mesh):
    placed = (P("col", "row"), P(), P(None, "row", None, None), P())
    return jax.shard_map(
        shards, mesh=mesh, in_specs=placed, out_specs=P("col", "row"), check_vma=False
    )
```

profile of v0, /device:TPU:0, one launch (start us, length us, event | category | flops | bytes accessed | tf_op | source)
XLA Modules:
  0.0 74.9 jit_solution(17386780961140291769)
XLA Ops:
  0.0 3.0 %collective-permute-start = (f32[64,2048]{1,0:T(8,128)}, f32[64,2048]{1,0:T(8,128)S(1)}, u32[]{:S(2)}, u32[]{:S(2)}) collective-permute-start(f32[64,2048]{1,0:T(8,128)} %refs_0_.1), channel_id=1, source_target_pairs={{0,2},{1,3},{2,0},{3,1},{4,6},{5,7},{6,4},{7,5},{8,10},{9,11},{10,... | collective-permute-start | bytes 1572872 | tf_op jit(solution)/shard_map/ppermute | solution.py:248
  3.0 0.0 collective-permute-start.1
  3.0 0.1 pad_add_fusion.place
  3.0 0.0 copy-start
  3.0 2.2 %copy-done = f32[2,16,256,128]{3,2,1,0:T(8,128)S(1)} copy-done((f32[2,16,256,128]{3,2,1,0:T(8,128)S(1)}, f32[2,16,256,128]{3,2,1,0:T(8,128)}, u32[]{:S(2)}) %copy-start) | copy-done | bytes 4194328
  5.2 0.0 copy-start.1
  5.2 0.0 copy-start.2
  5.2 6.9 %shard_map.46 = (bf16[16,256,256]{2,1,0:T(8,128)(2,1)S(1)}, bf16[16,256,256]{2,1,0:T(8,128)(2,1)S(1)}, bf16[4,128,512]{2,1,0:T(8,128)(2,1)S(1)}, bf16[4,128,512]...) custom-call(s32[2]{0:T(128)S(1)} %pad_add_fusion.place, ...), custom_call_target="tpu_custom_call" | custom-call | flops 8000000000 | bytes 6400000 | tf_op jit(solution)/shard_map/pallas_call | solution.py:211
  12.2 2.9 %collective-permute-done.refs_1_ = f32[64,2048]{1,0:T(8,128)S(1)} collective-permute-done((f32[64,2048]{1,0:T(8,128)}, f32[64,2048]{1,0:T(8,128)S(1)}, u32[]{:S(2)}, u32[]{:S(2)}) %collective-permute-start) | collective-permute-done | bytes 524320 | tf_op jit(solution)/shard_map/ppermute | solution.py:248
  15.1 0.0 copy-start.3
  15.1 0.0 collective-permute-start.2
  15.1 0.0 collective-permute-done.1.refs_2_
  15.1 1.9 %collective-permute-done.2.refs_3_ = f32[64,2048]{1,0:T(8,128)S(1)} collective-permute-done((f32[64,2048]{1,0:T(8,128)S(1)}, f32[64,2048]{1,0:T(8,128)S(1)}, u32[]{:S(2)}, u32[]{:S(2)}) %collective-permute-start.2) | collective-permute-done | bytes 524320 | tf_op jit(solution)/shard_map/ppermute | solution.py:248
  17.0 0.0 copy-done.1
  17.0 0.0 copy-done.2
  17.0 1.4 %shard_map.47.home = f32[64,2048]{1,0:T(8,128)S(1)} custom-call(s32[2]{0:T(128)S(1)} %pad_add_fusion.place, f32[256,256]{1,0:T(8,128)S(1)} %copy-done.2, f32[64,2048]{1,0:T(8,128)S(1)} %copy-done.1, f32[64,2048]{1,0:T(8,128)S(1)} %collective-permute-done.refs_1_, f32[64,2048]{1,0:T(8,128)S(1)} %collective-permute-done.1.refs_2_, ...), custom_call_target="tpu_custom_call" | custom-call | flops 1000000000 | bytes 4000000 | tf_op jit(solution)/shard_map/pallas_call | solution.py:442
  18.5 5.0 %collective-permute-start.3 = (f32[192,256]{1,0:T(8,128)S(1)}, f32[192,256]{1,0:T(8,128)S(1)}, u32[]{:S(2)}, u32[]{:S(2)}) collective-permute-start(f32[192,256]{1,0:T(8,128)S(1)} %pad_maximum_fusion), channel_id=1, source_target_pairs={{0,28},{4,0},{8,4},{12,8},{16,12},{20,16},{24,20},{28,24},{1,29},{... | collective-permute-start | bytes 589832 | tf_op jit(solution)/shard_map/ppermute | solution.py:243
  23.5 0.0 collective-permute-start.5
  23.5 4.3 %collective-permute-done.5.other = f32[128,128]{1,0:T(8,128)S(1)} collective-permute-done((f32[128,128]{1,0:T(8,128)S(1)}, f32[128,128]{1,0:T(8,128)S(1)}, u32[]{:S(2)}, u32[]{:S(2)}) %collective-permute-start.5) | collective-permute-done | bytes 65568 | tf_op jit(solution)/shard_map/ppermute | solution.py:248
  27.7 0.7 shard_map.49
  28.5 1.2 %collective-permute-start.7 = (f32[128,128]{1,0:T(8,128)S(1)}, f32[128,128]{1,0:T(8,128)S(1)}, u32[]{:S(2)}, u32[]{:S(2)}) collective-permute-start(f32[128,128]{1,0:T(8,128)S(1)} %get-tuple-element.61.mine), channel_id=1, source_target_pairs={{0,8},{4,12},{8,0},{12,4},{16,24},{20,28},{24,16},{28,20},{1,9},{5... | collective-permute-start | bytes 196616 | tf_op jit(solution)/shard_map/ppermute | solution.py:248
  29.7 0.0 collective-permute-done.3.after
  29.7 0.0 copy-done.3
  29.7 1.9 %shard_map.48 = (f32[16,64,128]{2,1,0:T(8,128)S(1)}, f32[4,64,128]{2,1,0:T(8,128)S(1)}, f32[64,128]{1,0:T(8,128)S(1)}, f32[64,128]{1,0:T(8,128)S(1)}) custom-call(s32[2]{0:T(128)S(1)} %pad_add_fusion.place, s32[2]{0:T(128)S(1)} %copy-done.3, bf16[16,256,256]{2,1,0:T(8,128)(2,1)S(1)} %get-tuple-element.52.k_high, ...), custom_call_target="tpu_custom_call" | custom-call | flops 3000000000 | bytes 4000000 | tf_op jit(solution)/shard_map/pallas_call | solution.py:442
  31.6 1.8 %collective-permute-start.4 = (f32[64,128]{1,0:T(8,128)S(1)}, f32[64,128]{1,0:T(8,128)S(1)}, u32[]{:S(2)}, u32[]{:S(2)}) collective-permute-start(f32[64,128]{1,0:T(8,128)S(1)} %get-tuple-element.58.mine.state_in), channel_id=1, source_target_pairs={{0,4},{4,0},{8,12},{12,8},{16,20},{20,16},{24,28},{28,24},{1,5},{5... | collective-permute-start | bytes 98312 | tf_op jit(solution)/shard_map/ppermute | solution.py:248
  33.4 6.8 %shard_map.53 = (bf16[16,256,256]{2,1,0:T(8,128)(2,1)S(1)}, bf16[16,256,256]{2,1,0:T(8,128)(2,1)S(1)}, bf16[4,128,512]{2,1,0:T(8,128)(2,1)S(1)}, bf16[4,128,512]...) custom-call(s32[2]{0:T(128)S(1)} %pad_add_fusion.place, ...), custom_call_target="tpu_custom_call" | custom-call | flops 8000000000 | bytes 6400000 | tf_op jit(solution)/shard_map/pallas_call | solution.py:211
  40.2 0.3 collective-permute-start.11
  40.5 0.0 collective-permute-done.4.other
  40.5 0.7 shard_map.50
  41.2 1.0 %collective-permute-start.6 = (f32[64,128]{1,0:T(8,128)S(1)}, f32[64,128]{1,0:T(8,128)S(1)}, u32[]{:S(2)}, u32[]{:S(2)}) collective-permute-start(f32[64,128]{1,0:T(8,128)S(1)} %get-tuple-element.60.mine), channel_id=1, source_target_pairs={{0,8},{4,12},{8,0},{12,4},{16,24},{20,28},{24,16},{28,20},{1,9},{5... | collective-permute-start | bytes 98312 | tf_op jit(solution)/shard_map/ppermute | solution.py:248
  42.1 2.8 %collective-permute-start.9 = (f32[2,64,128]{2,1,0:T(8,128)S(1)}, f32[2,64,128]{2,1,0:T(8,128)S(1)}, u32[]{:S(2)}, u32[]{:S(2)}) collective-permute-start(f32[2,64,128]{2,1,0:T(8,128)S(1)} %slice.7), channel_id=1, source_target_pairs={{0,28},{4,0},{8,4},{12,8},{16,12},{20,16},{24,20},{28,24},{1,29},{... | collective-permute-start | bytes 196616 | tf_op jit(solution)/shard_map/ppermute | solution.py:243
  45.0 0.0 collective-permute-done.7.other
  45.0 1.4 %shard_map.51 = (f32[128,128]{1,0:T(8,128)S(1)}, f32[128,128]{1,0:T(8,128)}, f32[128,128]{1,0:T(8,128)S(1)}) custom-call(s32[2]{0:T(128)S(1)} %pad_add_fusion.place, f32[128,128]{1,0:T(8,128)S(1)} %get-tuple-element.61.mine, f32[128,128]{1,0:T(8,128)S(1)} %collective-permute-done.7.other, f32[128,128]{1,0:T(8,128)S(1)} %get-tuple-element.62.refs_0_), custom_call_target="tpu_custom_call" | custom-call | flops 100000000 | bytes 4000000 | tf_op jit(solution)/shard_map/pallas_call | solution.py:442
  46.4 0.0 collective-permute-done.6.other
  46.4 0.7 shard_map.52
  47.1 1.4 %collective-permute-start.8 = (f32[64,128]{1,0:T(8,128)S(1)}, f32[64,128]{1,0:T(8,128)S(1)}, u32[]{:S(2)}, u32[]{:S(2)}) collective-permute-start(f32[64,128]{1,0:T(8,128)S(1)} %get-tuple-element.65), channel_id=1, source_target_pairs={{0,16},{4,20},{8,24},{12,28},{16,0},{20,4},{24,8},{28,12},{1,17},{... | collective-permute-start | bytes 98312 | tf_op jit(solution)/shard_map/ppermute | solution.py:248
  48.5 0.0 collective-permute-done.11.other
  48.5 0.7 shard_map.55
  49.3 1.2 %collective-permute-start.13 = (f32[128,128]{1,0:T(8,128)S(1)}, f32[128,128]{1,0:T(8,128)S(1)}, u32[]{:S(2)}, u32[]{:S(2)}) collective-permute-start(f32[128,128]{1,0:T(8,128)S(1)} %get-tuple-element.82.mine), channel_id=1, source_target_pairs={{0,8},{4,12},{8,0},{12,4},{16,24},{20,28},{24,16},{28,20},{1,9},{5... | collective-permute-start | bytes 196616 | tf_op jit(solution)/shard_map/ppermute | solution.py:248
  50.5 0.0 collective-permute-done.9.y_after
  50.5 1.8 %collective-permute-done.8.half = f32[64,128]{1,0:T(8,128)S(1)} collective-permute-done((f32[64,128]{1,0:T(8,128)S(1)}, f32[64,128]{1,0:T(8,128)S(1)}, u32[]{:S(2)}, u32[]{:S(2)}) %collective-permute-start.8) | collective-permute-done | bytes 32800 | tf_op jit(solution)/shard_map/ppermute | solution.py:248
  52.3 2.9 %shard_map.54 = (f32[16,64,128]{2,1,0:T(8,128)S(1)}, f32[4,64,128]{2,1,0:T(8,128)S(1)}, f32[64,128]{1,0:T(8,128)S(1)}, f32[64,128]{1,0:T(8,128)S(1)}, f32[64,128]{1,0:T(8,128)S(1)}) custom-call(s32[2]{0:T(128)S(1)} %pad_add_fusion.place, s32[2]{0:T(128)S(1)} %copy-done.3, f32[64,128]{1,0:T(8,128)S(1)} %collective-permute-done.8.half, ...), custom_call_target="tpu_custom_call" | custom-call | flops 4000000000 | bytes 4000000 | tf_op jit(solution)/shard_map/pallas_call | solution.py:442
  55.2 0.2 collective-permute-start.10
  55.5 3.7 %collective-permute-done.10.other = f32[64,128]{1,0:T(8,128)S(1)} collective-permute-done((f32[64,128]{1,0:T(8,128)S(1)}, f32[64,128]{1,0:T(8,128)S(1)}, u32[]{:S(2)}, u32[]{:S(2)}) %collective-permute-start.10) | collective-permute-done | bytes 32800 | tf_op jit(solution)/shard_map/ppermute | solution.py:248
  59.2 0.7 shard_map.56
  59.9 0.4 collective-permute-start.12
  60.3 0.0 collective-permute-done.13.other
  60.3 1.4 %shard_map.57 = (f32[128,128]{1,0:T(8,128)S(1)}, f32[128,128]{1,0:T(8,128)}, f32[128,128]{1,0:T(8,128)S(1)}, f32[128,128]{1,0:T(8,128)S(1)}) custom-call(s32[2]{0:T(128)S(1)} %pad_add_fusion.place, f32[128,128]{1,0:T(8,128)S(1)} %get-tuple-element.82.mine, f32[128,128]{1,0:T(8,128)S(1)} %collective-permute-done.13.other, ...), custom_call_target="tpu_custom_call" | custom-call | flops 100000000 | bytes 4000000 | tf_op jit(solution)/shard_map/pallas_call | solution.py:442
  61.7 0.9 %collective-permute-start.16 = (f32[128,128]{1,0:T(8,128)S(1)}, f32[128,128]{1,0:T(8,128)S(1)}, u32[]{:S(2)}, u32[]{:S(2)}) collective-permute-start(f32[128,128]{1,0:T(8,128)S(1)} %get-tuple-element.98), channel_id=1, source_target_pairs={{0,4},{4,8},{8,12},{12,16},{16,20},{20,24},{24,28},{28,0},{1,5},{5... | collective-permute-start | bytes 196616 | tf_op jit(solution)/shard_map/ppermute | solution.py:243
  62.7 1.2 %collective-permute-done.12.other = f32[64,128]{1,0:T(8,128)S(1)} collective-permute-done((f32[64,128]{1,0:T(8,128)S(1)}, f32[64,128]{1,0:T(8,128)S(1)}, u32[]{:S(2)}, u32[]{:S(2)}) %collective-permute-start.12) | collective-permute-done | bytes 32800 | tf_op jit(solution)/shard_map/ppermute | solution.py:248
  63.9 0.9 %shard_map.58 = (f32[64,128]{1,0:T(8,128)S(1)}, f32[64,128]{1,0:T(8,128)S(1)}, f32[64,128]{1,0:T(8,128)S(1)}) custom-call(s32[2]{0:T(128)S(1)} %pad_add_fusion.place, f32[64,128]{1,0:T(8,128)S(1)} %get-tuple-element.81.mine, f32[64,128]{1,0:T(8,128)S(1)} %collective-permute-done.12.other, f32[128,128]{1,0:T(8,128)S(1)} %get-tuple-element.85.high, ...), custom_call_target="tpu_custom_call" | custom-call | flops 50000000 | bytes 4000000 | tf_op jit(solution)/shard_map/pallas_call | solution.py:442
  64.8 1.1 %collective-permute-start.14 = (f32[64,128]{1,0:T(8,128)S(1)}, f32[64,128]{1,0:T(8,128)S(1)}, u32[]{:S(2)}, u32[]{:S(2)}) collective-permute-start(f32[64,128]{1,0:T(8,128)S(1)} %get-tuple-element.88), channel_id=1, source_target_pairs={{0,16},{4,20},{8,24},{12,28},{16,0},{20,4},{24,8},{28,12},{1,17},{... | collective-permute-start | bytes 98312 | tf_op jit(solution)/shard_map/ppermute | solution.py:248
  65.9 1.0 %collective-permute-start.15 = (f32[64,128]{1,0:T(8,128)S(1)}, f32[64,128]{1,0:T(8,128)S(1)}, u32[]{:S(2)}, u32[]{:S(2)}) collective-permute-start(f32[64,128]{1,0:T(8,128)S(1)} %get-tuple-element.97), channel_id=1, source_target_pairs={{0,4},{4,8},{8,12},{12,16},{16,20},{20,24},{24,28},{28,0},{1,5},{5... | collective-permute-start | bytes 98312 | tf_op jit(solution)/shard_map/ppermute | solution.py:243
  66.9 1.8 %collective-permute-done.16.final = f32[128,128]{1,0:T(8,128)S(1)} collective-permute-done((f32[128,128]{1,0:T(8,128)S(1)}, f32[128,128]{1,0:T(8,128)S(1)}, u32[]{:S(2)}, u32[]{:S(2)}) %collective-permute-start.16) | collective-permute-done | bytes 65568 | tf_op jit(solution)/shard_map/ppermute | solution.py:243
  68.7 1.0 %collective-permute-done.14.half = f32[64,128]{1,0:T(8,128)S(1)} collective-permute-done((f32[64,128]{1,0:T(8,128)S(1)}, f32[64,128]{1,0:T(8,128)S(1)}, u32[]{:S(2)}, u32[]{:S(2)}) %collective-permute-start.14) | collective-permute-done | bytes 32800 | tf_op jit(solution)/shard_map/ppermute | solution.py:248
  69.8 2.7 %collective-permute-done.15.tail = f32[64,128]{1,0:T(8,128)S(1)} collective-permute-done((f32[64,128]{1,0:T(8,128)S(1)}, f32[64,128]{1,0:T(8,128)S(1)}, u32[]{:S(2)}, u32[]{:S(2)}) %collective-permute-start.15) | collective-permute-done | bytes 32800 | tf_op jit(solution)/shard_map/ppermute | solution.py:243
  72.5 2.4 %shard_map.59 = f32[64,2048]{1,0:T(8,128)} custom-call(s32[2]{0:T(128)S(1)} %pad_add_fusion.place, s32[2]{0:T(128)S(1)} %copy-done.3, f32[64,128]{1,0:T(8,128)S(1)} %collective-permute-done.14.half, f32[128,128]{1,0:T(8,128)S(1)} %get-tuple-element.89.inner, f32[64,128]{1,0:T(8,128)S(1)} %get-tuple-element.90.before, ...), custom_call_target="tpu_custom_call" | custom-call | flops 1000000000 | bytes 4000000 | tf_op jit(solution)/shard_map/pallas_call | solution.py:442
  (3 shorter events, 0.0 us)
Async XLA Ops:
  0.0 15.1 %collective-permute-start = (f32[64,2048]{1,0:T(8,128)}, f32[64,2048]{1,0:T(8,128)S(1)}, u32[]{:S(2)}, u32[]{:S(2)}) collective-permute-start(f32[64,2048]{1,0:T(8,128)} %refs_0_.1), channel_id=1, source_target_pairs={{0,2},{1,3},{2,0},{3,1},{4,6},{5,7},{6,4},{7,5},{8,10},{9,11},{10,... | collective-permute-start | bytes 1572872 | tf_op jit(solution)/shard_map/ppermute | solution.py:248
  3.0 12.1 %collective-permute-start.1 = (f32[64,2048]{1,0:T(8,128)}, f32[64,2048]{1,0:T(8,128)S(1)}, u32[]{:S(2)}, u32[]{:S(2)}) collective-permute-start(f32[64,2048]{1,0:T(8,128)} %refs_0_.1), channel_id=1, source_target_pairs={{0,1},{1,0},{2,3},{3,2},{4,5},{5,4},{6,7},{7,6},{8,9},{9,8},{10,11... | collective-permute-start | bytes 1572872 | tf_op jit(solution)/shard_map/ppermute | solution.py:248
  3.0 2.2 %copy-start = (f32[2,16,256,128]{3,2,1,0:T(8,128)S(1)}, f32[2,16,256,128]{3,2,1,0:T(8,128)}, u32[]{:S(2)}) copy-start(f32[2,16,256,128]{3,2,1,0:T(8,128)} %source.3) | copy-start | bytes 12582916
  5.2 11.8 %copy-start.1 = (f32[64,2048]{1,0:T(8,128)S(1)}, f32[64,2048]{1,0:T(8,128)}, u32[]{:S(2)}) copy-start(f32[64,2048]{1,0:T(8,128)} %refs_0_.1) | copy-start | bytes 1572868
  5.2 11.8 %copy-start.2 = (f32[256,256]{1,0:T(8,128)S(1)}, f32[256,256]{1,0:T(8,128)}, u32[]{:S(2)}) copy-start(f32[256,256]{1,0:T(8,128)} %cauchy.1) | copy-start | bytes 786436
  15.1 14.6 %copy-start.3 = (s32[2]{0:T(128)S(1)}, s32[2]{0:T(128)}, u32[]{:S(2)}) copy-start(s32[2]{0:T(128)} %start.5) | copy-start | bytes 28
  15.1 1.9 %collective-permute-start.2 = (f32[64,2048]{1,0:T(8,128)S(1)}, f32[64,2048]{1,0:T(8,128)S(1)}, u32[]{:S(2)}, u32[]{:S(2)}) collective-permute-start(f32[64,2048]{1,0:T(8,128)S(1)} %collective-permute-done.refs_1_), channel_id=1, source_target_pairs={{0,1},{1,0},{2,3},{3,2},{4,5},{5,4},{6,7},{7,6},{8,9},{9,8},{10,11... | collective-permute-start | bytes 1572872 | tf_op jit(solution)/shard_map/ppermute | solution.py:248
  18.5 11.2 %collective-permute-start.3 = (f32[192,256]{1,0:T(8,128)S(1)}, f32[192,256]{1,0:T(8,128)S(1)}, u32[]{:S(2)}, u32[]{:S(2)}) collective-permute-start(f32[192,256]{1,0:T(8,128)S(1)} %pad_maximum_fusion), channel_id=1, source_target_pairs={{0,28},{4,0},{8,4},{12,8},{16,12},{20,16},{24,20},{28,24},{1,29},{... | collective-permute-start | bytes 589832 | tf_op jit(solution)/shard_map/ppermute | solution.py:243
  23.5 4.3 %collective-permute-start.5 = (f32[128,128]{1,0:T(8,128)S(1)}, f32[128,128]{1,0:T(8,128)S(1)}, u32[]{:S(2)}, u32[]{:S(2)}) collective-permute-start(f32[128,128]{1,0:T(8,128)S(1)} %get-tuple-element.55.mine.total_in), channel_id=1, source_target_pairs={{0,4},{4,0},{8,12},{12,8},{16,20},{20,16},{24,28},{28,24},{1,5},{5... | collective-permute-start | bytes 196616 | tf_op jit(solution)/shard_map/ppermute | solution.py:248
  28.5 16.5 %collective-permute-start.7 = (f32[128,128]{1,0:T(8,128)S(1)}, f32[128,128]{1,0:T(8,128)S(1)}, u32[]{:S(2)}, u32[]{:S(2)}) collective-permute-start(f32[128,128]{1,0:T(8,128)S(1)} %get-tuple-element.61.mine), channel_id=1, source_target_pairs={{0,8},{4,12},{8,0},{12,4},{16,24},{20,28},{24,16},{28,20},{1,9},{5... | collective-permute-start | bytes 196616 | tf_op jit(solution)/shard_map/ppermute | solution.py:248
  31.6 8.9 %collective-permute-start.4 = (f32[64,128]{1,0:T(8,128)S(1)}, f32[64,128]{1,0:T(8,128)S(1)}, u32[]{:S(2)}, u32[]{:S(2)}) collective-permute-start(f32[64,128]{1,0:T(8,128)S(1)} %get-tuple-element.58.mine.state_in), channel_id=1, source_target_pairs={{0,4},{4,0},{8,12},{12,8},{16,20},{20,16},{24,28},{28,24},{1,5},{5... | collective-permute-start | bytes 98312 | tf_op jit(solution)/shard_map/ppermute | solution.py:248
  40.2 8.3 %collective-permute-start.11 = (f32[128,128]{1,0:T(8,128)S(1)}, f32[128,128]{1,0:T(8,128)S(1)}, u32[]{:S(2)}, u32[]{:S(2)}) collective-permute-start(f32[128,128]{1,0:T(8,128)S(1)} %get-tuple-element.79.mine), channel_id=1, source_target_pairs={{0,4},{4,0},{8,12},{12,8},{16,20},{20,16},{24,28},{28,24},{1,5},{5... | collective-permute-start | bytes 196616 | tf_op jit(solution)/shard_map/ppermute | solution.py:248
  41.2 5.2 %collective-permute-start.6 = (f32[64,128]{1,0:T(8,128)S(1)}, f32[64,128]{1,0:T(8,128)S(1)}, u32[]{:S(2)}, u32[]{:S(2)}) collective-permute-start(f32[64,128]{1,0:T(8,128)S(1)} %get-tuple-element.60.mine), channel_id=1, source_target_pairs={{0,8},{4,12},{8,0},{12,4},{16,24},{20,28},{24,16},{28,20},{1,9},{5... | collective-permute-start | bytes 98312 | tf_op jit(solution)/shard_map/ppermute | solution.py:248
  42.1 8.4 %collective-permute-start.9 = (f32[2,64,128]{2,1,0:T(8,128)S(1)}, f32[2,64,128]{2,1,0:T(8,128)S(1)}, u32[]{:S(2)}, u32[]{:S(2)}) collective-permute-start(f32[2,64,128]{2,1,0:T(8,128)S(1)} %slice.7), channel_id=1, source_target_pairs={{0,28},{4,0},{8,4},{12,8},{16,12},{20,16},{24,20},{28,24},{1,29},{... | collective-permute-start | bytes 196616 | tf_op jit(solution)/shard_map/ppermute | solution.py:243
  47.1 5.2 %collective-permute-start.8 = (f32[64,128]{1,0:T(8,128)S(1)}, f32[64,128]{1,0:T(8,128)S(1)}, u32[]{:S(2)}, u32[]{:S(2)}) collective-permute-start(f32[64,128]{1,0:T(8,128)S(1)} %get-tuple-element.65), channel_id=1, source_target_pairs={{0,16},{4,20},{8,24},{12,28},{16,0},{20,4},{24,8},{28,12},{1,17},{... | collective-permute-start | bytes 98312 | tf_op jit(solution)/shard_map/ppermute | solution.py:248
  49.3 11.0 %collective-permute-start.13 = (f32[128,128]{1,0:T(8,128)S(1)}, f32[128,128]{1,0:T(8,128)S(1)}, u32[]{:S(2)}, u32[]{:S(2)}) collective-permute-start(f32[128,128]{1,0:T(8,128)S(1)} %get-tuple-element.82.mine), channel_id=1, source_target_pairs={{0,8},{4,12},{8,0},{12,4},{16,24},{20,28},{24,16},{28,20},{1,9},{5... | collective-permute-start | bytes 196616 | tf_op jit(solution)/shard_map/ppermute | solution.py:248
  55.2 4.0 %collective-permute-start.10 = (f32[64,128]{1,0:T(8,128)S(1)}, f32[64,128]{1,0:T(8,128)S(1)}, u32[]{:S(2)}, u32[]{:S(2)}) collective-permute-start(f32[64,128]{1,0:T(8,128)S(1)} %get-tuple-element.78.mine), channel_id=1, source_target_pairs={{0,4},{4,0},{8,12},{12,8},{16,20},{20,16},{24,28},{28,24},{1,5},{5... | collective-permute-start | bytes 98312 | tf_op jit(solution)/shard_map/ppermute | solution.py:248
  59.9 4.0 %collective-permute-start.12 = (f32[64,128]{1,0:T(8,128)S(1)}, f32[64,128]{1,0:T(8,128)S(1)}, u32[]{:S(2)}, u32[]{:S(2)}) collective-permute-start(f32[64,128]{1,0:T(8,128)S(1)} %get-tuple-element.81.mine), channel_id=1, source_target_pairs={{0,8},{4,12},{8,0},{12,4},{16,24},{20,28},{24,16},{28,20},{1,9},{5... | collective-permute-start | bytes 98312 | tf_op jit(solution)/shard_map/ppermute | solution.py:248
  61.7 7.0 %collective-permute-start.16 = (f32[128,128]{1,0:T(8,128)S(1)}, f32[128,128]{1,0:T(8,128)S(1)}, u32[]{:S(2)}, u32[]{:S(2)}) collective-permute-start(f32[128,128]{1,0:T(8,128)S(1)} %get-tuple-element.98), channel_id=1, source_target_pairs={{0,4},{4,8},{8,12},{12,16},{16,20},{20,24},{24,28},{28,0},{1,5},{5... | collective-permute-start | bytes 196616 | tf_op jit(solution)/shard_map/ppermute | solution.py:243
  64.8 5.0 %collective-permute-start.14 = (f32[64,128]{1,0:T(8,128)S(1)}, f32[64,128]{1,0:T(8,128)S(1)}, u32[]{:S(2)}, u32[]{:S(2)}) collective-permute-start(f32[64,128]{1,0:T(8,128)S(1)} %get-tuple-element.88), channel_id=1, source_target_pairs={{0,16},{4,20},{8,24},{12,28},{16,0},{20,4},{24,8},{28,12},{1,17},{... | collective-permute-start | bytes 98312 | tf_op jit(solution)/shard_map/ppermute | solution.py:248
  65.9 6.6 %collective-permute-start.15 = (f32[64,128]{1,0:T(8,128)S(1)}, f32[64,128]{1,0:T(8,128)S(1)}, u32[]{:S(2)}, u32[]{:S(2)}) collective-permute-start(f32[64,128]{1,0:T(8,128)S(1)} %get-tuple-element.97), channel_id=1, source_target_pairs={{0,4},{4,8},{8,12},{12,16},{16,20},{20,24},{24,28},{28,0},{1,5},{5... | collective-permute-start | bytes 98312 | tf_op jit(solution)/shard_map/ppermute | solution.py:243
where the time goes:
time: 75 us; the launch traced here: 74.9 us
  Pallas kernels  29.6 us (39%)
  waiting for transfers between devices  21.5 us (29%)
  starting transfers between devices  21.4 us (29%)
  local copies, waits for them, and re-layouts  2.21 us (3%)
    ppermute x13, waiting for transfers between devices, swapped(): lax.ppermute(array, axis, [(i, i ^ distance) for i in range(devices)])  16.9 us
    pallas_call x12, Pallas kernels, whole_call(): pl.pallas_call(kernel, out_shape=shapes, in_specs=[SMEM] * len(scalars) +...  15.8 us
    pallas_call x2, Pallas kernels, reflect(): pl.pallas_call(functools.partial(reflect_kernel, run, sweep, last_slot),...  13.7 us
    ppermute x13, starting transfers between devices, swapped(): lax.ppermute(array, axis, [(i, i ^ distance) for i in range(devices)])  11.6 us
    ppermute x4, starting transfers between devices, shifted(): lax.ppermute(array, 'row', [(i, (i + by) % devices) for i in range(device...  9.79 us
    ppermute x4, waiting for transfers between devices, shifted(): lax.ppermute(array, 'row', [(i, (i + by) % devices) for i in range(device...  4.54 us
    unnamed x8, local copies, waits for them, and re-layouts  2.2 us
  transfers between devices with their start and end apart: 17, of which 9 were waited for; matrix products, arithmetic and copies ran while one was open for 0% of the time, Pallas kernels for 34%

commit v1 on v0

--- a/solution.py
+++ b/solution.py
@@ -135,13 +135,14 @@
     return [result / column for result, column in zip(results, columns)]
 
 
-def reflect_kernel(
-    run, sweep, last_slot, place, source,
-    k_high, k_low, q_high, q_low, maps, reach, total, first, last, final,
-):
-    blocks, double, spread = source.shape[1:]
-    limit = last_slot - place[0] * blocks
-    pairs = [wide(source[sweep, b]) for b in range(blocks)]
+def reflect_kernel(run, sweep, part, parts, last_slot, source, *refs):
+    earlier = refs[:part]
+    k_high, k_low, q_high, q_low, maps = refs[part : part + 5]
+    refs = list(refs[part + 5 :])
+    first = refs.pop(0) if part == 0 else None
+    blocks, double, spread = k_high.shape[0], *source.shape[2:]
+    limit = last_slot - lax.axis_index("row") * source.shape[1] - part * blocks
+    pairs = [wide(source[sweep, part * blocks + b]) for b in range(blocks)]
     grams = [dot(pair, pair, TN) for pair in pairs]
     grams = [
         (g[:spread, :spread] + g[spread:, spread:]) + (g[:spread, spread:] + g[spread:, :spread])
@@ -177,53 +178,65 @@
             high, low = split(out[j])
             q_high[j, :, step * spread : (step + 1) * spread] = high
             q_low[j, :, step * spread : (step + 1) * spread] = low
-            if j == 0 and step < 2:
+            if part == 0 and j == 0 and step < 2:
                 first[:, step * spread : (step + 1) * spread] = out[j]
-    so_far = state[0]
     for j in range(runs):
         maps[j] = state[j]
-        if j:
+    if part == parts - 1:
+        reach, total, last, final = refs
+        every = [ref[j] for ref in earlier for j in range(runs)] + state
+        so_far = every[0]
+        for j in range(1, len(every)):
             reach[j - 1] = so_far
-            if j == runs - 1:
-                last[...] = out[j]
-                final[...] = times(so_far, out[j])
-            so_far = times(so_far, state[j])
-    total[...] = so_far
-
-
-def reflect(place, refl_v, sweep, run):
-    count, double, spread = refl_v.shape[1:]
-    runs = count // run
-    last_slot = lax.axis_size("row") * count - 3
-    square = jax.ShapeDtypeStruct((spread, spread), F32)
-    shapes = [
-        jax.ShapeDtypeStruct((count, double, double), BF16),
-        jax.ShapeDtypeStruct((count, double, double), BF16),
-        jax.ShapeDtypeStruct((runs, spread, run * spread), BF16),
-        jax.ShapeDtypeStruct((runs, spread, run * spread), BF16),
-        jax.ShapeDtypeStruct((runs, spread, spread), F32),
-        jax.ShapeDtypeStruct((runs - 1, spread, spread), F32),
-        square,
-        jax.ShapeDtypeStruct((spread, 2 * spread), F32),
-        square,
-        square,
-    ]
-    return pl.pallas_call(
-        functools.partial(reflect_kernel, run, sweep, last_slot),
-        out_shape=shapes,
-        in_specs=[SMEM, VMEM],
-        out_specs=[VMEM] * len(shapes),
-        compiler_params=pltpu.CompilerParams(vmem_limit_bytes=16 << 20),
-        cost_estimate=pl.CostEstimate(
-            flops=count * 500_000_000, bytes_accessed=count * 400_000, transcendentals=0
-        ),
-    )(place, refl_v)
-
-
-def merge_kernel(owners, place, cauchy, *refs):
+            if j == len(every) - 1:
+                last[...] = out[-1]
+                final[...] = times(so_far, out[-1])
+            so_far = times(so_far, every[j])
+        total[...] = so_far
+
+
+class Sweep:
+    def __init__(self, refl_v, sweep, parts, run):
+        self.refl_v, self.sweep, self.parts, self.run = refl_v, sweep, parts, run
+        self.high, self.low, self.q_high, self.q_low, self.maps = [], [], [], [], []
+
+    def part(self):
+        slots, double, spread = self.refl_v.shape[1:]
+        part, count = len(self.maps), slots // self.parts
+        runs = count // self.run
+        shape = jax.ShapeDtypeStruct
+        square = shape((spread, spread), F32)
+        shapes = [shape((count, double, double), BF16)] * 2
+        shapes += [shape((runs, spread, self.run * spread), BF16)] * 2
+        shapes += [shape((runs, spread, spread), F32)]
+        if part == 0:
+            shapes.append(shape((spread, 2 * spread), F32))
+        if part == self.parts - 1:
+            every = slots // self.run
+            shapes += [shape((every - 1, spread, spread), F32), square, square, square]
+        last_slot = lax.axis_size("row") * slots - 3
+        results = whole_call(
+            functools.partial(
+                reflect_kernel, self.run, self.sweep, part, self.parts, last_slot
+            ),
+            shapes, count * 500_000_000, [], [self.refl_v] + self.maps, vmem=16,
+        )
+        for kept, result in zip(
+            (self.high, self.low, self.q_high, self.q_low, self.maps), results[:5]
+        ):
+            kept.append(result)
+        rest = list(results[5:])
+        if part == 0:
+            self.first = rest.pop(0)
+        if part == self.parts - 1:
+            self.reach, self.total, self.last, self.final = rest
+        return results
+
+
+def merge_kernel(owners, cauchy, *refs):
     pieces, (merged, chosen) = refs[:-2], refs[-2:]
     rows, columns = pieces[0].shape
-    mine = place[1]
+    mine = lax.axis_index("col")
     chosen[...] = rolled(cauchy[...], mine * rows)[:, : chosen.shape[1]]
     left = [
         chosen[pl.ds(pl.multiple_of((mine ^ owner) * rows, rows), rows), :rows] for owner in owners
@@ -248,22 +261,8 @@
     return lax.ppermute(array, axis, [(i, i ^ distance) for i in range(devices)])
 
 
-def merge(place, panel, cauchy, ready):
-    rows, columns = panel.shape
-    count = lax.axis_size("col")
-    pieces, owners = [panel], [0]
-    distance = count // 2
-    while distance:
-        pieces += [swapped(piece, "col", distance) for piece in pieces]
-        if owners == [0]:
-            pieces[-1] = lax.optimization_barrier((pieces[-1], ready))[0]
-        owners += [owner ^ distance for owner in owners]
-        distance //= 2
-    return whole_call(
-        functools.partial(merge_kernel, owners), jax.ShapeDtypeStruct((rows, columns), F32),
-        1_000_000_000, [place], [cauchy] + pieces,
-        [pltpu.VMEM((cauchy.shape[0], 128 * pl.cdiv(rows, 128)), F32)],
-    )
+def after_all(array, *others):
+    return lax.optimization_barrier((array, *others))[0]
 
 
 def rolled(value, left):
@@ -271,9 +270,11 @@
     return pltpu.roll(value, lax.rem(width - left, width), 1)
 
 
-def chain(first, aligned, k_high, k_low, maps, y_local, joins, state):
+def chain(first, aligned, parts, k, maps, y_local, joins, state):
     slots, rows, spread = y_local.shape
-    runs = maps.shape[0]
+    per = slots // parts
+    maps = [ref[j] for ref in maps for j in range(ref.shape[0])]
+    runs = len(maps)
     run = slots // runs
 
     def segment(slot):
@@ -285,7 +286,8 @@
         for j in range(runs):
             slot = j * run + step
             fresh = jnp.concatenate([carry[j], segment(slot + 1)], axis=1)
-            both = apply(fresh, k_high[slot], k_low[slot])
+            part, at = slot // per, slot % per
+            both = apply(fresh, k[part][at], k[parts + part][at])
             y_local[slot] = both[:, :spread]
             carry[j] = both[:, spread:]
     so_far = carry[0]
@@ -296,20 +298,23 @@
     state[...] = so_far
 
 
-def first_kernel(place, start, k_high, k_low, maps, home, after, y_local, joins, state, head):
+def first_kernel(parts, start, home, after, *refs):
+    k, maps = refs[: 2 * parts], refs[2 * parts : 3 * parts]
+    y_local, joins, state, head, front = refs[3 * parts :]
     slots, rows, spread = y_local.shape
     offset = start[0]
     head[...] = pltpu.roll(home[:, :spread], lax.rem(spread - offset, spread), 1)
-    aligned = rolled(jnp.concatenate([home[...], after[: home.shape[0]]], axis=1), offset)
-    chain(place[0] == 0, aligned, k_high, k_low, maps, y_local, joins, state)
-
-
-def is_upper(place, level):
-    return lax.rem(place[0] // (1 << level), 2) == 1
-
-
-def join_maps_kernel(level, top, place, mine, other, *refs):
-    upper = is_upper(place, level)
+    aligned = rolled(jnp.concatenate([home[...], after[:rows]], axis=1), offset)
+    chain(lax.axis_index("row") == 0, aligned, parts, k, maps, y_local, joins, state)
+    front[...] = y_local[:2]
+
+
+def is_upper(level):
+    return lax.rem(lax.axis_index("row") // (1 << level), 2) == 1
+
+
+def join_maps_kernel(level, top, mine, other, *refs):
+    upper = is_upper(level)
     if level:
         inner, refs = refs[0], refs[1:]
     if top:
@@ -323,13 +328,11 @@
     else:
         inside[...] = jnp.where(upper, low, eye(*low.shape).astype(F32))
     if top:
-        refs[3][...] = jnp.where(
-            is_upper(place, level + 1), times(inside[...], final[...]), 0.0
-        )
-
-
-def join_states_kernel(level, top, place, mine, other, high, *refs):
-    upper = is_upper(place, level)
+        refs[3][...] = jnp.where(is_upper(level + 1), times(inside[...], final[...]), 0.0)
+
+
+def join_states_kernel(level, top, mine, other, high, *refs):
+    upper = is_upper(level)
     if level:
         inner, before, refs = refs[0], refs[1], refs[2:]
     if top:
@@ -345,7 +348,7 @@
         refs[2][...] = tail[...] + times(enters, final[...])
 
 
-def join_maps(place, total, final=None):
+def join_maps(total, final=None):
     levels = lax.axis_size("row").bit_length() - 1
     square = jax.ShapeDtypeStruct(total.shape, F32)
     inside, found, seam = None, [], None
@@ -355,13 +358,13 @@
         arrays += ([inside] if level else []) + ([final] if top else [])
         high, total, inside, *seam = whole_call(
             functools.partial(join_maps_kernel, level, top), [square] * (4 if top else 3),
-            100_000_000, [place], arrays,
+            100_000_000, [], arrays,
         )
         found.append((high, inside))
     return found, seam
 
 
-def join_states(place, state, maps, tail=None, final=None):
+def join_states(state, maps, tail=None, final=None):
     levels = len(maps) + 1
     segment = jax.ShapeDtypeStruct(state.shape, F32)
     enters, moved = None, None
@@ -372,80 +375,83 @@
         arrays += [tail, final] if top else []
         state, enters, *moved = whole_call(
             functools.partial(join_states_kernel, level, top), [segment] * (3 if top else 2),
-            50_000_000, [place], arrays,
+            50_000_000, [], arrays,
         )
     return swapped(state, "row", 1 << (levels - 1)), enters, moved
 
 
-def entering(levels, place, half, inner, before):
-    enters = jnp.where(is_upper(place, levels - 1), half[...], 0.0)
+def entering(levels, half, inner, before):
+    enters = jnp.where(is_upper(levels - 1), half[...], 0.0)
     return enters, before[...] + times(enters, inner[...])
 
 
-def settled(incoming, reach, joins, q_high, q_low, y_local, put):
-    runs = joins.shape[0]
+def settled(incoming, reach, joins, q, y_local, put):
     spread = incoming.shape[1]
-    run = q_high.shape[2] // spread
-    for j in range(runs):
+    parts = len(q) // 2
+    per, _, width = q[0].shape
+    run = width // spread
+    for j in range(parts * per):
         enters = incoming if j == 0 else joins[j] + times(incoming, reach[j - 1])
-        added = apply(enters, q_high[j], q_low[j])
+        part, at = j // per, j % per
+        added = apply(enters, q[part][at], q[parts + part][at])
         for step in range(run):
             slot = j * run + step
             put(slot, y_local[slot] + added[:, step * spread : (step + 1) * spread])
 
 
 def second_kernel(
-    levels, place, start, half, inner, before, k_high, k_low, maps, q_high, q_low, reach, joins_in,
-    y_in, state_in, total_in, head, y_after, after, final,
-    y_local, joins, state, head_out, tail, line,
+    levels, parts_in, parts, start, half, inner, before, reach, joins_in, y_in, state_in, total_in,
+    head, front, after, final, *refs,
 ):
+    q, refs = refs[: 2 * parts_in], refs[2 * parts_in :]
+    k, maps = refs[: 2 * parts], refs[2 * parts : 3 * parts]
+    y_local, joins, state, head_out, tail, line = refs[3 * parts :]
     slots, rows, spread = y_local.shape
-    incoming = entering(levels, place, half, inner, before)[1]
+    incoming = entering(levels, half, inner, before)[1]
 
     def put(slot, value):
         line[:, (slot + 1) * spread : (slot + 2) * spread] = value
 
     line[:, :spread] = head[...]
-    settled(incoming, reach, joins_in, q_high, q_low, y_in, put)
+    settled(incoming, reach, joins_in, q, y_in, put)
     leaving = times(incoming, total_in[...]) + state_in[...]
     added = times(leaving, after[rows:])
     for extra in range(2):
-        put(slots + extra, y_after[extra] + added[:, extra * spread : (extra + 1) * spread])
+        put(slots + extra, front[extra] + added[:, extra * spread : (extra + 1) * spread])
     ahead = start[1] - start[0]
     head_out[...] = pltpu.roll(
         line[:, : 2 * spread], lax.rem(4 * spread - ahead, 2 * spread), 1
     )[:, :spread]
-    chain(
-        place[0] == 0, rolled(line[...], ahead + spread), k_high, k_low, maps, y_local, joins, state
-    )
+    aligned = rolled(line[...], ahead + spread)
+    chain(lax.axis_index("row") == 0, aligned, parts, k, maps, y_local, joins, state)
     tail[...] = y_local[slots - 1] + times(joins[joins.shape[0] - 1], final[...])
 
 
 def final_kernel(
-    levels, place, start, half, inner, before, q_high, q_low, reach, joins, y_local, head, tail,
-    final, out, line,
+    levels, parts, start, half, inner, before, reach, joins, y_local, head, tail, final, *refs
 ):
+    q, (out, line) = refs[: 2 * parts], refs[2 * parts :]
     spread = head.shape[1]
-    earlier, incoming = entering(levels, place, half, inner, before)
+    earlier, incoming = entering(levels, half, inner, before)
 
     def put(slot, value):
         line[:, (slot + 1) * spread : (slot + 2) * spread] = value
 
     line[:, :spread] = jnp.where(
-        place[0] == 0, head[...], tail[...] + times(earlier, final[...])
-    )
-    settled(incoming, reach, joins, q_high, q_low, y_local, put)
+        lax.axis_index("row") == 0, head[...], tail[...] + times(earlier, final[...])
+    )
+    settled(incoming, reach, joins, q, y_local, put)
     out[...] = rolled(line[...], spread - start[1])[:, : out.shape[1]]
 
 
-def whole_call(kernel, shapes, flops, scalars, arrays, scratch=()):
+def whole_call(kernel, shapes, flops, scalars, arrays, scratch=(), vmem=8):
     return pl.pallas_call(
         kernel,
         out_shape=shapes,
         in_specs=[SMEM] * len(scalars) + [VMEM] * len(arrays),
         out_specs=jax.tree.map(lambda shape: VMEM, shapes),
         scratch_shapes=list(scratch),
-        compiler_params=pltpu.CompilerParams(vmem_limit_bytes=8 << 20),
+        compiler_params=pltpu.CompilerParams(vmem_limit_bytes=vmem << 20),
         cost_estimate=pl.CostEstimate(
             flops=flops, bytes_accessed=4_000_000, transcendentals=0
         ),
@@ -453,7 +459,7 @@
 
 
 def run_length(slots):
-    return next(size for size in (4, 2, 1) if slots % size == 0 and slots // size > 1)
+    return next(size for size in (4, 2, 1) if slots % (2 * size) == 0)
 
 
 def shards(panel, cauchy, refl_v, block_start):
@@ -461,38 +467,57 @@
     slots, _, spread = refl_v.shape[1:]
     run = run_length(slots)
     levels = lax.axis_size("row").bit_length() - 1
-    place = jnp.stack([lax.axis_index("row"), lax.axis_index("col")]).astype(jnp.int32)
-    scalars = [place, block_start]
     shape = functools.partial(jax.ShapeDtypeStruct, dtype=F32)
     segment = shape((rows, spread))
     chained = [shape((slots, rows, spread)), shape((slots // run, rows, spread)), segment]
-
-    high1, low1, qh1, ql1, maps1, reach1, total1, first1, _, _ = reflect(place, refl_v, 0, run)
-    groups1, _ = join_maps(place, total1)
-    high2, low2, qh2, ql2, maps2, reach2, total2, _, last2, final2 = reflect(place, refl_v, 1, run)
-    groups2, [seam2] = join_maps(place, total2, final2)
-    seam2 = shifted(seam2, 1)
-
-    merged = merge(place, panel, cauchy, total1)
-    after = shifted(jnp.concatenate([merged[:, : 2 * spread], first1], axis=0), -1)
-    y1, joins1, state1, head1 = whole_call(
-        first_kernel, chained + [segment], 3_000_000_000, scalars,
-        [high1, low1, maps1, merged, after],
-    )
-    y_after = shifted(y1[:2], -1)
-    half1, enters1, _ = join_states(place, state1, groups1)
-    y2, joins2, state2, head2, tail2 = whole_call(
-        functools.partial(second_kernel, levels), chained + [segment, segment], 4_000_000_000,
-        scalars,
-        [half1, groups1[-1][1], enters1, high2, low2, maps2, qh1, ql1, reach1, joins1, y1, state1,
-         total1, head1, y_after, after, last2],
+    starts = [block_start]
+
+    one = Sweep(refl_v, 0, 1, run)
+    two = Sweep(refl_v, 1, 2, run)
+    count = lax.axis_size("col")
+    pieces, owners = [panel], [0]
+    distance = count // 2
+    while distance:
+        pieces += [swapped(piece, "col", distance) for piece in pieces]
+        if owners == [0]:
+            one.part()
+            pieces[-1] = after_all(pieces[-1], one.total)
+        owners += [owner ^ distance for owner in owners]
+        distance //= 2
+    groups1, _ = join_maps(one.total)
+    two.part()
+    pieces[0] = after_all(pieces[0], two.maps[0], groups1[0][0])
+    merged = whole_call(
+        functools.partial(merge_kernel, owners), shape((rows, columns)),
+        1_000_000_000, [], [cauchy] + pieces,
+        [pltpu.VMEM((cauchy.shape[0], 128 * pl.cdiv(rows, 128)), F32)],
+    )
+    after = shifted(jnp.concatenate([merged[:, : 2 * spread], one.first], axis=0), -1)
+    two.maps[0] = after_all(two.maps[0], merged)
+    two.part()
+    merged = after_all(merged, two.total)
+    y1, joins1, state1, head1, front = whole_call(
+        functools.partial(first_kernel, one.parts), chained + [segment, shape((2, rows, spread))],
+        3_000_000_000, starts, [merged, after] + one.high + one.low + one.maps,
+    )
+    groups2, [seam] = join_maps(two.total, two.final)
+    seam = shifted(seam, 1)
+    front = shifted(front, -1)
+    half1, enters1, _ = join_states(state1, groups1)
+    y2, joins2, state2, head2, tail = whole_call(
+        functools.partial(second_kernel, levels, one.parts, two.parts),
+        chained + [segment, segment], 4_000_000_000, starts,
+        [half1, groups1[-1][1], enters1, one.reach, joins1, y1, state1, one.total, head1, front,
+         after, two.last] + one.q_high + one.q_low + two.high + two.low + two.maps,
         [pltpu.VMEM((rows, columns + 3 * spread), F32)],
     )
-    half2, enters2, [tail2] = join_states(place, state2, groups2, tail2, final2)
-    tail2 = shifted(tail2, 1)
+    half2, enters2, [tail] = join_states(state2, groups2, tail, two.final)
+    tail = shifted(tail, 1)
     return whole_call(
-        functools.partial(final_kernel, levels), shape((rows, columns)), 1_000_000_000, scalars,
-        [half2, groups2[-1][1], enters2, qh2, ql2, reach2, joins2, y2, head2, tail2, seam2],
+        functools.partial(final_kernel, levels, two.parts), shape((rows, columns)), 1_000_000_000,
+        starts,
+        [half2, groups2[-1][1], enters2, two.reach, joins2, y2, head2, tail, seam]
+        + two.q_high + two.q_low,
         [pltpu.VMEM((rows, columns + spread), F32)],
     )
 

time: 75 us -> 69.6 us (0.928)
  Pallas kernels: 29.6 us -> 25.1 us
  waiting for transfers between devices: 21.5 us -> 18.4 us
  starting transfers between devices: 21.4 us -> 23.7 us
    pallas_call x2 -> x0, Pallas kernels: 13.7 us -> none  [reflect(): pl.pallas_call(functools.partial(reflect_kernel, run, sweep, last_slot),...]
    pallas_call x12 -> x15, Pallas kernels: 15.8 us -> 25.1 us  [whole_call(): pl.pallas_call(kernel, out_shape=shapes, in_specs=[SMEM] * len(scalars) +...]
    ppermute x13, waiting for transfers between devices: 16.9 us -> 13.8 us  [swapped(): lax.ppermute(array, axis, [(i, i ^ distance) for i in range(devices)])]
    ppermute x13, starting transfers between devices: 11.6 us -> 14.5 us  [swapped(): lax.ppermute(array, axis, [(i, i ^ distance) for i in range(devices)])]
  transfers between devices with their start and end apart: 17 -> 17, of which waited for: 9 -> 9; matrix products, arithmetic and copies ran while one was open for 0% -> 0% of each run, Pallas kernels for 34% -> 33%
where the time goes in v1:
time: 69.6 us; the launch traced here: 69.5 us
  Pallas kernels  25.1 us (36%)
  starting transfers between devices  23.7 us (34%)
  waiting for transfers between devices  18.4 us (26%)
  local copies, waits for them, and re-layouts  2.21 us (3%)
    pallas_call x15, Pallas kernels, whole_call(): pl.pallas_call(kernel, out_shape=shapes, in_specs=[SMEM] * len(scalars) +...  25.1 us
    ppermute x13, starting transfers between devices, swapped(): lax.ppermute(array, axis, [(i, i ^ distance) for i in range(devices)])  14.5 us
    ppermute x13, waiting for transfers between devices, swapped(): lax.ppermute(array, axis, [(i, i ^ distance) for i in range(devices)])  13.8 us
    ppermute x4, starting transfers between devices, shifted(): lax.ppermute(array, 'row', [(i, (i + by) % devices) for i in range(device...  9.22 us
    ppermute x4, waiting for transfers between devices, shifted(): lax.ppermute(array, 'row', [(i, (i + by) % devices) for i in range(device...  4.56 us
    unnamed x8, local copies, waits for them, and re-layouts  2.2 us
  transfers between devices with their start and end apart: 17, of which 9 were waited for; matrix products, arithmetic and copies ran while one was open for 0% of the time, Pallas kernels for 33%

profile of v1, /device:TPU:0, one launch (start us, length us, event | category | flops | bytes accessed | tf_op | source)
XLA Modules:
  0.0 69.5 jit_solution(8605687302105531783)
XLA Ops:
  0.0 3.0 %collective-permute-start.1 = (f32[64,2048]{1,0:T(8,128)}, f32[64,2048]{1,0:T(8,128)S(1)}, u32[]{:S(2)}, u32[]{:S(2)}) collective-permute-start(f32[64,2048]{1,0:T(8,128)} %refs_0_), channel_id=1, source_target_pairs={{0,2},{1,3},{2,0},{3,1},{4,6},{5,7},{6,4},{7,5},{8,10},{9,11},{10,... | collective-permute-start | bytes 1572872 | tf_op jit(solution)/shard_map/ppermute | solution.py:261
  3.0 0.0 collective-permute-start.2
  3.0 0.0 copy-start
  3.0 2.2 %copy-done = f32[2,16,256,128]{3,2,1,0:T(8,128)S(1)} copy-done((f32[2,16,256,128]{3,2,1,0:T(8,128)S(1)}, f32[2,16,256,128]{3,2,1,0:T(8,128)}, u32[]{:S(2)}) %copy-start) | copy-done | bytes 4194328
  5.2 6.4 %shard_map.47 = (bf16[16,256,256]{2,1,0:T(8,128)(2,1)S(1)}, bf16[16,256,256]{2,1,0:T(8,128)(2,1)S(1)}, bf16[4,128,512]{2,1,0:T(8,128)(2,1)S(1)}, bf16[4,128,512]...) custom-call(f32[2,16,256,128]{3,2,1,0:T(8,128)S(1)} %copy-done), custom_call_target="tpu_custom_call" | custom-call | flops 8000000000 | bytes 4000000 | tf_op jit(solution)/shard_map/pallas_call | solution.py:448
  11.5 3.6 %collective-permute-done.1.refs_1_ = f32[64,2048]{1,0:T(8,128)S(1)} collective-permute-done((f32[64,2048]{1,0:T(8,128)}, f32[64,2048]{1,0:T(8,128)S(1)}, u32[]{:S(2)}, u32[]{:S(2)}) %collective-permute-start.1) | collective-permute-done | bytes 524320 | tf_op jit(solution)/shard_map/ppermute | solution.py:261
  15.1 0.0 copy-start.1
  15.1 0.0 copy-start.2
  15.1 0.0 collective-permute-start.3
  15.1 1.8 %collective-permute-start = (f32[128,128]{1,0:T(8,128)S(1)}, f32[128,128]{1,0:T(8,128)S(1)}, u32[]{:S(2)}, u32[]{:S(2)}) collective-permute-start(f32[128,128]{1,0:T(8,128)S(1)} %get-tuple-element.62.mine.total_in), channel_id=1, source_target_pairs={{0,4},{4,0},{8,12},{12,8},{16,20},{20,16},{24,28},{28,24},{1,5},{5... | collective-permute-start | bytes 196616 | tf_op jit(solution)/shard_map/ppermute | solution.py:261
  16.9 4.0 %shard_map.46 = (bf16[8,256,256]{2,1,0:T(8,128)(2,1)S(1)}, bf16[8,256,256]{2,1,0:T(8,128)(2,1)S(1)}, bf16[2,128,512]{2,1,0:T(8,128)(2,1)S(1)}, bf16[2,128,512]{2...) custom-call(f32[2,16,256,128]{3,2,1,0:T(8,128)S(1)} %copy-done), custom_call_target="tpu_custom_call" | custom-call | flops 4000000000 | bytes 4000000 | tf_op jit(solution)/shard_map/pallas_call | solution.py:448
  20.9 0.0 collective-permute-done.other
  20.9 0.2 shard_map.48
  21.0 1.6 %collective-permute-start.7 = (f32[128,128]{1,0:T(8,128)S(1)}, f32[128,128]{1,0:T(8,128)S(1)}, u32[]{:S(2)}, u32[]{:S(2)}) collective-permute-start(f32[128,128]{1,0:T(8,128)S(1)} %get-tuple-element.75.mine), channel_id=1, source_target_pairs={{0,8},{4,12},{8,0},{12,4},{16,24},{20,28},{24,16},{28,20},{1,9},{5... | collective-permute-start | bytes 196616 | tf_op jit(solution)/shard_map/ppermute | solution.py:261
  22.7 0.0 collective-permute-done.2.refs_2_
  22.7 0.0 collective-permute-done.3.refs_3_
  22.7 0.0 copy-done.1
  22.7 0.0 copy-done.2
  22.7 0.9 %shard_map.49.home = f32[64,2048]{1,0:T(8,128)S(1)} custom-call(f32[256,256]{1,0:T(8,128)S(1)} %copy-done.2, f32[64,2048]{1,0:T(8,128)S(1)} %copy-done.1, f32[64,2048]{1,0:T(8,128)S(1)} %collective-permute-done.1.refs_1_, f32[64,2048]{1,0:T(8,128)S(1)} %collective-permute-done.2.refs_2_, f32[64,2048]{1,0:T(8,128)S(1)} %collective-permute-done.3.refs_3_), custom_call_target="tpu_custom_call" | custom-call | flops 1000000000 | bytes 4000000 | tf_op jit(solution)/shard_map/pallas_call | solution.py:448
  23.6 0.0 copy-start.3
  23.6 2.7 %collective-permute-start.4 = (f32[192,256]{1,0:T(8,128)S(1)}, f32[192,256]{1,0:T(8,128)S(1)}, u32[]{:S(2)}, u32[]{:S(2)}) collective-permute-start(f32[192,256]{1,0:T(8,128)S(1)} %pad_maximum_fusion), channel_id=1, source_target_pairs={{0,28},{4,0},{8,4},{12,8},{16,12},{20,16},{24,20},{28,24},{1,29},{... | collective-permute-start | bytes 589832 | tf_op jit(solution)/shard_map/ppermute | solution.py:256
  26.3 3.9 %shard_map.50 = (bf16[8,256,256]{2,1,0:T(8,128)(2,1)S(1)}, bf16[8,256,256]{2,1,0:T(8,128)(2,1)S(1)}, bf16[2,128,512]{2,1,0:T(8,128)(2,1)S(1)}, bf16[2,128,512]{2...) custom-call(f32[2,16,256,128]{3,2,1,0:T(8,128)S(1)} %copy-done, ...), custom_call_target="tpu_custom_call" | custom-call | flops 4000000000 | bytes 4000000 | tf_op jit(solution)/shard_map/pallas_call | solution.py:448
  30.2 0.4 collective-permute-done.4.after
  30.6 0.0 copy-done.3
  30.6 1.9 %shard_map.51 = (f32[16,64,128]{2,1,0:T(8,128)S(1)}, f32[4,64,128]{2,1,0:T(8,128)S(1)}, f32[64,128]{1,0:T(8,128)S(1)}, f32[64,128]{1,0:T(8,128)S(1)}, f32[2,64,128]{2,1,0:T(8,128)S(1)}) custom-call(s32[2]{0:T(128)S(1)} %copy-done.3, f32[64,2048]{1,0:T(8,128)S(1)} %shard_map.49.home, f32[192,256]{1,0:T(8,128)S(1)} %collective-permute-done.4.after, ...), custom_call_target="tpu_custom_call" | custom-call | flops 3000000000 | bytes 4000000 | tf_op jit(solution)/shard_map/pallas_call | solution.py:448
  32.5 1.5 %collective-permute-start.5 = (f32[64,128]{1,0:T(8,128)S(1)}, f32[64,128]{1,0:T(8,128)S(1)}, u32[]{:S(2)}, u32[]{:S(2)}) collective-permute-start(f32[64,128]{1,0:T(8,128)S(1)} %get-tuple-element.73.mine.state_in), channel_id=1, source_target_pairs={{0,4},{4,0},{8,12},{12,8},{16,20},{20,16},{24,28},{28,24},{1,5},{5... | collective-permute-start | bytes 98312 | tf_op jit(solution)/shard_map/ppermute | solution.py:261
  34.0 0.6 collective-permute-start.11
  34.6 1.9 %collective-permute-done.5.other = f32[64,128]{1,0:T(8,128)S(1)} collective-permute-done((f32[64,128]{1,0:T(8,128)S(1)}, f32[64,128]{1,0:T(8,128)S(1)}, u32[]{:S(2)}, u32[]{:S(2)}) %collective-permute-start.5) | collective-permute-done | bytes 32800 | tf_op jit(solution)/shard_map/ppermute | solution.py:261
  36.4 0.1 shard_map.52
  36.6 1.2 %collective-permute-start.6 = (f32[64,128]{1,0:T(8,128)S(1)}, f32[64,128]{1,0:T(8,128)S(1)}, u32[]{:S(2)}, u32[]{:S(2)}) collective-permute-start(f32[64,128]{1,0:T(8,128)S(1)} %get-tuple-element.74.mine), channel_id=1, source_target_pairs={{0,8},{4,12},{8,0},{12,4},{16,24},{20,28},{24,16},{28,20},{1,9},{5... | collective-permute-start | bytes 98312 | tf_op jit(solution)/shard_map/ppermute | solution.py:261
  37.8 4.1 %collective-permute-start.9 = (f32[2,64,128]{2,1,0:T(8,128)S(1)}, f32[2,64,128]{2,1,0:T(8,128)S(1)}, u32[]{:S(2)}, u32[]{:S(2)}) collective-permute-start(f32[2,64,128]{2,1,0:T(8,128)S(1)} %get-tuple-element.86), channel_id=1, source_target_pairs={{0,28},{4,0},{8,4},{12,8},{16,12},{20,16},{24,20},{28,24},{1,29},{... | collective-permute-start | bytes 196616 | tf_op jit(solution)/shard_map/ppermute | solution.py:256
  41.9 0.0 collective-permute-done.7.other
  41.9 0.9 %shard_map.53 = (f32[128,128]{1,0:T(8,128)S(1)}, f32[128,128]{1,0:T(8,128)}, f32[128,128]{1,0:T(8,128)S(1)}) custom-call(f32[128,128]{1,0:T(8,128)S(1)} %get-tuple-element.75.mine, f32[128,128]{1,0:T(8,128)S(1)} %collective-permute-done.7.other, f32[128,128]{1,0:T(8,128)S(1)} %get-tuple-element.76.refs_0_), custom_call_target="tpu_custom_call" | custom-call | flops 100000000 | bytes 4000000 | tf_op jit(solution)/shard_map/pallas_call | solution.py:448
  42.7 0.0 collective-permute-done.6.other
  42.7 0.2 shard_map.54
  42.9 0.8 %collective-permute-start.8 = (f32[64,128]{1,0:T(8,128)S(1)}, f32[64,128]{1,0:T(8,128)S(1)}, u32[]{:S(2)}, u32[]{:S(2)}) collective-permute-start(f32[64,128]{1,0:T(8,128)S(1)} %get-tuple-element.79), channel_id=1, source_target_pairs={{0,16},{4,20},{8,24},{12,28},{16,0},{20,4},{24,8},{28,12},{1,17},{... | collective-permute-start | bytes 98312 | tf_op jit(solution)/shard_map/ppermute | solution.py:261
  43.8 0.0 collective-permute-done.11.other
  43.8 0.2 shard_map.56
  44.0 2.3 %collective-permute-start.13 = (f32[128,128]{1,0:T(8,128)S(1)}, f32[128,128]{1,0:T(8,128)S(1)}, u32[]{:S(2)}, u32[]{:S(2)}) collective-permute-start(f32[128,128]{1,0:T(8,128)S(1)} %get-tuple-element.98.mine), channel_id=1, source_target_pairs={{0,8},{4,12},{8,0},{12,4},{16,24},{20,28},{24,16},{28,20},{1,9},{5... | collective-permute-start | bytes 196616 | tf_op jit(solution)/shard_map/ppermute | solution.py:261
  46.3 0.0 collective-permute-done.9.front
  46.3 1.5 %collective-permute-done.8.half = f32[64,128]{1,0:T(8,128)S(1)} collective-permute-done((f32[64,128]{1,0:T(8,128)S(1)}, f32[64,128]{1,0:T(8,128)S(1)}, u32[]{:S(2)}, u32[]{:S(2)}) %collective-permute-start.8) | collective-permute-done | bytes 32800 | tf_op jit(solution)/shard_map/ppermute | solution.py:261
  47.8 2.9 %shard_map.55 = (f32[16,64,128]{2,1,0:T(8,128)S(1)}, f32[4,64,128]{2,1,0:T(8,128)S(1)}, f32[64,128]{1,0:T(8,128)S(1)}, f32[64,128]{1,0:T(8,128)S(1)}, f32[64,128]{1,0:T(8,128)S(1)}) custom-call(s32[2]{0:T(128)S(1)} %copy-done.3, f32[64,128]{1,0:T(8,128)S(1)} %collective-permute-done.8.half, f32[128,128]{1,0:T(8,128)S(1)} %get-tuple-element.80.inner, ...), custom_call_target="tpu_custom_call" | custom-call | flops 4000000000 | bytes 4000000 | tf_op jit(solution)/shard_map/pallas_call | solution.py:448
  50.7 0.1 collective-permute-start.10
  50.7 3.9 %collective-permute-done.10.other = f32[64,128]{1,0:T(8,128)S(1)} collective-permute-done((f32[64,128]{1,0:T(8,128)S(1)}, f32[64,128]{1,0:T(8,128)S(1)}, u32[]{:S(2)}, u32[]{:S(2)}) %collective-permute-start.10) | collective-permute-done | bytes 32800 | tf_op jit(solution)/shard_map/ppermute | solution.py:261
  54.6 0.1 shard_map.57
  54.8 0.2 collective-permute-start.12
  55.0 0.0 collective-permute-done.13.other
  55.0 0.9 %shard_map.58 = (f32[128,128]{1,0:T(8,128)S(1)}, f32[128,128]{1,0:T(8,128)}, f32[128,128]{1,0:T(8,128)S(1)}, f32[128,128]{1,0:T(8,128)S(1)}) custom-call(f32[128,128]{1,0:T(8,128)S(1)} %get-tuple-element.98.mine, f32[128,128]{1,0:T(8,128)S(1)} %collective-permute-done.13.other, f32[128,128]{1,0:T(8,128)S(1)} %get-tuple-element.99.refs_0_, ...), custom_call_target="tpu_custom_call" | custom-call | flops 100000000 | bytes 4000000 | tf_op jit(solution)/shard_map/pallas_call | solution.py:448
  55.9 1.3 %collective-permute-start.16 = (f32[128,128]{1,0:T(8,128)S(1)}, f32[128,128]{1,0:T(8,128)S(1)}, u32[]{:S(2)}, u32[]{:S(2)}) collective-permute-start(f32[128,128]{1,0:T(8,128)S(1)} %get-tuple-element.112), channel_id=1, source_target_pairs={{0,4},{4,8},{8,12},{12,16},{16,20},{20,24},{24,28},{28,0},{1,5},{5... | collective-permute-start | bytes 196616 | tf_op jit(solution)/shard_map/ppermute | solution.py:256
  57.2 1.6 %collective-permute-done.12.other = f32[64,128]{1,0:T(8,128)S(1)} collective-permute-done((f32[64,128]{1,0:T(8,128)S(1)}, f32[64,128]{1,0:T(8,128)S(1)}, u32[]{:S(2)}, u32[]{:S(2)}) %collective-permute-start.12) | collective-permute-done | bytes 32800 | tf_op jit(solution)/shard_map/ppermute | solution.py:261
  58.8 0.3 shard_map.59
  59.1 1.4 %collective-permute-start.14 = (f32[64,128]{1,0:T(8,128)S(1)}, f32[64,128]{1,0:T(8,128)S(1)}, u32[]{:S(2)}, u32[]{:S(2)}) collective-permute-start(f32[64,128]{1,0:T(8,128)S(1)} %get-tuple-element.104), channel_id=1, source_target_pairs={{0,16},{4,20},{8,24},{12,28},{16,0},{20,4},{24,8},{28,12},{1,17},{... | collective-permute-start | bytes 98312 | tf_op jit(solution)/shard_map/ppermute | solution.py:261
  60.5 1.1 %collective-permute-start.15 = (f32[64,128]{1,0:T(8,128)S(1)}, f32[64,128]{1,0:T(8,128)S(1)}, u32[]{:S(2)}, u32[]{:S(2)}) collective-permute-start(f32[64,128]{1,0:T(8,128)S(1)} %get-tuple-element.111), channel_id=1, source_target_pairs={{0,4},{4,8},{8,12},{12,16},{16,20},{20,24},{24,28},{28,0},{1,5},{5... | collective-permute-start | bytes 98312 | tf_op jit(solution)/shard_map/ppermute | solution.py:256
  61.6 1.2 %collective-permute-done.16.final = f32[128,128]{1,0:T(8,128)S(1)} collective-permute-done((f32[128,128]{1,0:T(8,128)S(1)}, f32[128,128]{1,0:T(8,128)S(1)}, u32[]{:S(2)}, u32[]{:S(2)}) %collective-permute-start.16) | collective-permute-done | bytes 65568 | tf_op jit(solution)/shard_map/ppermute | solution.py:256
  62.8 1.3 %collective-permute-done.14.half = f32[64,128]{1,0:T(8,128)S(1)} collective-permute-done((f32[64,128]{1,0:T(8,128)S(1)}, f32[64,128]{1,0:T(8,128)S(1)}, u32[]{:S(2)}, u32[]{:S(2)}) %collective-permute-start.14) | collective-permute-done | bytes 32800 | tf_op jit(solution)/shard_map/ppermute | solution.py:261
  64.2 2.9 %collective-permute-done.15.tail = f32[64,128]{1,0:T(8,128)S(1)} collective-permute-done((f32[64,128]{1,0:T(8,128)S(1)}, f32[64,128]{1,0:T(8,128)S(1)}, u32[]{:S(2)}, u32[]{:S(2)}) %collective-permute-start.15) | collective-permute-done | bytes 32800 | tf_op jit(solution)/shard_map/ppermute | solution.py:256
  67.1 2.4 %shard_map.60 = f32[64,2048]{1,0:T(8,128)} custom-call(s32[2]{0:T(128)S(1)} %copy-done.3, f32[64,128]{1,0:T(8,128)S(1)} %collective-permute-done.14.half, f32[128,128]{1,0:T(8,128)S(1)} %get-tuple-element.105.inner, f32[64,128]{1,0:T(8,128)S(1)} %get-tuple-element.106.before, f32[3,128,128]{2,1,0:T(8,128)S(1)} %get-tuple-element.107.reach, ...), custom_call_target="tpu_custom_call" | custom-call | flops 1000000000 | bytes 4000000 | tf_op jit(solution)/shard_map/pallas_call | solution.py:448
  (2 shorter events, 0.0 us)
Async XLA Ops:
  0.0 15.1 %collective-permute-start.1 = (f32[64,2048]{1,0:T(8,128)}, f32[64,2048]{1,0:T(8,128)S(1)}, u32[]{:S(2)}, u32[]{:S(2)}) collective-permute-start(f32[64,2048]{1,0:T(8,128)} %refs_0_), channel_id=1, source_target_pairs={{0,2},{1,3},{2,0},{3,1},{4,6},{5,7},{6,4},{7,5},{8,10},{9,11},{10,... | collective-permute-start | bytes 1572872 | tf_op jit(solution)/shard_map/ppermute | solution.py:261
  3.0 19.7 %collective-permute-start.2 = (f32[64,2048]{1,0:T(8,128)}, f32[64,2048]{1,0:T(8,128)S(1)}, u32[]{:S(2)}, u32[]{:S(2)}) collective-permute-start(f32[64,2048]{1,0:T(8,128)} %refs_0_), channel_id=1, source_target_pairs={{0,1},{1,0},{2,3},{3,2},{4,5},{5,4},{6,7},{7,6},{8,9},{9,8},{10,11... | collective-permute-start | bytes 1572872 | tf_op jit(solution)/shard_map/ppermute | solution.py:261
  3.0 2.2 %copy-start = (f32[2,16,256,128]{3,2,1,0:T(8,128)S(1)}, f32[2,16,256,128]{3,2,1,0:T(8,128)}, u32[]{:S(2)}) copy-start(f32[2,16,256,128]{3,2,1,0:T(8,128)} %source.5) | copy-start | bytes 12582916
  15.1 7.6 %copy-start.1 = (f32[64,2048]{1,0:T(8,128)S(1)}, f32[64,2048]{1,0:T(8,128)}, u32[]{:S(2)}) copy-start(f32[64,2048]{1,0:T(8,128)} %refs_0_) | copy-start | bytes 1572868
  15.1 7.6 %copy-start.2 = (f32[256,256]{1,0:T(8,128)S(1)}, f32[256,256]{1,0:T(8,128)}, u32[]{:S(2)}) copy-start(f32[256,256]{1,0:T(8,128)} %cauchy.1) | copy-start | bytes 786436
  15.1 7.6 %collective-permute-start.3 = (f32[64,2048]{1,0:T(8,128)S(1)}, f32[64,2048]{1,0:T(8,128)S(1)}, u32[]{:S(2)}, u32[]{:S(2)}) collective-permute-start(f32[64,2048]{1,0:T(8,128)S(1)} %collective-permute-done.1.refs_1_), channel_id=1, source_target_pairs={{0,1},{1,0},{2,3},{3,2},{4,5},{5,4},{6,7},{7,6},{8,9},{9,8},{10,11... | collective-permute-start | bytes 1572872 | tf_op jit(solution)/shard_map/ppermute | solution.py:261
  15.1 5.7 %collective-permute-start = (f32[128,128]{1,0:T(8,128)S(1)}, f32[128,128]{1,0:T(8,128)S(1)}, u32[]{:S(2)}, u32[]{:S(2)}) collective-permute-start(f32[128,128]{1,0:T(8,128)S(1)} %get-tuple-element.62.mine.total_in), channel_id=1, source_target_pairs={{0,4},{4,0},{8,12},{12,8},{16,20},{20,16},{24,28},{28,24},{1,5},{5... | collective-permute-start | bytes 196616 | tf_op jit(solution)/shard_map/ppermute | solution.py:261
  21.0 20.8 %collective-permute-start.7 = (f32[128,128]{1,0:T(8,128)S(1)}, f32[128,128]{1,0:T(8,128)S(1)}, u32[]{:S(2)}, u32[]{:S(2)}) collective-permute-start(f32[128,128]{1,0:T(8,128)S(1)} %get-tuple-element.75.mine), channel_id=1, source_target_pairs={{0,8},{4,12},{8,0},{12,4},{16,24},{20,28},{24,16},{28,20},{1,9},{5... | collective-permute-start | bytes 196616 | tf_op jit(solution)/shard_map/ppermute | solution.py:261
  23.6 6.9 %copy-start.3 = (s32[2]{0:T(128)S(1)}, s32[2]{0:T(128)}, u32[]{:S(2)}) copy-start(s32[2]{0:T(128)} %start.5) | copy-start | bytes 28
  23.6 6.9 %collective-permute-start.4 = (f32[192,256]{1,0:T(8,128)S(1)}, f32[192,256]{1,0:T(8,128)S(1)}, u32[]{:S(2)}, u32[]{:S(2)}) collective-permute-start(f32[192,256]{1,0:T(8,128)S(1)} %pad_maximum_fusion), channel_id=1, source_target_pairs={{0,28},{4,0},{8,4},{12,8},{16,12},{20,16},{24,20},{28,24},{1,29},{... | collective-permute-start | bytes 589832 | tf_op jit(solution)/shard_map/ppermute | solution.py:256
  32.5 4.0 %collective-permute-start.5 = (f32[64,128]{1,0:T(8,128)S(1)}, f32[64,128]{1,0:T(8,128)S(1)}, u32[]{:S(2)}, u32[]{:S(2)}) collective-permute-start(f32[64,128]{1,0:T(8,128)S(1)} %get-tuple-element.73.mine.state_in), channel_id=1, source_target_pairs={{0,4},{4,0},{8,12},{12,8},{16,20},{20,16},{24,28},{28,24},{1,5},{5... | collective-permute-start | bytes 98312 | tf_op jit(solution)/shard_map/ppermute | solution.py:261
  34.0 9.8 %collective-permute-start.11 = (f32[128,128]{1,0:T(8,128)S(1)}, f32[128,128]{1,0:T(8,128)S(1)}, u32[]{:S(2)}, u32[]{:S(2)}) collective-permute-start(f32[128,128]{1,0:T(8,128)S(1)} %get-tuple-element.67.mine), channel_id=1, source_target_pairs={{0,4},{4,0},{8,12},{12,8},{16,20},{20,16},{24,28},{28,24},{1,5},{5... | collective-permute-start | bytes 196616 | tf_op jit(solution)/shard_map/ppermute | solution.py:261
  36.6 6.1 %collective-permute-start.6 = (f32[64,128]{1,0:T(8,128)S(1)}, f32[64,128]{1,0:T(8,128)S(1)}, u32[]{:S(2)}, u32[]{:S(2)}) collective-permute-start(f32[64,128]{1,0:T(8,128)S(1)} %get-tuple-element.74.mine), channel_id=1, source_target_pairs={{0,8},{4,12},{8,0},{12,4},{16,24},{20,28},{24,16},{28,20},{1,9},{5... | collective-permute-start | bytes 98312 | tf_op jit(solution)/shard_map/ppermute | solution.py:261
  37.8 8.5 %collective-permute-start.9 = (f32[2,64,128]{2,1,0:T(8,128)S(1)}, f32[2,64,128]{2,1,0:T(8,128)S(1)}, u32[]{:S(2)}, u32[]{:S(2)}) collective-permute-start(f32[2,64,128]{2,1,0:T(8,128)S(1)} %get-tuple-element.86), channel_id=1, source_target_pairs={{0,28},{4,0},{8,4},{12,8},{16,12},{20,16},{24,20},{28,24},{1,29},{... | collective-permute-start | bytes 196616 | tf_op jit(solution)/shard_map/ppermute | solution.py:256
  42.9 4.9 %collective-permute-start.8 = (f32[64,128]{1,0:T(8,128)S(1)}, f32[64,128]{1,0:T(8,128)S(1)}, u32[]{:S(2)}, u32[]{:S(2)}) collective-permute-start(f32[64,128]{1,0:T(8,128)S(1)} %get-tuple-element.79), channel_id=1, source_target_pairs={{0,16},{4,20},{8,24},{12,28},{16,0},{20,4},{24,8},{28,12},{1,17},{... | collective-permute-start | bytes 98312 | tf_op jit(solution)/shard_map/ppermute | solution.py:261
  44.0 11.0 %collective-permute-start.13 = (f32[128,128]{1,0:T(8,128)S(1)}, f32[128,128]{1,0:T(8,128)S(1)}, u32[]{:S(2)}, u32[]{:S(2)}) collective-permute-start(f32[128,128]{1,0:T(8,128)S(1)} %get-tuple-element.98.mine), channel_id=1, source_target_pairs={{0,8},{4,12},{8,0},{12,4},{16,24},{20,28},{24,16},{28,20},{1,9},{5... | collective-permute-start | bytes 196616 | tf_op jit(solution)/shard_map/ppermute | solution.py:261
  50.7 4.0 %collective-permute-start.10 = (f32[64,128]{1,0:T(8,128)S(1)}, f32[64,128]{1,0:T(8,128)S(1)}, u32[]{:S(2)}, u32[]{:S(2)}) collective-permute-start(f32[64,128]{1,0:T(8,128)S(1)} %get-tuple-element.95.mine), channel_id=1, source_target_pairs={{0,4},{4,0},{8,12},{12,8},{16,20},{20,16},{24,28},{28,24},{1,5},{5... | collective-permute-start | bytes 98312 | tf_op jit(solution)/shard_map/ppermute | solution.py:261
  54.8 4.0 %collective-permute-start.12 = (f32[64,128]{1,0:T(8,128)S(1)}, f32[64,128]{1,0:T(8,128)S(1)}, u32[]{:S(2)}, u32[]{:S(2)}) collective-permute-start(f32[64,128]{1,0:T(8,128)S(1)} %get-tuple-element.97.mine), channel_id=1, source_target_pairs={{0,8},{4,12},{8,0},{12,4},{16,24},{20,28},{24,16},{28,20},{1,9},{5... | collective-permute-start | bytes 98312 | tf_op jit(solution)/shard_map/ppermute | solution.py:261
  55.9 7.0 %collective-permute-start.16 = (f32[128,128]{1,0:T(8,128)S(1)}, f32[128,128]{1,0:T(8,128)S(1)}, u32[]{:S(2)}, u32[]{:S(2)}) collective-permute-start(f32[128,128]{1,0:T(8,128)S(1)} %get-tuple-element.112), channel_id=1, source_target_pairs={{0,4},{4,8},{8,12},{12,16},{16,20},{20,24},{24,28},{28,0},{1,5},{5... | collective-permute-start | bytes 196616 | tf_op jit(solution)/shard_map/ppermute | solution.py:256
  59.1 5.1 %collective-permute-start.14 = (f32[64,128]{1,0:T(8,128)S(1)}, f32[64,128]{1,0:T(8,128)S(1)}, u32[]{:S(2)}, u32[]{:S(2)}) collective-permute-start(f32[64,128]{1,0:T(8,128)S(1)} %get-tuple-element.104), channel_id=1, source_target_pairs={{0,16},{4,20},{8,24},{12,28},{16,0},{20,4},{24,8},{28,12},{1,17},{... | collective-permute-start | bytes 98312 | tf_op jit(solution)/shard_map/ppermute | solution.py:261
  60.5 6.6 %collective-permute-start.15 = (f32[64,128]{1,0:T(8,128)S(1)}, f32[64,128]{1,0:T(8,128)S(1)}, u32[]{:S(2)}, u32[]{:S(2)}) collective-permute-start(f32[64,128]{1,0:T(8,128)S(1)} %get-tuple-element.111), channel_id=1, source_target_pairs={{0,4},{4,8},{8,12},{12,16},{16,20},{20,24},{24,28},{28,0},{1,5},{5... | collective-permute-start | bytes 98312 | tf_op jit(solution)/shard_map/ppermute | solution.py:256

commit v2 on v1

v2 whole, which is shorter than its diff:
```python
import functools

import jax
import jax.numpy as jnp
from jax import lax
from jax.experimental import pallas as pl
from jax.experimental.pallas import tpu as pltpu
from jax.sharding import PartitionSpec as P

F32, BF16 = jnp.float32, jnp.bfloat16
VMEM = pl.BlockSpec(memory_space=pltpu.VMEM)
SMEM = pl.BlockSpec(memory_space=pltpu.SMEM)
NN = (((1,), (0,)), ((), ()))
NT = (((1,), (1,)), ((), ()))
TN = (((0,), (0,)), ((), ()))


def split(value):
    high = value.astype(BF16)
    return high, (value - high.astype(F32)).astype(BF16)


def dot(left, right, dims=NN):
    return lax.dot_general(left, right, dims, preferred_element_type=F32)


def wide(value):
    return jnp.concatenate(split(value), axis=1)


def tall(value):
    terms = [jnp.concatenate([term, term], axis=1) for term in split(value)]
    return jnp.concatenate(terms, axis=0)


def doubled(rows_high, rows_low):
    return jnp.concatenate([rows_high, rows_low], axis=0)


def folded(product):
    half = product.shape[0] // 2
    return product[:half] + product[half:]


def apply(left, high, low):
    if left.shape[1] <= 128:
        return folded(dot(tall(left), doubled(high, low)))
    left_high, left_low = split(left)
    return folded(dot(jnp.concatenate([left_high, left_low], axis=0), high)) + dot(left_high, low)


def times(left, right):
    return apply(left, *split(right))


def eye(rows, columns):
    shape = (rows, columns)
    return lax.broadcasted_iota(jnp.int32, shape, 0) == lax.broadcasted_iota(jnp.int32, shape, 1)


def upper_inverses(grams):
    spread = grams[0].shape[0]
    base = spread // 4
    diagonal = eye(spread, spread)
    above = lax.broadcasted_iota(jnp.int32, (spread, spread), 0) < lax.broadcasted_iota(
        jnp.int32, (spread, spread), 1
    )
    halves = [jnp.where(diagonal, 0.5 * gram, 0.0) for gram in grams]
    columns = [jnp.sum(half, axis=0, keepdims=True) for half in halves]
    scaled = [
        jnp.where(above, gram, 0.0) / jnp.sum(half, axis=1, keepdims=True)
        for gram, half in zip(grams, halves)
    ]

    def owner(size):
        return lax.broadcasted_iota(jnp.int32, (size, spread), 1) // size

    def compact(value, size, row=lambda block: block):
        owns = owner(size)
        result = value[row(0) * size : (row(0) + 1) * size]
        for block in range(1, spread // size):
            at = row(block) * size
            result = jnp.where(owns == block, value[at : at + size], result)
        return result

    def expanded(value, size, row=lambda block: block):
        owns = owner(size)
        masks = [(owns == block).astype(BF16) for block in range(spread // size)]
        terms = []
        for term in split(value):
            rows = [jnp.zeros_like(term)] * (spread // size)
            for block, mask in enumerate(masks):
                if row(block) is not None:
                    rows[row(block)] = term * mask
            terms.append(jnp.concatenate(rows, axis=0))
        return doubled(*terms)

    size = base
    unit = compact(diagonal.astype(F32), size)
    powers = [compact(value, size) for value in scaled]
    results = [unit - power for power in powers]
    rights = [expanded(power, size) for power in powers]
    powers = [folded(dot(tall(power), right)) for power, right in zip(powers, rights)]
    reach = 2
    while reach < size:
        reach *= 2
        rights = [expanded(power, size) for power in powers]
        if reach < size:
            lefts = [jnp.concatenate([r, p], axis=0) for r, p in zip(results, powers)]
        else:
            lefts = results
        products = [folded(dot(tall(left), right)) for left, right in zip(lefts, rights)]
        results = [result + product[:size] for result, product in zip(results, products)]
        if reach < size:
            powers = [product[size:] for product in products]
    while size < spread:
        odd = lax.rem(owner(size), 2) == 1
        edges = [
            jnp.where(odd, compact(value, size, lambda block: block & ~1), 0.0) for value in scaled
        ]
        rights = [expanded(result, size) for result in results]
        products = [folded(dot(tall(edge), right)) for edge, right in zip(edges, rights)]
        rights = [
            expanded(product, size, lambda block: block - 1 if block & 1 else None)
            for product in products
        ]
        products = [folded(dot(tall(result), right)) for result, right in zip(results, rights)]
        results = [
            jnp.concatenate(
                [jnp.where(odd, -product, result), jnp.where(odd, result, 0.0)], axis=0
            )
            for result, product in zip(results, products)
        ]
        size *= 2
    return [result / column for result, column in zip(results, columns)]


def reflect_kernel(run, sweeps, last_slot, source, *refs):
    count, double, spread = source.shape[1:]
    found = [refs[i * 8 : i * 8 + 8] for i in range(len(sweeps))]
    limit = last_slot - lax.axis_index("row") * count
    pairs = [wide(source[sweep, b]) for sweep in sweeps for b in range(count)]
    grams = [dot(pair, pair, TN) for pair in pairs]
    grams = [
        (g[:spread, :spread] + g[spread:, spread:]) + (g[:spread, spread:] + g[spread:, :spread])
        for g in grams
    ]
    triangles = upper_inverses(grams)
    unit = eye(double, double).astype(F32)
    scaled = []
    for pair, triangle in zip(pairs, triangles):
        high, low = split(triangle)
        right = jnp.concatenate(
            [jnp.concatenate([high, high], axis=1), jnp.concatenate([low, low], axis=1)], axis=0
        )
        product = dot(pair, right, NT)
        scaled.append(product[:, :spread] + product[:, spread:])
    for i, (pair, value) in enumerate(zip(pairs, scaled)):
        k_high, k_low = found[i // count][:2]
        product = folded(dot(tall(value), pair, NT))
        high, low = split(unit - jnp.where(i % count <= limit, product, 0.0))
        k_high[i % count] = high
        k_low[i % count] = low
    runs = count // run
    state, out = [[None] * runs for _ in found], [[None] * runs for _ in found]
    for step in range(run):
        for j in range(runs):
            for i, (k_high, k_low, q_high, q_low, _, _, _, first) in enumerate(found):
                b = j * run + step
                high, low = k_high[b, :spread, :], k_low[b, :spread, :]
                if step == 0:
                    both = high.astype(F32) + low.astype(F32)
                else:
                    both = apply(state[i][j], high, low)
                state[i][j] = both[:, spread:]
                out[i][j] = both[:, :spread]
                high, low = split(out[i][j])
                q_high[j, :, step * spread : (step + 1) * spread] = high
                q_low[j, :, step * spread : (step + 1) * spread] = low
                if j == 0 and step < 2:
                    first[:, step * spread : (step + 1) * spread] = out[i][j]
    so_far = [state[i][0] for i in range(len(found))]
    for j in range(runs):
        for i, (_, _, _, _, maps, reach, total, _) in enumerate(found):
            maps[j] = state[i][j]
            if j:
                reach[j - 1] = so_far[i]
                so_far[i] = times(so_far[i], state[i][j])
            if j == runs - 1:
                total[...] = so_far[i]


def reflect(refl_v, sweeps, run):
    slots, double, spread = refl_v.shape[1:]
    runs = slots // run
    shape = jax.ShapeDtypeStruct
    square = shape((spread, spread), F32)
    shapes = [shape((slots, double, double), BF16)] * 2
    shapes += [shape((runs, spread, run * spread), BF16)] * 2
    shapes += [shape((runs, spread, spread), F32), shape((runs - 1, spread, spread), F32), square]
    shapes += [shape((spread, 2 * spread), F32)]
    results = whole_call(
        functools.partial(reflect_kernel, run, sweeps, lax.axis_size("row") * slots - 3),
        shapes * len(sweeps), len(sweeps) * slots * 300_000_000, [], [refl_v], vmem=24,
    )
    return [results[i * 8 : i * 8 + 8] for i in range(len(sweeps))]


def merge_kernel(owners, cauchy, *refs):
    pieces, (merged, chosen) = refs[:-2], refs[-2:]
    rows, columns = pieces[0].shape
    mine = lax.axis_index("col")
    chosen[...] = rolled(cauchy[...], mine * rows)[:, : chosen.shape[1]]
    left = [
        chosen[pl.ds(pl.multiple_of((mine ^ owner) * rows, rows), rows), :rows] for owner in owners
    ]
    left_high, left_low = split(jnp.concatenate(left, axis=0))
    step = columns // 4
    for part in range(4):
        at = slice(part * step, (part + 1) * step)
        right_high, right_low = split(jnp.concatenate([piece[:, at] for piece in pieces], axis=0))
        merged[:, at] = dot(left_high, right_high, TN) + (
            dot(left_high, right_low, TN) + dot(left_low, right_high, TN)
        )


def shifted(array, by):
    devices = lax.axis_size("row")
    return lax.ppermute(array, "row", [(i, (i + by) % devices) for i in range(devices)])


def swapped(array, axis, distance):
    devices = lax.axis_size(axis)
    return lax.ppermute(array, axis, [(i, i ^ distance) for i in range(devices)])


def after_all(array, *others):
    return lax.optimization_barrier((array, *others))[0]


def rolled(value, left):
    width = value.shape[1]
    return pltpu.roll(value, lax.rem(width - left, width), 1)


def chain(first, aligned, k_high, k_low, maps, y_local, joins):
    slots, rows, spread = y_local.shape
    runs = maps.shape[0]
    run = slots // runs

    def segment(slot):
        return aligned[:, slot * spread : (slot + 1) * spread]

    carry = [jnp.zeros((rows, spread), F32)] * runs
    if first is not None:
        carry[0] = jnp.where(first, segment(0), 0.0)
    for step in range(run):
        for j in range(runs):
            slot = j * run + step
            fresh = jnp.concatenate([carry[j], segment(slot + 1)], axis=1)
            both = apply(fresh, k_high[slot], k_low[slot])
            y_local[slot] = both[:, :spread]
            carry[j] = both[:, spread:]
    so_far = carry[0]
    joins[0] = jnp.zeros_like(so_far)
    for j in range(1, runs):
        joins[j] = so_far
        so_far = times(so_far, maps[j]) + carry[j]
    return so_far


def first_kernel(start, home, after, k_high, k_low, maps, y_local, joins, state, head, front):
    slots, rows, spread = y_local.shape
    offset = start[0]
    head[...] = pltpu.roll(home[:, :spread], lax.rem(spread - offset, spread), 1)
    aligned = rolled(jnp.concatenate([home[...], after[...]], axis=1), offset)
    first = lax.axis_index("row") == 0
    state[...] = chain(first, aligned, k_high, k_low, maps, y_local, joins)
    front[...] = y_local[:2]


def settled(joins, q_high, q_low, y_local, put):
    runs, spread, width = q_high.shape
    run = width // spread
    for j in range(runs):
        added = apply(joins[j], q_high[j], q_low[j]) if j else None
        for step in range(run):
            slot = j * run + step
            value = y_local[slot]
            if j:
                value = value + added[:, step * spread : (step + 1) * spread]
            put(slot, value)


def line_kernel(head, joins, y_local, q_high, q_low, line):
    spread = head.shape[1]
    line[:, :spread] = head[...]

    def put(slot, value):
        line[:, (slot + 1) * spread : (slot + 2) * spread] = value

    settled(joins, q_high, q_low, y_local, put)


def second_kernel(
    start, ready, state_in, front, first_next, k_high, k_low, maps, y_local, joins, state, head,
    line,
):
    slots, rows, spread = y_local.shape
    width = ready.shape[1]
    line[:, :width] = ready[...]
    added = times(state_in[...], first_next[...])
    for extra in range(2):
        at = slice(extra * spread, (extra + 1) * spread)
        line[:, width + extra * spread : width + (extra + 1) * spread] = front[extra] + added[:, at]
    ahead = start[1] - start[0]
    head[...] = pltpu.roll(
        line[:, : 2 * spread], lax.rem(4 * spread - ahead, 2 * spread), 1
    )[:, :spread]
    first = lax.axis_index("row") == 0
    aligned = rolled(line[...], ahead + spread)
    state[:, :spread] = state_in[...]
    state[:, spread:] = chain(first, aligned, k_high, k_low, maps, y_local, joins)


def base_kernel(start, head, joins, y_local, q_high, q_low, base, tail, line):
    spread = head.shape[1]
    line[:, :spread] = jnp.where(lax.axis_index("row") == 0, head[...], 0.0)

    def put(slot, value):
        line[:, (slot + 1) * spread : (slot + 2) * spread] = value

    settled(joins, q_high, q_low, y_local, put)
    tail[...] = line[:, base.shape[1] :]
    base[...] = rolled(line[...], spread - start[1])[:, : base.shape[1]]


def response_kernel(
    start, q_high, q_low, reach, total, first_next, k_high, k_low, maps, y_local, joins, gamma, line
):
    runs, spread, width = q_high.shape
    line[:, :spread] = jnp.zeros((spread, spread), F32)
    for j in range(runs):
        if j:
            out = apply(reach[j - 1], q_high[j], q_low[j])
        else:
            out = q_high[j].astype(F32) + q_low[j].astype(F32)
        line[:, spread + j * width : spread + (j + 1) * width] = out
    line[:, spread + runs * width :] = times(total[...], first_next[...])
    aligned = rolled(line[...], start[1] - start[0] + spread)
    gamma[...] = chain(None, aligned, k_high, k_low, maps, y_local, joins)


def home_kernel(start, joins, y_local, q_high, q_low, reach, high, low, seam, line):
    runs, spread, width = q_high.shape
    columns = high.shape[1]
    line[:, :spread] = jnp.zeros((spread, spread), F32)

    def put(slot, value):
        line[:, (slot + 1) * spread : (slot + 2) * spread] = value

    for sweep in range(2):
        at = slice(sweep * spread, (sweep + 1) * spread)
        if sweep == 0:
            settled(joins, q_high, q_low, y_local, put)
        else:
            for j in range(runs):
                if j:
                    out = apply(reach[j - 1], q_high[j], q_low[j])
                else:
                    out = q_high[j].astype(F32) + q_low[j].astype(F32)
                line[:, spread + j * width : spread + (j + 1) * width] = out
        seam[at] = line[:, columns:]
        moved = split(rolled(line[...], spread - start[1])[:, :columns])
        high[at], low[at] = moved


def is_upper(level):
    return lax.rem(lax.axis_index("row") // (1 << level), 2) == 1


def through(states, maps):
    spread = maps.shape[1]
    first, second = states[:, :spread], states[:, spread:]
    return jnp.concatenate(
        [times(first, maps[0]), times(first, maps[1]) + times(second, maps[2])], axis=1
    )


def through_seam(states, seam):
    spread = seam.shape[1]
    return times(states[:, :spread], seam[:spread]) + times(states[:, spread:], seam[spread:])


def join_maps_kernel(level, mine, other, *refs):
    upper = is_upper(level)
    if level:
        inner, refs = refs[0], refs[1:]
    high, both, inside = refs
    spread = mine.shape[1]
    low = [jnp.where(upper, other[i], mine[i]) for i in range(3)]
    high[...] = jnp.where(upper, mine[...], other[...])

    def joined(later):
        return [
            times(low[0], later[0]),
            times(low[0], later[1]) + times(low[1], later[2]),
            times(low[2], later[2]),
        ]

    for i, value in enumerate(joined(high)):
        both[i] = value
    if level:
        for i, value in enumerate(joined(inner)):
            inside[i] = jnp.where(upper, value, inner[i])
    else:
        unit = eye(spread, spread).astype(F32)
        for i, value in enumerate([unit, jnp.zeros_like(unit), unit]):
            inside[i] = jnp.where(upper, low[i], value)


def seam_kernel(levels, inside, seam, out):
    spread = seam.shape[1]
    first, second = seam[:spread], seam[spread:]
    upper = is_upper(levels - 1)
    out[:spread] = jnp.where(upper, times(inside[0], first) + times(inside[1], second), 0.0)
    out[spread:] = jnp.where(upper, times(inside[2], second), 0.0)


def join_states_kernel(level, top, mine, other, high, *refs):
    upper = is_upper(level)
    if level:
        inner, before, refs = refs[0], refs[1], refs[2:]
    if top:
        tail, seam, refs = refs[0], refs[1], refs[2:]
    low = jnp.where(upper, other[...], mine[...])
    refs[0][...] = through(low, high) + jnp.where(upper, mine[...], other[...])
    if level:
        enters = before[...] + jnp.where(upper, through(low, inner), 0.0)
    else:
        enters = jnp.where(upper, low, 0.0)
    refs[1][...] = enters
    if top:
        refs[2][...] = tail[...] + through_seam(enters, seam)


def final_kernel(levels, start, half, inner, before, base, high, low, tail, seam, out):
    spread = tail.shape[1]
    enters = jnp.where(is_upper(levels - 1), half[...], 0.0)
    incoming = before[...] + through(enters, inner)
    out[...] = base[...] + apply(incoming, high[...], low[...])
    offset = start[1]
    lead = pltpu.roll(tail[...] + through_seam(enters, seam), offset, 1)
    column = lax.broadcasted_iota(jnp.int32, lead.shape, 1)
    kept = (column < offset) & (lax.axis_index("row") > 0)
    out[:, :spread] += jnp.where(kept, lead, 0.0)


def whole_call(kernel, shapes, flops, scalars, arrays, scratch=(), vmem=8):
    return pl.pallas_call(
        kernel,
        out_shape=shapes,
        in_specs=[SMEM] * len(scalars) + [VMEM] * len(arrays),
        out_specs=jax.tree.map(lambda shape: VMEM, shapes),
        scratch_shapes=list(scratch),
        compiler_params=pltpu.CompilerParams(vmem_limit_bytes=vmem << 20),
        cost_estimate=pl.CostEstimate(
            flops=flops, bytes_accessed=4_000_000, transcendentals=0
        ),
    )(*scalars, *arrays)


def run_length(slots):
    return next(size for size in (4, 2, 1) if slots % (2 * size) == 0)


def shards(panel, cauchy, refl_v, block_start):
    rows, columns = panel.shape
    slots, _, spread = refl_v.shape[1:]
    run = run_length(slots)
    levels = lax.axis_size("row").bit_length() - 1
    shape = functools.partial(jax.ShapeDtypeStruct, dtype=F32)
    segment = shape((rows, spread))
    chained = [shape((slots, rows, spread)), shape((slots // run, rows, spread)), segment]
    starts = [block_start]

    count = lax.axis_size("col")
    pieces, owners = [panel], [0]
    distance = count // 2
    while distance:
        pieces += [swapped(piece, "col", distance) for piece in pieces]
        if owners == [0]:
            if slots <= 16:
                one, two = reflect(refl_v, (0, 1), run)
            else:
                [one], [two] = reflect(refl_v, (0,), run), reflect(refl_v, (1,), run)
            high1, low1, qh1, ql1, maps1, reach1, total1, first1 = one
            high2, low2, qh2, ql2, maps2, reach2, total2, _ = two
            pieces[-1] = after_all(pieces[-1], total1)
        owners += [owner ^ distance for owner in owners]
        distance //= 2
    first_next = shifted(first1, -1)
    merged = whole_call(
        functools.partial(merge_kernel, owners), shape((rows, columns)),
        1_000_000_000, [], [cauchy] + pieces,
        [pltpu.VMEM((cauchy.shape[0], 128 * pl.cdiv(rows, 128)), F32)],
    )
    after = shifted(merged[:, : 2 * spread], -1)

    square = shape((spread, spread))
    long = columns + 3 * spread
    responses = [
        shape((slots, spread, spread)), shape((slots // run, spread, spread)), square
    ]
    y_response, joins_response, gamma = whole_call(
        response_kernel, responses, 4_000_000_000, starts,
        [qh1, ql1, reach1, after_all(total1, merged), first_next, high2, low2, maps2],
        [pltpu.VMEM((spread, long), F32)],
    )
    maps = jnp.stack([total1, gamma, total2])
    groups, inside = [], None
    for level in range(levels - 1):
        arrays = [maps, swapped(maps, "row", 1 << level)] + ([inside] if level else [])
        high, maps, inside = whole_call(
            functools.partial(join_maps_kernel, level), [shape(maps.shape)] * 3, 400_000_000, [],
            arrays,
        )
        groups.append((high, inside))

    y1, joins1, state1, head1, front = whole_call(
        first_kernel, chained + [segment, shape((2, rows, spread))], 3_000_000_000, starts,
        [after_all(merged, gamma), after, high1, low1, maps1],
    )
    front = shifted(front, -1)
    line = whole_call(
        line_kernel, shape((rows, columns + spread)), 1_000_000_000, [],
        [head1, joins1, y1, qh1, ql1],
    )
    states = shape((rows, 2 * spread))
    y2, joins2, state, head2 = whole_call(
        second_kernel, chained[:2] + [states, segment], 3_000_000_000, starts,
        [line, state1, front, first_next, high2, low2, maps2],
        [pltpu.VMEM((rows, long), F32)],
    )
    base, tail = whole_call(
        base_kernel, [shape((rows, columns)), segment], 2_000_000_000, starts,
        [head2, joins2, y2, qh2, ql2], [pltpu.VMEM((rows, columns + spread), F32)],
    )
    home = jax.ShapeDtypeStruct((2 * spread, columns), BF16)
    home_high, home_low, seam = whole_call(
        home_kernel, [home, home, shape((2 * spread, spread))], 3_000_000_000, starts,
        [joins_response, y_response, qh2, ql2, reach2],
        [pltpu.VMEM((spread, columns + spread), F32)],
    )
    seam_far = whole_call(
        functools.partial(seam_kernel, levels), shape(seam.shape), 100_000_000, [],
        [groups[-1][1], seam],
    )
    seam_far = shifted(seam_far, 1)

    enters = None
    for level in range(levels - 1):
        top = level == levels - 2
        arrays = [state, swapped(state, "row", 1 << level), groups[level][0]]
        arrays += [groups[level - 1][1], enters] if level else []
        arrays += [tail, seam] if top else []
        state, enters, *moved = whole_call(
            functools.partial(join_states_kernel, level, top),
            [states] * 2 + [segment] * top, 100_000_000, [], arrays,
        )
    half = swapped(state, "row", 1 << (levels - 1))
    tail = shifted(moved[0], 1)
    return whole_call(
        functools.partial(final_kernel, levels), shape((rows, columns)), 1_000_000_000, starts,
        [half, groups[-1][1], enters, base, home_high, home_low, tail, seam_far],
    )


def solution(mesh):
    placed = (P("col", "row"), P(), P(None, "row", None, None), P())
    return jax.shard_map(
        shards, mesh=mesh, in_specs=placed, out_specs=P("col", "row"), check_vma=False
    )
```

time: 69.6 us -> 61.1 us (0.88)
  waiting for transfers between devices: 18.4 us -> 10.1 us
  starting transfers between devices: 23.7 us -> 22.5 us
  Pallas kernels: 25.1 us -> 26 us
    ppermute x13 -> x8, waiting for transfers between devices: 13.8 us -> 4.18 us  [swapped(): lax.ppermute(array, axis, [(i, i ^ distance) for i in range(devices)])]
    ppermute x13 -> x8, starting transfers between devices: 14.5 us -> 7.38 us  [swapped(): lax.ppermute(array, axis, [(i, i ^ distance) for i in range(devices)])]
    ppermute x4 -> x5, starting transfers between devices: 9.22 us -> 15.1 us  [shifted(): lax.ppermute(array, 'row', [(i, (i + by) % devices) for i in range(device...]
    ppermute x4 -> x5, waiting for transfers between devices: 4.56 us -> 5.91 us  [shifted(): lax.ppermute(array, 'row', [(i, (i + by) % devices) for i in range(device...]
    pallas_call x15 -> x14, Pallas kernels: 25.1 us -> 26 us  [whole_call(): pl.pallas_call(kernel, out_shape=shapes, in_specs=[SMEM] * len(scalars) +...]
  transfers between devices with their start and end apart: 17 -> 13, of which waited for: 9 -> 5; matrix products, arithmetic and copies ran while one was open for 0% -> 0% of each run, Pallas kernels for 33% -> 39%
where the time goes in v2:
time: 61.1 us; the launch traced here: 60.9 us
  Pallas kernels  26 us (43%)
  starting transfers between devices  22.5 us (37%)
  waiting for transfers between devices  10.1 us (17%)
  local copies, waits for them, and re-layouts  2.2 us (4%)
    pallas_call x14, Pallas kernels, whole_call(): pl.pallas_call(kernel, out_shape=shapes, in_specs=[SMEM] * len(scalars) +...  26 us
    ppermute x5, starting transfers between devices, shifted(): lax.ppermute(array, 'row', [(i, (i + by) % devices) for i in range(device...  15.1 us
    ppermute x8, starting transfers between devices, swapped(): lax.ppermute(array, axis, [(i, i ^ distance) for i in range(devices)])  7.38 us
    ppermute x5, waiting for transfers between devices, shifted(): lax.ppermute(array, 'row', [(i, (i + by) % devices) for i in range(device...  5.91 us
    ppermute x8, waiting for transfers between devices, swapped(): lax.ppermute(array, axis, [(i, i ^ distance) for i in range(devices)])  4.18 us
    unnamed x8, local copies, waits for them, and re-layouts  2.2 us
  transfers between devices with their start and end apart: 13, of which 5 were waited for; matrix products, arithmetic and copies ran while one was open for 0% of the time, Pallas kernels for 39%

profile of v2, /device:TPU:0, one launch (start us, length us, event | category | flops | bytes accessed | tf_op | source)
XLA Modules:
  0.0 60.9 jit_solution(6938414839147959163)
XLA Ops:
  0.0 3.0 %collective-permute-start = (f32[64,2048]{1,0:T(8,128)}, f32[64,2048]{1,0:T(8,128)S(1)}, u32[]{:S(2)}, u32[]{:S(2)}) collective-permute-start(f32[64,2048]{1,0:T(8,128)} %refs_0_.1), channel_id=1, source_target_pairs={{0,2},{1,3},{2,0},{3,1},{4,6},{5,7},{6,4},{7,5},{8,10},{9,11},{10,... | collective-permute-start | bytes 1572872 | tf_op jit(solution)/shard_map/ppermute | solution.py:234
  3.0 0.0 collective-permute-start.1
  3.0 0.0 copy-start
  3.0 2.2 %copy-done = f32[2,16,256,128]{3,2,1,0:T(8,128)S(1)} copy-done((f32[2,16,256,128]{3,2,1,0:T(8,128)S(1)}, f32[2,16,256,128]{3,2,1,0:T(8,128)}, u32[]{:S(2)}) %copy-start) | copy-done | bytes 4194328
  5.2 0.0 copy-start.1
  5.2 0.0 copy-start.2
  5.2 11.5 %shard_map.46 = (bf16[16,256,256]{2,1,0:T(8,128)(2,1)S(1)}, bf16[16,256,256]{2,1,0:T(8,128)(2,1)S(1)}, bf16[4,128,512]{2,1,0:T(8,128)(2,1)S(1)}, bf16[4,128,512]...) custom-call(f32[2,16,256,128]{3,2,1,0:T(8,128)S(1)} %copy-done), custom_call_target="tpu_custom_call" | custom-call | flops 9600000000 | bytes 4000000 | tf_op jit(solution)/shard_map/pallas_call | solution.py:460
  16.6 0.0 copy-start.3
  16.6 0.0 collective-permute-done.refs_1_
  16.6 0.5 collective-permute-start.2
  17.1 4.5 %collective-permute-start.3 = (f32[128,256]{1,0:T(8,128)S(1)}, f32[128,256]{1,0:T(8,128)S(1)}, u32[]{:S(2)}, u32[]{:S(2)}) collective-permute-start(f32[128,256]{1,0:T(8,128)S(1)} %get-tuple-element.56), channel_id=1, source_target_pairs={{0,28},{4,0},{8,4},{12,8},{16,12},{20,16},{24,20},{28,24},{1,29},{... | collective-permute-start | bytes 393224 | tf_op jit(solution)/shard_map/ppermute | solution.py:229
  21.7 0.0 collective-permute-done.1.refs_2_
  21.7 0.0 collective-permute-done.2.refs_3_
  21.7 0.0 copy-done.1
  21.7 0.0 copy-done.2
  21.7 0.9 %shard_map.47.home = f32[64,2048]{1,0:T(8,128)S(1)} custom-call(f32[256,256]{1,0:T(8,128)S(1)} %copy-done.2, f32[64,2048]{1,0:T(8,128)S(1)} %copy-done.1, f32[64,2048]{1,0:T(8,128)S(1)} %collective-permute-done.refs_1_, f32[64,2048]{1,0:T(8,128)S(1)} %collective-permute-done.1.refs_2_, f32[64,2048]{1,0:T(8,128)S(1)} %collective-permute-done.2.refs_3_), custom_call_target="tpu_custom_call" | custom-call | flops 1000000000 | bytes 4000000 | tf_op jit(solution)/shard_map/pallas_call | solution.py:460
  22.6 1.8 %collective-permute-start.4 = (f32[64,256]{1,0:T(8,128)S(1)}, f32[64,256]{1,0:T(8,128)S(1)}, u32[]{:S(2)}, u32[]{:S(2)}) collective-permute-start(f32[64,256]{1,0:T(8,128)S(1)} %slice.4), channel_id=1, source_target_pairs={{0,28},{4,0},{8,4},{12,8},{16,12},{20,16},{24,20},{28,24},{1,29},{... | collective-permute-start | bytes 196616 | tf_op jit(solution)/shard_map/ppermute | solution.py:229
  24.4 0.3 collective-permute-done.3.first_next
  24.6 0.0 copy-done.3
  24.6 2.6 %shard_map.48 = (f32[16,128,128]{2,1,0:T(8,128)S(1)}, f32[4,128,128]{2,1,0:T(8,128)S(1)}, f32[128,128]{1,0:T(8,128)S(1)}) custom-call(s32[2]{0:T(128)S(1)} %copy-done.3, bf16[4,128,512]{2,1,0:T(8,128)(2,1)S(1)} %get-tuple-element.52.q_high, bf16[4,128,512]{2,1,0:T(8,128)(2,1)S(1)} %get-tuple-element.53.q_low, f32[3,128,128]{2,1,0:T(8,128)S(1)} %get-tuple-element.54.reach, ...), custom_call_target="tpu_custom_call" | custom-call | flops 4000000000 | bytes 4000000 | tf_op jit(solution)/shard_map/pallas_call | solution.py:460
  27.2 0.4 collective-permute-start.7
  27.6 0.0 collective-permute-done.4.after
  27.6 1.9 %shard_map.49 = (f32[16,64,128]{2,1,0:T(8,128)S(1)}, f32[4,64,128]{2,1,0:T(8,128)S(1)}, f32[64,128]{1,0:T(8,128)S(1)}, f32[64,128]{1,0:T(8,128)S(1)}, f32[2,64,128]{2,1,0:T(8,128)S(1)}) custom-call(s32[2]{0:T(128)S(1)} %copy-done.3, f32[64,2048]{1,0:T(8,128)S(1)} %shard_map.47.home, f32[64,256]{1,0:T(8,128)S(1)} %collective-permute-done.4.after, ...), custom_call_target="tpu_custom_call" | custom-call | flops 3000000000 | bytes 4000000 | tf_op jit(solution)/shard_map/pallas_call | solution.py:460
  29.5 4.9 %collective-permute-start.5 = (f32[2,64,128]{2,1,0:T(8,128)S(1)}, f32[2,64,128]{2,1,0:T(8,128)S(1)}, u32[]{:S(2)}, u32[]{:S(2)}) collective-permute-start(f32[2,64,128]{2,1,0:T(8,128)S(1)} %get-tuple-element.69), channel_id=1, source_target_pairs={{0,28},{4,0},{8,4},{12,8},{16,12},{20,16},{24,20},{28,24},{1,29},{... | collective-permute-start | bytes 196616 | tf_op jit(solution)/shard_map/ppermute | solution.py:229
  34.5 0.3 shard_map.50.ready
  34.7 1.6 %collective-permute-done.5.front = f32[2,64,128]{2,1,0:T(8,128)S(1)} collective-permute-done((f32[2,64,128]{2,1,0:T(8,128)S(1)}, f32[2,64,128]{2,1,0:T(8,128)S(1)}, u32[]{:S(2)}, u32[]{:S(2)}) %collective-permute-start.5) | collective-permute-done | bytes 65568 | tf_op jit(solution)/shard_map/ppermute | solution.py:229
  36.4 2.0 %shard_map.51 = (f32[16,64,128]{2,1,0:T(8,128)S(1)}, f32[4,64,128]{2,1,0:T(8,128)S(1)}, f32[64,256]{1,0:T(8,128)S(1)}, f32[64,128]{1,0:T(8,128)S(1)}) custom-call(s32[2]{0:T(128)S(1)} %copy-done.3, f32[64,2176]{1,0:T(8,128)S(1)} %shard_map.50.ready, f32[64,128]{1,0:T(8,128)S(1)} %get-tuple-element.68.state_in, ...), custom_call_target="tpu_custom_call" | custom-call | flops 3000000000 | bytes 4000000 | tf_op jit(solution)/shard_map/pallas_call | solution.py:460
  38.4 0.1 collective-permute-start.6
  38.5 0.0 collective-permute-done.7.other
  38.5 0.3 shard_map.52
  38.8 0.2 collective-permute-start.9
  39.0 1.8 %shard_map.56 = (bf16[256,2048]{1,0:T(8,128)(2,1)S(1)}, bf16[256,2048]{1,0:T(8,128)(2,1)S(1)}, f32[256,128]{1,0:T(8,128)S(1)}) custom-call(s32[2]{0:T(128)S(1)} %copy-done.3, f32[4,128,128]{2,1,0:T(8,128)S(1)} %get-tuple-element.84.joins, f32[16,128,128]{2,1,0:T(8,128)S(1)} %get-tuple-element.85.y_local, bf16[4,128,512]{2,1,0:T(8,128)(2,1)S(1)} %get-tuple-element.81.q_high, ...), custom_call_target="tpu_custom_call" | custom-call | flops 3000000000 | bytes 4000000 | tf_op jit(solution)/shard_map/pallas_call | solution.py:460
  40.8 1.9 %collective-permute-done.6.other = f32[64,256]{1,0:T(8,128)S(1)} collective-permute-done((f32[64,256]{1,0:T(8,128)S(1)}, f32[64,256]{1,0:T(8,128)S(1)}, u32[]{:S(2)}, u32[]{:S(2)}) %collective-permute-start.6) | collective-permute-done | bytes 65568 | tf_op jit(solution)/shard_map/ppermute | solution.py:234
  42.7 0.2 shard_map.53
  42.9 0.1 collective-permute-start.8
  43.0 2.3 %collective-permute-done.9.other = f32[3,128,128]{2,1,0:T(8,128)S(1)} collective-permute-done((f32[3,128,128]{2,1,0:T(8,128)S(1)}, f32[3,128,128]{2,1,0:T(8,128)S(1)}, u32[]{:S(2)}, u32[]{:S(2)}) %collective-permute-start.9) | collective-permute-done | bytes 196640 | tf_op jit(solution)/shard_map/ppermute | solution.py:234
  45.3 1.0 %shard_map.54 = (f32[3,128,128]{2,1,0:T(8,128)S(1)}, f32[3,128,128]{2,1,0:T(8,128)}, f32[3,128,128]{2,1,0:T(8,128)S(1)}) custom-call(f32[3,128,128]{2,1,0:T(8,128)S(1)} %get-tuple-element.74.mine, f32[3,128,128]{2,1,0:T(8,128)S(1)} %collective-permute-done.9.other, f32[3,128,128]{2,1,0:T(8,128)S(1)} %get-tuple-element.75.refs_0_), custom_call_target="tpu_custom_call" | custom-call | flops 400000000 | bytes 4000000 | tf_op jit(solution)/shard_map/pallas_call | solution.py:460
  46.2 0.2 shard_map.58
  46.5 1.3 %collective-permute-start.12 = (f32[256,128]{1,0:T(8,128)S(1)}, f32[256,128]{1,0:T(8,128)S(1)}, u32[]{:S(2)}, u32[]{:S(2)}) collective-permute-start(f32[256,128]{1,0:T(8,128)S(1)} %shard_map.58), channel_id=1, source_target_pairs={{0,4},{4,8},{8,12},{12,16},{16,20},{20,24},{24,28},{28,0},{1,5},{5... | collective-permute-start | bytes 393224 | tf_op jit(solution)/shard_map/ppermute | solution.py:229
  47.8 1.0 %shard_map.55 = (f32[64,2048]{1,0:T(8,128)S(1)}, f32[64,128]{1,0:T(8,128)S(1)}) custom-call(s32[2]{0:T(128)S(1)} %copy-done.3, f32[64,128]{1,0:T(8,128)S(1)} %get-tuple-element.78.head, f32[4,64,128]{2,1,0:T(8,128)S(1)} %get-tuple-element.79.joins, f32[16,64,128]{2,1,0:T(8,128)S(1)} %get-tuple-element.80.y_local, ...), custom_call_target="tpu_custom_call" | custom-call | flops 2000000000 | bytes 4000000 | tf_op jit(solution)/shard_map/pallas_call | solution.py:460
  48.8 0.0 collective-permute-done.8.other
  48.8 0.4 shard_map.57
  49.2 3.1 %collective-permute-start.10 = (f32[64,256]{1,0:T(8,128)S(1)}, f32[64,256]{1,0:T(8,128)S(1)}, u32[]{:S(2)}, u32[]{:S(2)}) collective-permute-start(f32[64,256]{1,0:T(8,128)S(1)} %get-tuple-element.88), channel_id=1, source_target_pairs={{0,16},{4,20},{8,24},{12,28},{16,0},{20,4},{24,8},{28,12},{1,17},{... | collective-permute-start | bytes 196616 | tf_op jit(solution)/shard_map/ppermute | solution.py:234
  52.2 2.6 %collective-permute-start.11 = (f32[64,128]{1,0:T(8,128)S(1)}, f32[64,128]{1,0:T(8,128)S(1)}, u32[]{:S(2)}, u32[]{:S(2)}) collective-permute-start(f32[64,128]{1,0:T(8,128)S(1)} %get-tuple-element.94), channel_id=1, source_target_pairs={{0,4},{4,8},{8,12},{12,16},{16,20},{20,24},{24,28},{28,0},{1,5},{5... | collective-permute-start | bytes 98312 | tf_op jit(solution)/shard_map/ppermute | solution.py:229
  54.9 4.0 %collective-permute-done.11.tail = f32[64,128]{1,0:T(8,128)S(1)} collective-permute-done((f32[64,128]{1,0:T(8,128)S(1)}, f32[64,128]{1,0:T(8,128)S(1)}, u32[]{:S(2)}, u32[]{:S(2)}) %collective-permute-start.11) | collective-permute-done | bytes 32800 | tf_op jit(solution)/shard_map/ppermute | solution.py:229
  58.9 0.0 collective-permute-done.10.half
  58.9 0.0 collective-permute-done.12.seam
  58.9 2.1 %shard_map.59 = f32[64,2048]{1,0:T(8,128)} custom-call(s32[2]{0:T(128)S(1)} %copy-done.3, f32[64,256]{1,0:T(8,128)S(1)} %collective-permute-done.10.half, f32[3,128,128]{2,1,0:T(8,128)S(1)} %get-tuple-element.89.inside.inner, f32[64,256]{1,0:T(8,128)S(1)} %get-tuple-element.90.before, f32[64,2048]{1,0:T(8,128)S(1)} %get-tuple-element.91.base, ...), custom_call_target="tpu_custom_call" | custom-call | flops 1000000000 | bytes 4000000 | tf_op jit(solution)/shard_map/pallas_call | solution.py:460
  (2 shorter events, 0.0 us)
Async XLA Ops:
  0.0 16.6 %collective-permute-start = (f32[64,2048]{1,0:T(8,128)}, f32[64,2048]{1,0:T(8,128)S(1)}, u32[]{:S(2)}, u32[]{:S(2)}) collective-permute-start(f32[64,2048]{1,0:T(8,128)} %refs_0_.1), channel_id=1, source_target_pairs={{0,2},{1,3},{2,0},{3,1},{4,6},{5,7},{6,4},{7,5},{8,10},{9,11},{10,... | collective-permute-start | bytes 1572872 | tf_op jit(solution)/shard_map/ppermute | solution.py:234
  3.0 18.7 %collective-permute-start.1 = (f32[64,2048]{1,0:T(8,128)}, f32[64,2048]{1,0:T(8,128)S(1)}, u32[]{:S(2)}, u32[]{:S(2)}) collective-permute-start(f32[64,2048]{1,0:T(8,128)} %refs_0_.1), channel_id=1, source_target_pairs={{0,1},{1,0},{2,3},{3,2},{4,5},{5,4},{6,7},{7,6},{8,9},{9,8},{10,11... | collective-permute-start | bytes 1572872 | tf_op jit(solution)/shard_map/ppermute | solution.py:234
  3.0 2.2 %copy-start = (f32[2,16,256,128]{3,2,1,0:T(8,128)S(1)}, f32[2,16,256,128]{3,2,1,0:T(8,128)}, u32[]{:S(2)}) copy-start(f32[2,16,256,128]{3,2,1,0:T(8,128)} %source.1) | copy-start | bytes 12582916
  5.2 16.5 %copy-start.1 = (f32[64,2048]{1,0:T(8,128)S(1)}, f32[64,2048]{1,0:T(8,128)}, u32[]{:S(2)}) copy-start(f32[64,2048]{1,0:T(8,128)} %refs_0_.1) | copy-start | bytes 1572868
  5.2 16.5 %copy-start.2 = (f32[256,256]{1,0:T(8,128)S(1)}, f32[256,256]{1,0:T(8,128)}, u32[]{:S(2)}) copy-start(f32[256,256]{1,0:T(8,128)} %cauchy.1) | copy-start | bytes 786436
  16.6 8.0 %copy-start.3 = (s32[2]{0:T(128)S(1)}, s32[2]{0:T(128)}, u32[]{:S(2)}) copy-start(s32[2]{0:T(128)} %start.11) | copy-start | bytes 28
  16.6 5.0 %collective-permute-start.2 = (f32[64,2048]{1,0:T(8,128)S(1)}, f32[64,2048]{1,0:T(8,128)S(1)}, u32[]{:S(2)}, u32[]{:S(2)}) collective-permute-start(f32[64,2048]{1,0:T(8,128)S(1)} %collective-permute-done.refs_1_), channel_id=1, source_target_pairs={{0,1},{1,0},{2,3},{3,2},{4,5},{5,4},{6,7},{7,6},{8,9},{9,8},{10,11... | collective-permute-start | bytes 1572872 | tf_op jit(solution)/shard_map/ppermute | solution.py:234
  17.1 7.5 %collective-permute-start.3 = (f32[128,256]{1,0:T(8,128)S(1)}, f32[128,256]{1,0:T(8,128)S(1)}, u32[]{:S(2)}, u32[]{:S(2)}) collective-permute-start(f32[128,256]{1,0:T(8,128)S(1)} %get-tuple-element.56), channel_id=1, source_target_pairs={{0,28},{4,0},{8,4},{12,8},{16,12},{20,16},{24,20},{28,24},{1,29},{... | collective-permute-start | bytes 393224 | tf_op jit(solution)/shard_map/ppermute | solution.py:229
  22.6 5.1 %collective-permute-start.4 = (f32[64,256]{1,0:T(8,128)S(1)}, f32[64,256]{1,0:T(8,128)S(1)}, u32[]{:S(2)}, u32[]{:S(2)}) collective-permute-start(f32[64,256]{1,0:T(8,128)S(1)} %slice.4), channel_id=1, source_target_pairs={{0,28},{4,0},{8,4},{12,8},{16,12},{20,16},{24,20},{28,24},{1,29},{... | collective-permute-start | bytes 196616 | tf_op jit(solution)/shard_map/ppermute | solution.py:229
  27.2 11.3 %collective-permute-start.7 = (f32[3,128,128]{2,1,0:T(8,128)S(1)}, f32[3,128,128]{2,1,0:T(8,128)S(1)}, u32[]{:S(2)}, u32[]{:S(2)}) collective-permute-start(f32[3,128,128]{2,1,0:T(8,128)S(1)} %pad_maximum_fusion.mine), channel_id=1, source_target_pairs={{0,4},{4,0},{8,12},{12,8},{16,20},{20,16},{24,28},{28,24},{1,5},{5... | collective-permute-start | bytes 589832 | tf_op jit(solution)/shard_map/ppermute | solution.py:234
  29.5 6.8 %collective-permute-start.5 = (f32[2,64,128]{2,1,0:T(8,128)S(1)}, f32[2,64,128]{2,1,0:T(8,128)S(1)}, u32[]{:S(2)}, u32[]{:S(2)}) collective-permute-start(f32[2,64,128]{2,1,0:T(8,128)S(1)} %get-tuple-element.69), channel_id=1, source_target_pairs={{0,28},{4,0},{8,4},{12,8},{16,12},{20,16},{24,20},{28,24},{1,29},{... | collective-permute-start | bytes 196616 | tf_op jit(solution)/shard_map/ppermute | solution.py:229
  38.4 4.3 %collective-permute-start.6 = (f32[64,256]{1,0:T(8,128)S(1)}, f32[64,256]{1,0:T(8,128)S(1)}, u32[]{:S(2)}, u32[]{:S(2)}) collective-permute-start(f32[64,256]{1,0:T(8,128)S(1)} %get-tuple-element.70.mine), channel_id=1, source_target_pairs={{0,4},{4,0},{8,12},{12,8},{16,20},{20,16},{24,28},{28,24},{1,5},{5... | collective-permute-start | bytes 196616 | tf_op jit(solution)/shard_map/ppermute | solution.py:234
  38.8 6.4 %collective-permute-start.9 = (f32[3,128,128]{2,1,0:T(8,128)S(1)}, f32[3,128,128]{2,1,0:T(8,128)S(1)}, u32[]{:S(2)}, u32[]{:S(2)}) collective-permute-start(f32[3,128,128]{2,1,0:T(8,128)S(1)} %get-tuple-element.74.mine), channel_id=1, source_target_pairs={{0,8},{4,12},{8,0},{12,4},{16,24},{20,28},{24,16},{28,20},{1,9},{5... | collective-permute-start | bytes 589832 | tf_op jit(solution)/shard_map/ppermute | solution.py:234
  42.9 5.9 %collective-permute-start.8 = (f32[64,256]{1,0:T(8,128)S(1)}, f32[64,256]{1,0:T(8,128)S(1)}, u32[]{:S(2)}, u32[]{:S(2)}) collective-permute-start(f32[64,256]{1,0:T(8,128)S(1)} %get-tuple-element.73.mine), channel_id=1, source_target_pairs={{0,8},{4,12},{8,0},{12,4},{16,24},{20,28},{24,16},{28,20},{1,9},{5... | collective-permute-start | bytes 196616 | tf_op jit(solution)/shard_map/ppermute | solution.py:234
  46.5 12.4 %collective-permute-start.12 = (f32[256,128]{1,0:T(8,128)S(1)}, f32[256,128]{1,0:T(8,128)S(1)}, u32[]{:S(2)}, u32[]{:S(2)}) collective-permute-start(f32[256,128]{1,0:T(8,128)S(1)} %shard_map.58), channel_id=1, source_target_pairs={{0,4},{4,8},{8,12},{12,16},{16,20},{20,24},{24,28},{28,0},{1,5},{5... | collective-permute-start | bytes 393224 | tf_op jit(solution)/shard_map/ppermute | solution.py:229
  49.2 9.7 %collective-permute-start.10 = (f32[64,256]{1,0:T(8,128)S(1)}, f32[64,256]{1,0:T(8,128)S(1)}, u32[]{:S(2)}, u32[]{:S(2)}) collective-permute-start(f32[64,256]{1,0:T(8,128)S(1)} %get-tuple-element.88), channel_id=1, source_target_pairs={{0,16},{4,20},{8,24},{12,28},{16,0},{20,4},{24,8},{28,12},{1,17},{... | collective-permute-start | bytes 196616 | tf_op jit(solution)/shard_map/ppermute | solution.py:234
  52.2 6.6 %collective-permute-start.11 = (f32[64,128]{1,0:T(8,128)S(1)}, f32[64,128]{1,0:T(8,128)S(1)}, u32[]{:S(2)}, u32[]{:S(2)}) collective-permute-start(f32[64,128]{1,0:T(8,128)S(1)} %get-tuple-element.94), channel_id=1, source_target_pairs={{0,4},{4,8},{8,12},{12,16},{16,20},{20,24},{24,28},{28,0},{1,5},{5... | collective-permute-start | bytes 98312 | tf_op jit(solution)/shard_map/ppermute | solution.py:229

commit v3 on v2

v3 whole, which is shorter than its diff:
```python
import functools

import jax
import jax.numpy as jnp
from jax import lax
from jax.experimental import pallas as pl
from jax.experimental.pallas import tpu as pltpu
from jax.sharding import PartitionSpec as P

F32, BF16 = jnp.float32, jnp.bfloat16
VMEM = pl.BlockSpec(memory_space=pltpu.VMEM)
SMEM = pl.BlockSpec(memory_space=pltpu.SMEM)
NN = (((1,), (0,)), ((), ()))
NT = (((1,), (1,)), ((), ()))
TN = (((0,), (0,)), ((), ()))


def split(value):
    high = value.astype(BF16)
    return high, (value - high.astype(F32)).astype(BF16)


def dot(left, right, dims=NN):
    return lax.dot_general(left, right, dims, preferred_element_type=F32)


def wide(value):
    return jnp.concatenate(split(value), axis=1)


def tall(value):
    terms = [jnp.concatenate([term, term], axis=1) for term in split(value)]
    return jnp.concatenate(terms, axis=0)


def doubled(rows_high, rows_low):
    return jnp.concatenate([rows_high, rows_low], axis=0)


def folded(product):
    half = product.shape[0] // 2
    return product[:half] + product[half:]


def apply(left, high, low):
    if left.shape[1] <= 128:
        return folded(dot(tall(left), doubled(high, low)))
    left_high, left_low = split(left)
    return folded(dot(jnp.concatenate([left_high, left_low], axis=0), high)) + dot(left_high, low)


def times(left, right):
    return apply(left, *split(right))


def eye(rows, columns):
    shape = (rows, columns)
    return lax.broadcasted_iota(jnp.int32, shape, 0) == lax.broadcasted_iota(jnp.int32, shape, 1)


def upper_inverses(grams):
    spread = grams[0].shape[0]
    base = spread // 4
    diagonal = eye(spread, spread)
    above = lax.broadcasted_iota(jnp.int32, (spread, spread), 0) < lax.broadcasted_iota(
        jnp.int32, (spread, spread), 1
    )
    halves = [jnp.where(diagonal, 0.5 * gram, 0.0) for gram in grams]
    columns = [jnp.sum(half, axis=0, keepdims=True) for half in halves]
    scaled = [
        jnp.where(above, gram, 0.0) / jnp.sum(half, axis=1, keepdims=True)
        for gram, half in zip(grams, halves)
    ]

    def owner(size):
        return lax.broadcasted_iota(jnp.int32, (size, spread), 1) // size

    def compact(value, size, row=lambda block: block):
        owns = owner(size)
        result = value[row(0) * size : (row(0) + 1) * size]
        for block in range(1, spread // size):
            at = row(block) * size
            result = jnp.where(owns == block, value[at : at + size], result)
        return result

    def expanded(value, size, row=lambda block: block):
        owns = owner(size)
        masks = [(owns == block).astype(BF16) for block in range(spread // size)]
        terms = []
        for term in split(value):
            rows = [jnp.zeros_like(term)] * (spread // size)
            for block, mask in enumerate(masks):
                if row(block) is not None:
                    rows[row(block)] = term * mask
            terms.append(jnp.concatenate(rows, axis=0))
        return doubled(*terms)

    size = base
    unit = compact(diagonal.astype(F32), size)
    powers = [compact(value, size) for value in scaled]
    results = [unit - power for power in powers]
    rights = [expanded(power, size) for power in powers]
    powers = [folded(dot(tall(power), right)) for power, right in zip(powers, rights)]
    reach = 2
    while reach < size:
        reach *= 2
        rights = [expanded(power, size) for power in powers]
        if reach < size:
            lefts = [jnp.concatenate([r, p], axis=0) for r, p in zip(results, powers)]
        else:
            lefts = results
        products = [folded(dot(tall(left), right)) for left, right in zip(lefts, rights)]
        results = [result + product[:size] for result, product in zip(results, products)]
        if reach < size:
            powers = [product[size:] for product in products]
    while size < spread:
        odd = lax.rem(owner(size), 2) == 1
        edges = [
            jnp.where(odd, compact(value, size, lambda block: block & ~1), 0.0) for value in scaled
        ]
        rights = [expanded(result, size) for result in results]
        products = [folded(dot(tall(edge), right)) for edge, right in zip(edges, rights)]
        rights = [
            expanded(product, size, lambda block: block - 1 if block & 1 else None)
            for product in products
        ]
        products = [folded(dot(tall(result), right)) for result, right in zip(results, rights)]
        results = [
            jnp.concatenate(
                [jnp.where(odd, -product, result), jnp.where(odd, result, 0.0)], axis=0
            )
            for result, product in zip(results, products)
        ]
        size *= 2
    return [result / column for result, column in zip(results, columns)]


def reflectors(values, active):
    double, spread = values[0].shape
    pairs = [wide(value) for value in values]
    grams = [dot(pair, pair, TN) for pair in pairs]
    grams = [
        (g[:spread, :spread] + g[spread:, spread:]) + (g[:spread, spread:] + g[spread:, :spread])
        for g in grams
    ]
    triangles = upper_inverses(grams)
    unit = eye(double, double).astype(F32)
    scaled = []
    for pair, triangle in zip(pairs, triangles):
        high, low = split(triangle)
        right = jnp.concatenate(
            [jnp.concatenate([high, high], axis=1), jnp.concatenate([low, low], axis=1)], axis=0
        )
        product = dot(pair, right, NT)
        scaled.append(product[:, :spread] + product[:, spread:])
    for pair, value, kept in zip(pairs, scaled, active):
        product = folded(dot(tall(value), pair, NT))
        yield split(unit - jnp.where(kept, product, 0.0))


def runs_of(slots, extra=0):
    size = next(size for size in (4, 2, 1) if slots % size == 0)
    bounds = [0, 1] + list(range(size, slots + 1, size)) if size > 1 else list(range(slots + 1))
    runs = list(zip(bounds[:-1], bounds[1:]))
    runs[-1] = (runs[-1][0], runs[-1][1] + extra)
    return runs


def edges_kernel(source, last, first):
    last[...] = source[:, source.shape[1] - 1]
    first[...] = source[0, :2]


def reflect_kernel(sweeps, last_slot, source, *refs):
    count, double, spread = source.shape[1:]
    found = [refs[i * 7 : i * 7 + 7] for i in range(len(sweeps))]
    limit = last_slot - lax.axis_index("row") * count
    values = [source[sweep, b] for sweep in sweeps for b in range(count)]
    active = [b <= limit for _ in sweeps for b in range(count)]
    for i, (high, low) in enumerate(reflectors(values, active)):
        found[i // count][0][i % count] = high
        found[i // count][1][i % count] = low
    runs = runs_of(count, 1)[1:]
    state = [[None] * len(runs) for _ in found]
    for step in range(max(stop - at for at, stop in runs)):
        for j, (at, stop) in enumerate(runs):
            if at + step >= stop:
                continue
            for i, (k_high, k_low, q_high, q_low, maps, upto, beyond) in enumerate(found):
                b = at + step - 1
                high, low = k_high[b, :spread, :], k_low[b, :spread, :]
                if step == 0:
                    both = high.astype(F32) + low.astype(F32)
                else:
                    both = apply(state[i][j], high, low)
                state[i][j] = both[:, spread:]
                q_high[b], q_low[b] = split(both[:, :spread])
                if b == count - 2 or (at + step + 1 == stop and b < count - 1):
                    maps[j] = both[:, spread:]
                if b == count - 1:
                    beyond[...] = both[:, spread:]
    for i, (_, _, _, _, maps, upto, _) in enumerate(found):
        so_far = maps[0]
        upto[0] = so_far
        for j in range(1, len(runs)):
            so_far = times(so_far, maps[j])
            upto[j] = so_far


def reflect(refl_v, sweeps):
    slots, double, spread = refl_v.shape[1:]
    runs = len(runs_of(slots)) - 1
    shape = jax.ShapeDtypeStruct
    shapes = [shape((slots, double, double), BF16)] * 2
    shapes += [shape((slots, spread, spread), BF16)] * 2
    shapes += [shape((runs, spread, spread), F32)] * 2 + [shape((spread, spread), F32)]
    results = whole_call(
        functools.partial(reflect_kernel, sweeps, lax.axis_size("row") * slots - 3),
        shapes * len(sweeps), len(sweeps) * slots * 300_000_000, [], [refl_v], vmem=24,
    )
    return [results[i * 7 : i * 7 + 7] for i in range(len(sweeps))]


def edge_kernel(
    count, last_slot, left, right, upto1, upto2, beyond, left_high, left_low, right_high, right_low,
    q_high, q_low, reach, total,
):
    sweeps, _, spread = left.shape
    extra = right.shape[0]
    first = lax.axis_index("row") * count
    values = [left[i] for i in range(sweeps)] + [right[i] for i in range(extra)]
    active = [(first > 0) & (first - 1 <= last_slot)] * sweeps
    active += [first + count + i <= last_slot for i in range(extra)]
    for i, (high, low) in enumerate(reflectors(values, active)):
        if i < sweeps:
            left_high[i], left_low[i] = high, low
        else:
            right_high[i - sweeps], right_low[i - sweeps] = high, low
    state = beyond[...]
    for i in range(extra):
        both = apply(state, right_high[i, :spread, :], right_low[i, :spread, :])
        q_high[i], q_low[i] = split(both[:, :spread])
        state = both[:, spread:]
    for i, upto in enumerate((upto1, upto2)):
        entry = left_high[i, :spread, spread:].astype(F32) + left_low[i, :spread, spread:].astype(F32)
        reach[i, 0] = entry
        for j in range(upto.shape[0] - 1):
            reach[i, j + 1] = times(entry, upto[j])
        total[i] = times(entry, upto[upto.shape[0] - 1])


def merge_kernel(owners, cauchy, *refs):
    pieces, (merged, chosen) = refs[:-2], refs[-2:]
    rows, columns = pieces[0].shape
    mine = lax.axis_index("col")
    chosen[...] = rolled(cauchy[...], mine * rows)[:, : chosen.shape[1]]
    left = [
        chosen[pl.ds(pl.multiple_of((mine ^ owner) * rows, rows), rows), :rows] for owner in owners
    ]
    left_high, left_low = split(jnp.concatenate(left, axis=0))
    step = columns // 4
    for part in range(4):
        at = slice(part * step, (part + 1) * step)
        right_high, right_low = split(jnp.concatenate([piece[:, at] for piece in pieces], axis=0))
        merged[:, at] = dot(left_high, right_high, TN) + (
            dot(left_high, right_low, TN) + dot(left_low, right_high, TN)
        )


def shifted(array, by):
    devices = lax.axis_size("row")
    return lax.ppermute(array, "row", [(i, (i + by) % devices) for i in range(devices)])


def swapped(array, axis, distance):
    devices = lax.axis_size(axis)
    return lax.ppermute(array, axis, [(i, i ^ distance) for i in range(devices)])


def after_all(array, *others):
    return lax.optimization_barrier((array, *others))[0]


def rolled(value, left):
    width = value.shape[1]
    return pltpu.roll(value, lax.rem(width - left, width), 1)


def slot_table(left, own, right=None):
    (left_ref, at), extra = left, 0 if right is None else right.shape[0]
    table = [(left_ref, at)] + [(own, b) for b in range(own.shape[0])]
    return table + [(right, b) for b in range(extra)]


def chain(aligned, k_high, k_low, runs, maps, slots, y_local, joins):
    rows, spread = joins.shape[1:]
    carry = [jnp.zeros((rows, spread), F32)] * len(runs)
    ends = [None] * len(runs)
    for step in range(max(stop - at for at, stop in runs)):
        for j, (at, stop) in enumerate(runs):
            slot = at + step
            if slot >= stop:
                continue
            fresh = aligned[:, slot * spread : (slot + 1) * spread]
            (high, b), (low, _) = k_high[slot], k_low[slot]
            both = apply(jnp.concatenate([carry[j], fresh], axis=1), high[b], low[b])
            y_local[slot] = both[:, :spread]
            carry[j] = both[:, spread:]
            if slot + 1 == min(stop, slots):
                ends[j] = carry[j]
    joins[0] = jnp.zeros_like(carry[0])
    so_far = ends[0]
    for j in range(1, len(runs)):
        joins[j] = so_far
        so_far = times(so_far, maps[j - 1]) + ends[j]
    return so_far


def terms(table, runs):
    return [jnp.concatenate([ref[b] for ref, b in table[at:stop]], axis=1) for at, stop in runs]


def settled(runs, joins, q_high, q_low, y_local, line):
    spread = y_local.shape[2]
    highs, lows = terms(q_high, runs[1:]), terms(q_low, runs[1:])
    for j, (at, stop) in enumerate(runs):
        added = apply(joins[j], highs[j - 1], lows[j - 1]) if j else None
        for slot in range(at, stop):
            value = y_local[slot]
            if j:
                value = value + added[:, (slot - at) * spread : (slot - at + 1) * spread]
            line[:, slot * spread : (slot + 1) * spread] = value


def reached(runs, entry, reach, q_high, q_low, line):
    spread = entry.shape[0]
    line[:, :spread] = entry
    highs, lows = terms(q_high, runs[1:]), terms(q_low, runs[1:])
    for j, (at, stop) in enumerate(runs[1:]):
        line[:, at * spread : stop * spread] = apply(reach[j], highs[j], lows[j])


def first_kernel(
    count, start, home, after, left_high, left_low, k_high, k_low, right_high, right_low, maps,
    q_high, q_low, q_right_high, q_right_low, line, state, y_local, joins,
):
    spread = state.shape[1]
    offset = start[0]
    aligned = rolled(jnp.concatenate([home[...], after[...]], axis=1), offset)
    runs = runs_of(count, y_local.shape[0] - count)
    highs = slot_table((left_high, 0), k_high, right_high)
    lows = slot_table((left_low, 0), k_low, right_low)
    state[...] = chain(aligned, highs, lows, runs, maps, count, y_local, joins)
    q_highs = slot_table((None, 0), q_high, q_right_high)
    q_lows = slot_table((None, 0), q_low, q_right_low)
    settled(runs, joins, q_highs, q_lows, y_local, line)

    @pl.when(lax.axis_index("row") == 0)
    def _():
        line[:, :spread] = pltpu.roll(home[:, :spread], lax.rem(spread - offset, spread), 1)


def second_kernel(
    count, start, line, state_in, left_high, left_low, k_high, k_low, maps, y_local, joins, state,
    head,
):
    spread = head.shape[1]
    ahead = start[1] - start[0]
    aligned = rolled(line[...], ahead + spread)
    runs = runs_of(count, y_local.shape[0] - count)
    highs, lows = slot_table((left_high, 1), k_high), slot_table((left_low, 1), k_low)
    state[:, spread:] = chain(aligned, highs, lows, runs, maps, count, y_local, joins)
    state[:, :spread] = state_in[...]
    head[...] = pltpu.roll(
        line[:, : 2 * spread], lax.rem(4 * spread - ahead, 2 * spread), 1
    )[:, :spread]


def base_kernel(count, start, head, joins, y_local, q_high, q_low, base, line):
    spread = head.shape[1]
    runs = runs_of(count, y_local.shape[0] - count)
    q_highs, q_lows = slot_table((None, 0), q_high), slot_table((None, 0), q_low)
    settled(runs, joins, q_highs, q_lows, y_local, line)

    @pl.when(lax.axis_index("row") == 0)
    def _():
        line[:, :spread] = head[...]

    base[...] = rolled(line[...], spread - start[1])[:, : base.shape[1]]


def response_kernel(
    count, start, q_high, q_low, q_right_high, q_right_low, reach, left_high, left_low, k_high,
    k_low, maps, y_local, joins, gamma, line,
):
    spread = gamma.shape[0]
    entry = left_high[0, :spread, :spread].astype(F32) + left_low[0, :spread, :spread].astype(F32)
    q_highs = slot_table((None, 0), q_high, q_right_high)
    q_lows = slot_table((None, 0), q_low, q_right_low)
    reached(runs_of(count, line.shape[1] // spread - count), entry, reach.at[0], q_highs, q_lows, line)
    aligned = rolled(line[...], start[1] - start[0] + spread)
    runs = runs_of(count, y_local.shape[0] - count)
    highs, lows = slot_table((left_high, 1), k_high), slot_table((left_low, 1), k_low)
    gamma[...] = chain(aligned, highs, lows, runs, maps, count, y_local, joins)


def home_kernel(
    count, start, joins, y_local, q_high, q_low, reach, left_high, left_low, high, low, line
):
    spread, columns = line.shape[0], high.shape[1]
    runs = runs_of(count, y_local.shape[0] - count)
    q_highs, q_lows = slot_table((None, 0), q_high), slot_table((None, 0), q_low)
    for sweep in range(2):
        at = slice(sweep * spread, (sweep + 1) * spread)
        if sweep == 0:
            settled(runs, joins, q_highs, q_lows, y_local, line)
        else:
            entry = left_high[1, :spread, :spread].astype(F32)
            entry = entry + left_low[1, :spread, :spread].astype(F32)
            reached(runs, entry, reach.at[1], q_highs, q_lows, line)
        high[at], low[at] = split(rolled(line[...], spread - start[1])[:, :columns])


def is_upper(level):
    return lax.rem(lax.axis_index("row") // (1 << level), 2) == 1


def through(states, maps):
    spread = maps.shape[1]
    first, second = states[:, :spread], states[:, spread:]
    return jnp.concatenate(
        [times(first, maps[0]), times(first, maps[1]) + times(second, maps[2])], axis=1
    )


def join_maps_kernel(level, *refs):
    upper = is_upper(level)
    if level:
        mine, other, inner, high, both, inside = refs
        mine, other = [mine[i] for i in range(3)], [other[i] for i in range(3)]
    else:
        mine, gamma, other, gamma_other, high, both, inside = refs
        mine, other = [mine[0], gamma[...], mine[1]], [other[0], gamma_other[...], other[1]]
    spread = both.shape[1]
    low = [jnp.where(upper, other[i], mine[i]) for i in range(3)]
    for i in range(3):
        high[i] = jnp.where(upper, mine[i], other[i])

    def joined(later):
        return [
            times(low[0], later[0]),
            times(low[0], later[1]) + times(low[1], later[2]),
            times(low[2], later[2]),
        ]

    for i, value in enumerate(joined(high)):
        both[i] = value
    if level:
        for i, value in enumerate(joined(inner)):
            inside[i] = jnp.where(upper, value, inner[i])
    else:
        unit = eye(spread, spread).astype(F32)
        for i, value in enumerate([unit, jnp.zeros_like(unit), unit]):
            inside[i] = jnp.where(upper, low[i], value)


def join_states_kernel(level, mine, other, high, *refs):
    upper = is_upper(level)
    if level:
        inner, before, refs = refs[0], refs[1], refs[2:]
    low = jnp.where(upper, other[...], mine[...])
    refs[0][...] = through(low, high) + jnp.where(upper, mine[...], other[...])
    if level:
        refs[1][...] = before[...] + jnp.where(upper, through(low, inner), 0.0)
    else:
        refs[1][...] = jnp.where(upper, low, 0.0)


def final_kernel(levels, half, inner, before, base, high, low, out):
    enters = jnp.where(is_upper(levels - 1), half[...], 0.0)
    incoming = before[...] + through(enters, inner)
    out[...] = base[...] + apply(incoming, high[...], low[...])


def whole_call(kernel, shapes, flops, scalars, arrays, scratch=(), vmem=8):
    return pl.pallas_call(
        kernel,
        out_shape=shapes,
        in_specs=[SMEM] * len(scalars) + [VMEM] * len(arrays),
        out_specs=jax.tree.map(lambda shape: VMEM, shapes),
        scratch_shapes=list(scratch),
        compiler_params=pltpu.CompilerParams(vmem_limit_bytes=vmem << 20),
        cost_estimate=pl.CostEstimate(
            flops=flops, bytes_accessed=4_000_000, transcendentals=0
        ),
    )(*scalars, *arrays)


def shards(panel, cauchy, refl_v, block_start):
    rows, columns = panel.shape
    slots, _, spread = refl_v.shape[1:]
    levels = lax.axis_size("row").bit_length() - 1
    last_slot = lax.axis_size("row") * slots - 3
    shape = functools.partial(jax.ShapeDtypeStruct, dtype=F32)
    starts = [block_start]
    count, runs = lax.axis_size("col"), len(runs_of(slots))
    square = (spread, spread)

    pieces, owners = [panel], [0]
    distance = count // 2
    while distance:
        pieces += [swapped(piece, "col", distance) for piece in pieces]
        if owners == [0]:
            pair = shape((2,) + refl_v.shape[2:])
            left, right = whole_call(edges_kernel, [pair, pair], 10_000_000, [], [refl_v])
            left, right = shifted(left, 1), shifted(right, -1)
            if slots <= 16:
                one, two = reflect(refl_v, (0, 1))
            else:
                [one], [two] = reflect(refl_v, (0,)), reflect(refl_v, (1,))
            high1, low1, qh1, ql1, maps1, upto1, beyond = one
            high2, low2, qh2, ql2, maps2, upto2, _ = two
            pieces[-1] = after_all(pieces[-1], beyond, left, right)
        owners += [owner ^ distance for owner in owners]
        distance //= 2
    k_pair = jax.ShapeDtypeStruct((2,) + (2 * spread, 2 * spread), BF16)
    q_pair = jax.ShapeDtypeStruct((2,) + square, BF16)
    lh, ll, rh, rl, qrh, qrl, reach, totals = whole_call(
        functools.partial(edge_kernel, slots, last_slot),
        [k_pair] * 4 + [q_pair] * 2 + [shape((2, runs - 1) + square), shape((2,) + square)],
        2_000_000_000, [], [left, right, upto1, upto2, beyond],
    )
    totals_other = swapped(totals, "row", 1)
    pieces[0] = after_all(pieces[0], totals)
    merged = whole_call(
        functools.partial(merge_kernel, owners), shape((rows, columns)),
        1_000_000_000, [], [cauchy] + pieces,
        [pltpu.VMEM((cauchy.shape[0], 128 * pl.cdiv(rows, 128)), F32)],
    )
    after = shifted(merged[:, : 4 * spread], -1)

    y_response, joins_response, gamma = whole_call(
        functools.partial(response_kernel, slots),
        [shape((slots + 1,) + square), shape((runs,) + square), shape(square)],
        4_000_000_000, starts,
        [qh1, ql1, qrh, qrl, after_all(reach, merged), lh, ll, high2, low2, maps2],
        [pltpu.VMEM((spread, columns + 3 * spread), F32)],
    )
    line, state1 = whole_call(
        functools.partial(first_kernel, slots),
        [shape((rows, columns + 3 * spread)), shape((rows, spread))], 3_000_000_000, starts,
        [after_all(merged, gamma), after, lh, ll, high1, low1, rh, rl, maps1, qh1, ql1, qrh, qrl],
        [pltpu.VMEM((slots + 3, rows, spread), F32), pltpu.VMEM((runs, rows, spread), F32)],
    )
    groups = []
    for level in range(levels - 1):
        if level:
            arrays = [maps, swapped(maps, "row", 1 << level), inside]
        else:
            arrays = [after_all(totals, state1), gamma, totals_other, swapped(gamma, "row", 1)]
        high, maps, inside = whole_call(
            functools.partial(join_maps_kernel, level), [shape((3,) + square)] * 3,
            400_000_000, [], arrays,
        )
        groups.append((high, inside))

    states = shape((rows, 2 * spread))
    y2, joins2, state, head2 = whole_call(
        functools.partial(second_kernel, slots),
        [shape((slots + 1, rows, spread)), shape((runs, rows, spread)), states,
         shape((rows, spread))],
        3_000_000_000, starts,
        [after_all(line, groups[0][0]), state1, lh, ll, high2, low2, maps2],
    )
    home = jax.ShapeDtypeStruct((2 * spread, columns), BF16)
    home_high, home_low = whole_call(
        functools.partial(home_kernel, slots), [home, home], 3_000_000_000, starts,
        [after_all(joins_response, state), y_response, qh2, ql2, reach, lh, ll],
        [pltpu.VMEM((spread, columns + spread), F32)],
    )
    base = whole_call(
        functools.partial(base_kernel, slots), shape((rows, columns)), 2_000_000_000, starts,
        [head2, joins2, y2, qh2, ql2], [pltpu.VMEM((rows, columns + spread), F32)],
    )
    enters = None
    for level in range(levels - 1):
        other = after_all(swapped(state, "row", 1 << level), groups[-1][0])
        arrays = [state, other, groups[level][0]]
        arrays += [groups[level - 1][1], enters] if level else []
        state, enters = whole_call(
            functools.partial(join_states_kernel, level), [states] * 2, 100_000_000, [], arrays,
        )
    half = swapped(state, "row", 1 << (levels - 1))
    return whole_call(
        functools.partial(final_kernel, levels), shape((rows, columns)), 1_000_000_000, [],
        [half, groups[-1][1], enters, base, home_high, home_low],
    )


def solution(mesh):
    placed = (P("col", "row"), P(), P(None, "row", None, None), P())
    return jax.shard_map(
        shards, mesh=mesh, in_specs=placed, out_specs=P("col", "row"), check_vma=False
    )
```

time: 61.1 us -> 56.2 us (0.920)
  starting transfers between devices: 22.5 us -> 18.4 us
  waiting for transfers between devices: 10.1 us -> 6.05 us
  Pallas kernels: 26 us -> 29.3 us
    ppermute x5 -> x3, starting transfers between devices: 15.1 us -> 9.27 us  [shifted(): lax.ppermute(array, 'row', [(i, (i + by) % devices) for i in range(device...]
    ppermute x5 -> x3, waiting for transfers between devices: 5.91 us -> 0.15 us  [shifted(): lax.ppermute(array, 'row', [(i, (i + by) % devices) for i in range(device...]
    pallas_call x14, Pallas kernels: 26 us -> 29.3 us  [whole_call(): pl.pallas_call(kernel, out_shape=shapes, in_specs=[SMEM] * len(scalars) +...]
    ppermute x8 -> x9, starting transfers between devices: 7.38 us -> 9.12 us  [swapped(): lax.ppermute(array, axis, [(i, i ^ distance) for i in range(devices)])]
    ppermute x8 -> x9, waiting for transfers between devices: 4.18 us -> 5.9 us  [swapped(): lax.ppermute(array, axis, [(i, i ^ distance) for i in range(devices)])]
    unnamed x8 -> x10, local copies, waits for them, and re-layouts: 2.2 us -> 2.21 us
  transfers between devices with their start and end apart: 13 -> 12, of which waited for: 5 -> 5; matrix products, arithmetic and copies ran while one was open for 0% -> 0% of each run, Pallas kernels for 39% -> 48%
where the time goes in v3:
time: 56.2 us; the launch traced here: 56.1 us
  Pallas kernels  29.3 us (52%)
  starting transfers between devices  18.4 us (33%)
  waiting for transfers between devices  6.05 us (11%)
  local copies, waits for them, and re-layouts  2.22 us (4%)
    pallas_call x14, Pallas kernels, whole_call(): pl.pallas_call(kernel, out_shape=shapes, in_specs=[SMEM] * len(scalars) +...  29.3 us
    ppermute x3, starting transfers between devices, shifted(): lax.ppermute(array, 'row', [(i, (i + by) % devices) for i in range(device...  9.27 us
    ppermute x9, starting transfers between devices, swapped(): lax.ppermute(array, axis, [(i, i ^ distance) for i in range(devices)])  9.12 us
    ppermute x9, waiting for transfers between devices, swapped(): lax.ppermute(array, axis, [(i, i ^ distance) for i in range(devices)])  5.9 us
    unnamed x10, local copies, waits for them, and re-layouts  2.21 us
  transfers between devices with their start and end apart: 12, of which 5 were waited for; matrix products, arithmetic and copies ran while one was open for 0% of the time, Pallas kernels for 48%

profile of v3, /device:TPU:0, one launch (start us, length us, event | category | flops | bytes accessed | tf_op | source)
XLA Modules:
  0.0 56.1 jit_solution(13094175436067689314)
XLA Ops:
  0.0 3.0 %collective-permute-start.2 = (f32[64,2048]{1,0:T(8,128)}, f32[64,2048]{1,0:T(8,128)S(1)}, u32[]{:S(2)}, u32[]{:S(2)}) collective-permute-start(f32[64,2048]{1,0:T(8,128)} %refs_0_), channel_id=1, source_target_pairs={{0,2},{1,3},{2,0},{3,1},{4,6},{5,7},{6,4},{7,5},{8,10},{9,11},{10,... | collective-permute-start | bytes 1572872 | tf_op jit(solution)/shard_map/ppermute | solution.py:277
  3.0 0.0 collective-permute-start.3
  3.0 0.0 copy-start
  3.0 2.2 %copy-done = f32[2,16,256,128]{3,2,1,0:T(8,128)S(1)} copy-done((f32[2,16,256,128]{3,2,1,0:T(8,128)S(1)}, f32[2,16,256,128]{3,2,1,0:T(8,128)}, u32[]{:S(2)}) %copy-start) | copy-done | bytes 4194328
  5.2 0.0 copy-start.1
  5.2 1.5 %collective-permute-start = (f32[2,256,128]{2,1,0:T(8,128)S(1)}, f32[2,256,128]{2,1,0:T(8,128)S(1)}, u32[]{:S(2)}, u32[]{:S(2)}) collective-permute-start(f32[2,256,128]{2,1,0:T(8,128)S(1)} %get-tuple-element.57), channel_id=1, source_target_pairs={{0,4},{4,8},{8,12},{12,16},{16,20},{20,24},{24,28},{28,0},{1,5},{5... | collective-permute-start | bytes 786440 | tf_op jit(solution)/shard_map/ppermute | solution.py:272
  6.7 3.2 %collective-permute-start.1 = (f32[2,256,128]{2,1,0:T(8,128)S(1)}, f32[2,256,128]{2,1,0:T(8,128)S(1)}, u32[]{:S(2)}, u32[]{:S(2)}) collective-permute-start(f32[2,256,128]{2,1,0:T(8,128)S(1)} %get-tuple-element.58), channel_id=1, source_target_pairs={{0,28},{4,0},{8,4},{12,8},{16,12},{20,16},{24,20},{28,24},{1,29},{... | collective-permute-start | bytes 786440 | tf_op jit(solution)/shard_map/ppermute | solution.py:272
  10.0 0.0 copy-done.1
  10.0 11.0 %shard_map.47 = (bf16[16,256,256]{2,1,0:T(8,128)(2,1)S(1)}, bf16[16,256,256]{2,1,0:T(8,128)(2,1)S(1)}, bf16[16,128,128]{2,1,0:T(8,128)(2,1)S(1)}, bf16[16,128,12...) custom-call(f32[2,16,256,128]{3,2,1,0:T(8,128)S(1)} %copy-done.1), custom_call_target="tpu_custom_call" | custom-call | flops 9600000000 | bytes 4000000 | tf_op jit(solution)/shard_map/pallas_call | solution.py:486
  21.0 0.0 collective-permute-done.left
  21.0 0.0 collective-permute-done.1.right
  21.0 0.0 collective-permute-done.2.refs_1_
  21.0 0.1 collective-permute-start.4
  21.1 0.0 copy-start.2
  21.1 0.0 copy-start.3
  21.1 3.2 %shard_map.48 = (bf16[2,256,256]{2,1,0:T(8,128)(2,1)S(1)}, bf16[2,256,256]{2,1,0:T(8,128)(2,1)S(1)}, bf16[2,256,256]{2,1,0:T(8,128)(2,1)S(1)}, bf16[2,256,256]{2...) custom-call(f32[2,256,128]{2,1,0:T(8,128)S(1)} %collective-permute-d, ...), custom_call_target="tpu_custom_call" | custom-call | flops 2000000000 | bytes 4000000 | tf_op jit(solution)/shard_map/pallas_call | solution.py:486
  24.4 0.0 copy-start.4
  24.4 0.1 collective-permute-start.6
  24.5 0.0 collective-permute-done.3.refs_2_
  24.5 0.0 collective-permute-done.4.refs_3_
  24.5 0.0 copy-done.2
  24.5 0.0 copy-done.3
  24.5 0.9 %shard_map.49.home = f32[64,2048]{1,0:T(8,128)S(1)} custom-call(f32[256,256]{1,0:T(8,128)S(1)} %copy-done.3, f32[64,2048]{1,0:T(8,128)S(1)} %copy-done.2, f32[64,2048]{1,0:T(8,128)S(1)} %collective-permute-done.2.refs_1_, f32[64,2048]{1,0:T(8,128)S(1)} %collective-permute-done.3.refs_2_, f32[64,2048]{1,0:T(8,128)S(1)} %collective-permute-done.4.refs_3_), custom_call_target="tpu_custom_call" | custom-call | flops 1000000000 | bytes 4000000 | tf_op jit(solution)/shard_map/pallas_call | solution.py:486
  25.4 4.5 %collective-permute-start.5 = (f32[64,512]{1,0:T(8,128)S(1)}, f32[64,512]{1,0:T(8,128)S(1)}, u32[]{:S(2)}, u32[]{:S(2)}) collective-permute-start(f32[64,512]{1,0:T(8,128)S(1)} %slice.4), channel_id=1, source_target_pairs={{0,28},{4,0},{8,4},{12,8},{16,12},{20,16},{24,20},{28,24},{1,29},{... | collective-permute-start | bytes 393224 | tf_op jit(solution)/shard_map/ppermute | solution.py:272
  29.9 0.0 copy-done.4
  29.9 3.0 %shard_map.50 = (f32[17,128,128]{2,1,0:T(8,128)S(1)}, f32[5,128,128]{2,1,0:T(8,128)S(1)}, f32[128,128]{1,0:T(8,128)S(1)}) custom-call(s32[2]{0:T(128)S(1)} %copy-done.4, bf16[16,128,128]{2,1,0:T(8,128)(2,1)S(1)} %get-tuple-element.65.q_high, bf16[16,128,128]{2,1,0:T(8,128)(2,1)S(1)} %get-tuple-element.66.q_low, ...), custom_call_target="tpu_custom_call" | custom-call | flops 4000000000 | bytes 4000000 | tf_op jit(solution)/shard_map/pallas_call | solution.py:486
  32.9 0.1 collective-permute-start.7
  33.0 0.1 collective-permute-done.5.after
  33.1 2.8 %shard_map.51 = (f32[64,2432]{1,0:T(8,128)S(1)}, f32[64,128]{1,0:T(8,128)S(1)}) custom-call(s32[2]{0:T(128)S(1)} %copy-done.4, f32[64,2048]{1,0:T(8,128)S(1)} %shard_map.49.home, f32[64,512]{1,0:T(8,128)S(1)} %collective-permute-done.5.after, bf16[2,256,256]{2,1,0:T(8,128)(2,1)S(1)} %get-tuple-element.71.left_high, ...), custom_call_target="tpu_custom_call" | custom-call | flops 3000000000 | bytes 4000000 | tf_op jit(solution)/shard_map/pallas_call | solution.py:486
  35.9 0.0 collective-permute-done.6.refs_2_
  35.9 1.3 %collective-permute-done.7.refs_3_ = f32[128,128]{1,0:T(8,128)S(1)} collective-permute-done((f32[128,128]{1,0:T(8,128)S(1)}, f32[128,128]{1,0:T(8,128)S(1)}, u32[]{:S(2)}, u32[]{:S(2)}) %collective-permute-start.7) | collective-permute-done | bytes 65568 | tf_op jit(solution)/shard_map/ppermute | solution.py:277
  37.2 0.3 shard_map.52
  37.5 0.1 collective-permute-start.9
  37.6 2.1 %shard_map.53 = (f32[17,64,128]{2,1,0:T(8,128)S(1)}, f32[5,64,128]{2,1,0:T(8,128)S(1)}, f32[64,256]{1,0:T(8,128)S(1)}, f32[64,128]{1,0:T(8,128)S(1)}) custom-call(s32[2]{0:T(128)S(1)} %copy-done.4, f32[64,2432]{1,0:T(8,128)S(1)} %get-tuple-element.87.line, f32[64,128]{1,0:T(8,128)S(1)} %get-tuple-element.84.state_in, ...), custom_call_target="tpu_custom_call" | custom-call | flops 3000000000 | bytes 4000000 | tf_op jit(solution)/shard_map/pallas_call | solution.py:486
  39.7 0.6 %collective-permute-start.8 = (f32[64,256]{1,0:T(8,128)S(1)}, f32[64,256]{1,0:T(8,128)S(1)}, u32[]{:S(2)}, u32[]{:S(2)}) collective-permute-start(f32[64,256]{1,0:T(8,128)S(1)} %get-tuple-element.88.mine), channel_id=1, source_target_pairs={{0,4},{4,0},{8,12},{12,8},{16,20},{20,16},{24,28},{28,24},{1,5},{5... | collective-permute-start | bytes 196616 | tf_op jit(solution)/shard_map/ppermute | solution.py:277
  40.3 3.0 %collective-permute-done.9.refs_1_ = f32[3,128,128]{2,1,0:T(8,128)S(1)} collective-permute-done((f32[3,128,128]{2,1,0:T(8,128)S(1)}, f32[3,128,128]{2,1,0:T(8,128)S(1)}, u32[]{:S(2)}, u32[]{:S(2)}) %collective-permute-start.9) | collective-permute-done | bytes 196640 | tf_op jit(solution)/shard_map/ppermute | solution.py:277
  43.3 1.0 %shard_map.54 = (f32[3,128,128]{2,1,0:T(8,128)S(1)}, f32[3,128,128]{2,1,0:T(8,128)}, f32[3,128,128]{2,1,0:T(8,128)S(1)}) custom-call(f32[3,128,128]{2,1,0:T(8,128)S(1)} %get-tuple-element.89.refs_0_, f32[3,128,128]{2,1,0:T(8,128)S(1)} %collective-permute-done.9.refs_1_, f32[3,128,128]{2,1,0:T(8,128)S(1)} %get-tuple-element.90.refs_2_.refs_0_), custom_call_target="tpu_custom_call" | custom-call | flops 400000000 | bytes 4000000 | tf_op jit(solution)/shard_map/pallas_call | solution.py:486
  44.3 0.0 collective-permute-done.8.other
  44.3 0.2 shard_map.55
  44.5 1.9 %collective-permute-start.10 = (f32[64,256]{1,0:T(8,128)S(1)}, f32[64,256]{1,0:T(8,128)S(1)}, u32[]{:S(2)}, u32[]{:S(2)}) collective-permute-start(f32[64,256]{1,0:T(8,128)S(1)} %get-tuple-element.93.mine), channel_id=1, source_target_pairs={{0,8},{4,12},{8,0},{12,4},{16,24},{20,28},{24,16},{28,20},{1,9},{5... | collective-permute-start | bytes 196616 | tf_op jit(solution)/shard_map/ppermute | solution.py:277
  46.3 2.0 %shard_map.58 = (bf16[256,2048]{1,0:T(8,128)(2,1)S(1)}, bf16[256,2048]{1,0:T(8,128)(2,1)S(1)}) custom-call(s32[2]{0:T(128)S(1)} %copy-done.4, f32[5,128,128]{2,1,0:T(8,128)S(1)} %get-tuple-element.105.joins, f32[17,128,128]{2,1,0:T(8,128)S(1)} %get-tuple-element.106.y_local, bf16[16,128,128]{2,1,0:T(8,128)(2,1)S(1)} %get-tuple-element.102.q_high, ...), custom_call_target="tpu_custom_call" | custom-call | flops 3000000000 | bytes 4000000 | tf_op jit(solution)/shard_map/pallas_call | solution.py:486
  48.3 0.5 collective-permute-done.10.other
  48.8 0.3 shard_map.56
  49.1 3.4 %collective-permute-start.11 = (f32[64,256]{1,0:T(8,128)S(1)}, f32[64,256]{1,0:T(8,128)S(1)}, u32[]{:S(2)}, u32[]{:S(2)}) collective-permute-start(f32[64,256]{1,0:T(8,128)S(1)} %get-tuple-element.96), channel_id=1, source_target_pairs={{0,16},{4,20},{8,24},{12,28},{16,0},{20,4},{24,8},{28,12},{1,17},{... | collective-permute-start | bytes 196616 | tf_op jit(solution)/shard_map/ppermute | solution.py:277
  52.4 1.1 %shard_map.57.base = f32[64,2048]{1,0:T(8,128)S(1)} custom-call(s32[2]{0:T(128)S(1)} %copy-done.4, f32[64,128]{1,0:T(8,128)S(1)} %get-tuple-element.99.head, f32[5,64,128]{2,1,0:T(8,128)S(1)} %get-tuple-element.100.joins, f32[17,64,128]{2,1,0:T(8,128)S(1)} %get-tuple-element.101.y_local, bf16[16,128,128]{2,1,0:T(8,128)(2,1)S(1)} %get-tuple-element.102.q_high, ...), custom_call_target="tpu_custom_call" | custom-call | flops 2000000000 | bytes 4000000 | tf_op jit(solution)/shard_map/pallas_call | solution.py:486
  53.6 1.1 %collective-permute-done.11.half = f32[64,256]{1,0:T(8,128)S(1)} collective-permute-done((f32[64,256]{1,0:T(8,128)S(1)}, f32[64,256]{1,0:T(8,128)S(1)}, u32[]{:S(2)}, u32[]{:S(2)}) %collective-permute-start.11) | collective-permute-done | bytes 65568 | tf_op jit(solution)/shard_map/ppermute | solution.py:277
  54.7 1.4 %shard_map.59 = f32[64,2048]{1,0:T(8,128)} custom-call(f32[64,256]{1,0:T(8,128)S(1)} %collective-permute-done.11.half, f32[3,128,128]{2,1,0:T(8,128)S(1)} %get-tuple-element.97.inner, f32[64,256]{1,0:T(8,128)S(1)} %get-tuple-element.98.before, f32[64,2048]{1,0:T(8,128)S(1)} %shard_map.57.base, bf16[256,2048]{1,0:T(8,128)(2,1)S(1)} %get-tuple-element.107.high, ...), custom_call_target="tpu_custom_call" | custom-call | flops 1000000000 | bytes 4000000 | tf_op jit(solution)/shard_map/pallas_call | solution.py:486
  (2 shorter events, 0.1 us)
Async XLA Ops:
  0.0 21.0 %collective-permute-start.2 = (f32[64,2048]{1,0:T(8,128)}, f32[64,2048]{1,0:T(8,128)S(1)}, u32[]{:S(2)}, u32[]{:S(2)}) collective-permute-start(f32[64,2048]{1,0:T(8,128)} %refs_0_), channel_id=1, source_target_pairs={{0,2},{1,3},{2,0},{3,1},{4,6},{5,7},{6,4},{7,5},{8,10},{9,11},{10,... | collective-permute-start | bytes 1572872 | tf_op jit(solution)/shard_map/ppermute | solution.py:277
  3.0 21.5 %collective-permute-start.3 = (f32[64,2048]{1,0:T(8,128)}, f32[64,2048]{1,0:T(8,128)S(1)}, u32[]{:S(2)}, u32[]{:S(2)}) collective-permute-start(f32[64,2048]{1,0:T(8,128)} %refs_0_), channel_id=1, source_target_pairs={{0,1},{1,0},{2,3},{3,2},{4,5},{5,4},{6,7},{7,6},{8,9},{9,8},{10,11... | collective-permute-start | bytes 1572872 | tf_op jit(solution)/shard_map/ppermute | solution.py:277
  3.0 2.2 %copy-start = (f32[2,16,256,128]{3,2,1,0:T(8,128)S(1)}, f32[2,16,256,128]{3,2,1,0:T(8,128)}, u32[]{:S(2)}) copy-start(f32[2,16,256,128]{3,2,1,0:T(8,128)} %source.3) | copy-start | bytes 12582916
  5.2 4.8 %copy-start.1 = (f32[2,16,256,128]{3,2,1,0:T(8,128)S(1)}, f32[2,16,256,128]{3,2,1,0:T(8,128)}, u32[]{:S(2)}) copy-start(f32[2,16,256,128]{3,2,1,0:T(8,128)} %source.3) | copy-start | bytes 12582916
  5.2 15.8 %collective-permute-start = (f32[2,256,128]{2,1,0:T(8,128)S(1)}, f32[2,256,128]{2,1,0:T(8,128)S(1)}, u32[]{:S(2)}, u32[]{:S(2)}) collective-permute-start(f32[2,256,128]{2,1,0:T(8,128)S(1)} %get-tuple-element.57), channel_id=1, source_target_pairs={{0,4},{4,8},{8,12},{12,16},{16,20},{20,24},{24,28},{28,0},{1,5},{5... | collective-permute-start | bytes 786440 | tf_op jit(solution)/shard_map/ppermute | solution.py:272
  6.7 14.2 %collective-permute-start.1 = (f32[2,256,128]{2,1,0:T(8,128)S(1)}, f32[2,256,128]{2,1,0:T(8,128)S(1)}, u32[]{:S(2)}, u32[]{:S(2)}) collective-permute-start(f32[2,256,128]{2,1,0:T(8,128)S(1)} %get-tuple-element.58), channel_id=1, source_target_pairs={{0,28},{4,0},{8,4},{12,8},{16,12},{20,16},{24,20},{28,24},{1,29},{... | collective-permute-start | bytes 786440 | tf_op jit(solution)/shard_map/ppermute | solution.py:272
  21.0 3.5 %collective-permute-start.4 = (f32[64,2048]{1,0:T(8,128)S(1)}, f32[64,2048]{1,0:T(8,128)S(1)}, u32[]{:S(2)}, u32[]{:S(2)}) collective-permute-start(f32[64,2048]{1,0:T(8,128)S(1)} %collective-permute-done.2.refs_1_), channel_id=1, source_target_pairs={{0,1},{1,0},{2,3},{3,2},{4,5},{5,4},{6,7},{7,6},{8,9},{9,8},{10,11... | collective-permute-start | bytes 1572872 | tf_op jit(solution)/shard_map/ppermute | solution.py:277
  21.1 3.4 %copy-start.2 = (f32[64,2048]{1,0:T(8,128)S(1)}, f32[64,2048]{1,0:T(8,128)}, u32[]{:S(2)}) copy-start(f32[64,2048]{1,0:T(8,128)} %refs_0_) | copy-start | bytes 1572868
  21.1 3.4 %copy-start.3 = (f32[256,256]{1,0:T(8,128)S(1)}, f32[256,256]{1,0:T(8,128)}, u32[]{:S(2)}) copy-start(f32[256,256]{1,0:T(8,128)} %cauchy.1) | copy-start | bytes 786436
  24.4 5.5 %copy-start.4 = (s32[2]{0:T(128)S(1)}, s32[2]{0:T(128)}, u32[]{:S(2)}) copy-start(s32[2]{0:T(128)} %start.9) | copy-start | bytes 28
  24.4 11.5 %collective-permute-start.6 = (f32[2,128,128]{2,1,0:T(8,128)S(1)}, f32[2,128,128]{2,1,0:T(8,128)S(1)}, u32[]{:S(2)}, u32[]{:S(2)}) collective-permute-start(f32[2,128,128]{2,1,0:T(8,128)S(1)} %get-tuple-element.85.refs_0_), channel_id=1, source_target_pairs={{0,4},{4,0},{8,12},{12,8},{16,20},{20,16},{24,28},{28,24},{1,5},{5... | collective-permute-start | bytes 393224 | tf_op jit(solution)/shard_map/ppermute | solution.py:277
  25.4 7.7 %collective-permute-start.5 = (f32[64,512]{1,0:T(8,128)S(1)}, f32[64,512]{1,0:T(8,128)S(1)}, u32[]{:S(2)}, u32[]{:S(2)}) collective-permute-start(f32[64,512]{1,0:T(8,128)S(1)} %slice.4), channel_id=1, source_target_pairs={{0,28},{4,0},{8,4},{12,8},{16,12},{20,16},{24,20},{28,24},{1,29},{... | collective-permute-start | bytes 393224 | tf_op jit(solution)/shard_map/ppermute | solution.py:272
  32.9 4.3 %collective-permute-start.7 = (f32[128,128]{1,0:T(8,128)S(1)}, f32[128,128]{1,0:T(8,128)S(1)}, u32[]{:S(2)}, u32[]{:S(2)}) collective-permute-start(f32[128,128]{1,0:T(8,128)S(1)} %get-tuple-element.76.refs_1_), channel_id=1, source_target_pairs={{0,4},{4,0},{8,12},{12,8},{16,20},{20,16},{24,28},{28,24},{1,5},{5... | collective-permute-start | bytes 196616 | tf_op jit(solution)/shard_map/ppermute | solution.py:277
  37.5 5.7 %collective-permute-start.9 = (f32[3,128,128]{2,1,0:T(8,128)S(1)}, f32[3,128,128]{2,1,0:T(8,128)S(1)}, u32[]{:S(2)}, u32[]{:S(2)}) collective-permute-start(f32[3,128,128]{2,1,0:T(8,128)S(1)} %get-tuple-element.89.refs_0_), channel_id=1, source_target_pairs={{0,8},{4,12},{8,0},{12,4},{16,24},{20,28},{24,16},{28,20},{1,9},{5... | collective-permute-start | bytes 589832 | tf_op jit(solution)/shard_map/ppermute | solution.py:277
  39.7 4.5 %collective-permute-start.8 = (f32[64,256]{1,0:T(8,128)S(1)}, f32[64,256]{1,0:T(8,128)S(1)}, u32[]{:S(2)}, u32[]{:S(2)}) collective-permute-start(f32[64,256]{1,0:T(8,128)S(1)} %get-tuple-element.88.mine), channel_id=1, source_target_pairs={{0,4},{4,0},{8,12},{12,8},{16,20},{20,16},{24,28},{28,24},{1,5},{5... | collective-permute-start | bytes 196616 | tf_op jit(solution)/shard_map/ppermute | solution.py:277
  44.5 4.3 %collective-permute-start.10 = (f32[64,256]{1,0:T(8,128)S(1)}, f32[64,256]{1,0:T(8,128)S(1)}, u32[]{:S(2)}, u32[]{:S(2)}) collective-permute-start(f32[64,256]{1,0:T(8,128)S(1)} %get-tuple-element.93.mine), channel_id=1, source_target_pairs={{0,8},{4,12},{8,0},{12,4},{16,24},{20,28},{24,16},{28,20},{1,9},{5... | collective-permute-start | bytes 196616 | tf_op jit(solution)/shard_map/ppermute | solution.py:277
  49.1 5.6 %collective-permute-start.11 = (f32[64,256]{1,0:T(8,128)S(1)}, f32[64,256]{1,0:T(8,128)S(1)}, u32[]{:S(2)}, u32[]{:S(2)}) collective-permute-start(f32[64,256]{1,0:T(8,128)S(1)} %get-tuple-element.96), channel_id=1, source_target_pairs={{0,16},{4,20},{8,24},{12,28},{16,0},{20,4},{24,8},{28,12},{1,17},{... | collective-permute-start | bytes 196616 | tf_op jit(solution)/shard_map/ppermute | solution.py:277

commit v4 on v3

--- a/solution.py
+++ b/solution.py
@@ -58,9 +58,8 @@
     return lax.broadcasted_iota(jnp.int32, shape, 0) == lax.broadcasted_iota(jnp.int32, shape, 1)
 
 
-def upper_inverses(grams):
+def upper_inverses(grams, base):
     spread = grams[0].shape[0]
-    base = spread // 4
     diagonal = eye(spread, spread)
     above = lax.broadcasted_iota(jnp.int32, (spread, spread), 0) < lax.broadcasted_iota(
         jnp.int32, (spread, spread), 1
@@ -143,7 +142,7 @@
         (g[:spread, :spread] + g[spread:, spread:]) + (g[:spread, spread:] + g[spread:, :spread])
         for g in grams
     ]
-    triangles = upper_inverses(grams)
+    triangles = upper_inverses(grams, 16 if len(values) > 8 else 32)
     unit = eye(double, double).astype(F32)
     scaled = []
     for pair, triangle in zip(pairs, triangles):
@@ -154,8 +153,9 @@
         product = dot(pair, right, NT)
         scaled.append(product[:, :spread] + product[:, spread:])
     for pair, value, kept in zip(pairs, scaled, active):
-        product = folded(dot(tall(value), pair, NT))
-        yield split(unit - jnp.where(kept, product, 0.0))
+        if kept is not True:
+            value = jnp.where(kept, value, 0.0)
+        yield split(unit - folded(dot(tall(value), pair, NT)))
 
 
 def runs_of(slots, extra=0):
@@ -176,7 +176,7 @@
     found = [refs[i * 7 : i * 7 + 7] for i in range(len(sweeps))]
     limit = last_slot - lax.axis_index("row") * count
     values = [source[sweep, b] for sweep in sweeps for b in range(count)]
-    active = [b <= limit for _ in sweeps for b in range(count)]
+    active = [b < count - 2 or b <= limit for _ in sweeps for b in range(count)]
     for i, (high, low) in enumerate(reflectors(values, active)):
         found[i // count][0][i % count] = high
         found[i // count][1][i % count] = low
@@ -199,12 +199,18 @@
                     maps[j] = both[:, spread:]
                 if b == count - 1:
                     beyond[...] = both[:, spread:]
-    for i, (_, _, _, _, maps, upto, _) in enumerate(found):
-        so_far = maps[0]
-        upto[0] = so_far
-        for j in range(1, len(runs)):
-            so_far = times(so_far, maps[j])
-            upto[j] = so_far
+    so_far = [[maps[j] for j in range(len(runs))] for _, _, _, _, maps, _, _ in found]
+    distance = 1
+    while distance < len(runs):
+        so_far = [
+            each[:distance]
+            + [times(each[j - distance], each[j]) for j in range(distance, len(runs))]
+            for each in so_far
+        ]
+        distance *= 2
+    for each, (_, _, _, _, _, upto, _) in zip(so_far, found):
+        for j, value in enumerate(each):
+            upto[j] = value
 
 
 def reflect(refl_v, sweeps):
@@ -295,24 +301,28 @@
 def chain(aligned, k_high, k_low, runs, maps, slots, y_local, joins):
     rows, spread = joins.shape[1:]
     carry = [jnp.zeros((rows, spread), F32)] * len(runs)
-    ends = [None] * len(runs)
-    for step in range(max(stop - at for at, stop in runs)):
+
+    def advance(j, slot):
+        fresh = aligned[:, slot * spread : (slot + 1) * spread]
+        (high, b), (low, _) = k_high[slot], k_low[slot]
+        both = apply(jnp.concatenate([carry[j], fresh], axis=1), high[b], low[b])
+        y_local[slot] = both[:, :spread]
+        carry[j] = both[:, spread:]
+
+    for step in range(max(min(stop, slots) - at for at, stop in runs)):
         for j, (at, stop) in enumerate(runs):
-            slot = at + step
-            if slot >= stop:
-                continue
-            fresh = aligned[:, slot * spread : (slot + 1) * spread]
-            (high, b), (low, _) = k_high[slot], k_low[slot]
-            both = apply(jnp.concatenate([carry[j], fresh], axis=1), high[b], low[b])
-            y_local[slot] = both[:, :spread]
-            carry[j] = both[:, spread:]
-            if slot + 1 == min(stop, slots):
-                ends[j] = carry[j]
+            if at + step < min(stop, slots):
+                advance(j, at + step)
+    beyond = list(range(slots, runs[-1][1]))
     joins[0] = jnp.zeros_like(carry[0])
-    so_far = ends[0]
+    so_far, ends = carry[0], list(carry)
     for j in range(1, len(runs)):
         joins[j] = so_far
         so_far = times(so_far, maps[j - 1]) + ends[j]
+        if beyond:
+            advance(len(runs) - 1, beyond.pop(0))
+    for slot in beyond:
+        advance(len(runs) - 1, slot)
     return so_far
 
 
@@ -391,9 +401,9 @@
 
 def response_kernel(
     count, start, q_high, q_low, q_right_high, q_right_low, reach, left_high, left_low, k_high,
-    k_low, maps, y_local, joins, gamma, line,
+    k_low, maps, totals, y_local, joins, through_device, line,
 ):
-    spread = gamma.shape[0]
+    spread = line.shape[0]
     entry = left_high[0, :spread, :spread].astype(F32) + left_low[0, :spread, :spread].astype(F32)
     q_highs = slot_table((None, 0), q_high, q_right_high)
     q_lows = slot_table((None, 0), q_low, q_right_low)
@@ -401,7 +411,8 @@
     aligned = rolled(line[...], start[1] - start[0] + spread)
     runs = runs_of(count, y_local.shape[0] - count)
     highs, lows = slot_table((left_high, 1), k_high), slot_table((left_low, 1), k_low)
-    gamma[...] = chain(aligned, highs, lows, runs, maps, count, y_local, joins)
+    through_device[1] = chain(aligned, highs, lows, runs, maps, count, y_local, joins)
+    through_device[0], through_device[2] = totals[0], totals[1]
 
 
 def home_kernel(
@@ -435,12 +446,8 @@
 
 def join_maps_kernel(level, *refs):
     upper = is_upper(level)
-    if level:
-        mine, other, inner, high, both, inside = refs
-        mine, other = [mine[i] for i in range(3)], [other[i] for i in range(3)]
-    else:
-        mine, gamma, other, gamma_other, high, both, inside = refs
-        mine, other = [mine[0], gamma[...], mine[1]], [other[0], gamma_other[...], other[1]]
+    mine, other, (high, both, inside) = refs[0], refs[1], refs[-3:]
+    inner = refs[2]
     spread = both.shape[1]
     low = [jnp.where(upper, other[i], mine[i]) for i in range(3)]
     for i in range(3):
@@ -530,7 +537,6 @@
         [k_pair] * 4 + [q_pair] * 2 + [shape((2, runs - 1) + square), shape((2,) + square)],
         2_000_000_000, [], [left, right, upto1, upto2, beyond],
     )
-    totals_other = swapped(totals, "row", 1)
     pieces[0] = after_all(pieces[0], totals)
     merged = whole_call(
         functools.partial(merge_kernel, owners), shape((rows, columns)),
@@ -539,58 +545,57 @@
     )
     after = shifted(merged[:, : 4 * spread], -1)
 
-    y_response, joins_response, gamma = whole_call(
+    y_response, joins_response, maps = whole_call(
         functools.partial(response_kernel, slots),
-        [shape((slots + 1,) + square), shape((runs,) + square), shape(square)],
+        [shape((slots + 1,) + square), shape((runs,) + square), shape((3,) + square)],
         4_000_000_000, starts,
-        [qh1, ql1, qrh, qrl, after_all(reach, merged), lh, ll, high2, low2, maps2],
+        [qh1, ql1, qrh, qrl, after_all(reach, merged), lh, ll, high2, low2, maps2,
+         totals],
         [pltpu.VMEM((spread, columns + 3 * spread), F32)],
     )
     line, state1 = whole_call(
         functools.partial(first_kernel, slots),
         [shape((rows, columns + 3 * spread)), shape((rows, spread))], 3_000_000_000, starts,
-        [after_all(merged, gamma), after, lh, ll, high1, low1, rh, rl, maps1, qh1, ql1, qrh, qrl],
+        [after_all(merged, maps), after, lh, ll, high1, low1, rh, rl, maps1, qh1, ql1, qrh, qrl],
         [pltpu.VMEM((slots + 3, rows, spread), F32), pltpu.VMEM((runs, rows, spread), F32)],
     )
-    groups = []
-    for level in range(levels - 1):
-        if level:
-            arrays = [maps, swapped(maps, "row", 1 << level), inside]
-        else:
-            arrays = [after_all(totals, state1), gamma, totals_other, swapped(gamma, "row", 1)]
-        high, maps, inside = whole_call(
-            functools.partial(join_maps_kernel, level), [shape((3,) + square)] * 3,
-            400_000_000, [], arrays,
-        )
-        groups.append((high, inside))
-
     states = shape((rows, 2 * spread))
     y2, joins2, state, head2 = whole_call(
         functools.partial(second_kernel, slots),
         [shape((slots + 1, rows, spread)), shape((runs, rows, spread)), states,
          shape((rows, spread))],
         3_000_000_000, starts,
-        [after_all(line, groups[0][0]), state1, lh, ll, high2, low2, maps2],
-    )
+        [line, state1, lh, ll, high2, low2, maps2],
+    )
+    groups = []
+    for level in range(levels - 1):
+        other = swapped(maps, "row", 1 << level)
+        arrays = [maps, other if level else after_all(other, state)]
+        arrays += [inside] if level else []
+        high, maps, inside = whole_call(
+            functools.partial(join_maps_kernel, level), [shape((3,) + square)] * 3,
+            400_000_000, [], arrays,
+        )
+        groups.append((high, inside))
+
+    base = whole_call(
+        functools.partial(base_kernel, slots), shape((rows, columns)), 2_000_000_000, starts,
+        [head2, joins2, y2, qh2, ql2], [pltpu.VMEM((rows, columns + spread), F32)],
+    )
+    enters = None
+    for level in range(levels - 1):
+        arrays = [state, swapped(state, "row", 1 << level), groups[level][0]]
+        arrays += [groups[level - 1][1], enters] if level else []
+        state, enters = whole_call(
+            functools.partial(join_states_kernel, level), [states] * 2, 100_000_000, [], arrays,
+        )
+    half = swapped(state, "row", 1 << (levels - 1))
     home = jax.ShapeDtypeStruct((2 * spread, columns), BF16)
     home_high, home_low = whole_call(
         functools.partial(home_kernel, slots), [home, home], 3_000_000_000, starts,
         [after_all(joins_response, state), y_response, qh2, ql2, reach, lh, ll],
         [pltpu.VMEM((spread, columns + spread), F32)],
     )
-    base = whole_call(
-        functools.partial(base_kernel, slots), shape((rows, columns)), 2_000_000_000, starts,
-        [head2, joins2, y2, qh2, ql2], [pltpu.VMEM((rows, columns + spread), F32)],
-    )
-    enters = None
-    for level in range(levels - 1):
-        other = after_all(swapped(state, "row", 1 << level), groups[-1][0])
-        arrays = [state, other, groups[level][0]]
-        arrays += [groups[level - 1][1], enters] if level else []
-        state, enters = whole_call(
-            functools.partial(join_states_kernel, level), [states] * 2, 100_000_000, [], arrays,
-        )
-    half = swapped(state, "row", 1 << (levels - 1))
     return whole_call(
         functools.partial(final_kernel, levels), shape((rows, columns)), 1_000_000_000, [],
         [half, groups[-1][1], enters, base, home_high, home_low],

time: 56.2 us -> 53.3 us (0.948)
  starting transfers between devices: 18.4 us -> 15.3 us
  waiting for transfers between devices: 6.05 us -> 6.8 us
  Pallas kernels: 29.3 us -> 28.6 us
    ppermute x3, starting transfers between devices: 9.27 us -> 7.62 us  [shifted(): lax.ppermute(array, 'row', [(i, (i + by) % devices) for i in range(device...]
    ppermute x9 -> x8, starting transfers between devices: 9.12 us -> 7.71 us  [swapped(): lax.ppermute(array, axis, [(i, i ^ distance) for i in range(devices)])]
    pallas_call x14, Pallas kernels: 29.3 us -> 28.6 us  [whole_call(): pl.pallas_call(kernel, out_shape=shapes, in_specs=[SMEM] * len(scalars) +...]
    ppermute x9 -> x8, waiting for transfers between devices: 5.9 us -> 6.25 us  [swapped(): lax.ppermute(array, axis, [(i, i ^ distance) for i in range(devices)])]
  transfers between devices with their start and end apart: 12 -> 11, of which waited for: 5 -> 5; matrix products, arithmetic and copies ran while one was open for 0% -> 0% of each run, Pallas kernels for 48% -> 49%
where the time goes in v4:
time: 53.3 us; the launch traced here: 53.2 us
  Pallas kernels  28.6 us (54%)
  starting transfers between devices  15.3 us (29%)
  waiting for transfers between devices  6.8 us (13%)
  local copies, waits for them, and re-layouts  2.23 us (4%)
    pallas_call x14, Pallas kernels, whole_call(): pl.pallas_call(kernel, out_shape=shapes, in_specs=[SMEM] * len(scalars) +...  28.6 us
    ppermute x8, starting transfers between devices, swapped(): lax.ppermute(array, axis, [(i, i ^ distance) for i in range(devices)])  7.71 us
    ppermute x3, starting transfers between devices, shifted(): lax.ppermute(array, 'row', [(i, (i + by) % devices) for i in range(device...  7.62 us
    ppermute x8, waiting for transfers between devices, swapped(): lax.ppermute(array, axis, [(i, i ^ distance) for i in range(devices)])  6.25 us
    unnamed x10, local copies, waits for them, and re-layouts  2.21 us
  transfers between devices with their start and end apart: 11, of which 5 were waited for; matrix products, arithmetic and copies ran while one was open for 0% of the time, Pallas kernels for 49%

profile of v4, /device:TPU:0, one launch (start us, length us, event | category | flops | bytes accessed | tf_op | source)
XLA Modules:
  0.0 53.2 jit_solution(8590979127460066769)
XLA Ops:
  0.0 0.5 collective-permute-start.3
  0.5 2.5 %collective-permute-start.2 = (f32[64,2048]{1,0:T(8,128)}, f32[64,2048]{1,0:T(8,128)S(1)}, u32[]{:S(2)}, u32[]{:S(2)}) collective-permute-start(f32[64,2048]{1,0:T(8,128)} %refs_0_), channel_id=1, source_target_pairs={{0,2},{1,3},{2,0},{3,1},{4,6},{5,7},{6,4},{7,5},{8,10},{9,11},{10,... | collective-permute-start | bytes 1572872 | tf_op jit(solution)/shard_map/ppermute | solution.py:283
  3.0 0.0 copy-start
  3.0 2.2 %copy-done = f32[2,16,256,128]{3,2,1,0:T(8,128)S(1)} copy-done((f32[2,16,256,128]{3,2,1,0:T(8,128)S(1)}, f32[2,16,256,128]{3,2,1,0:T(8,128)}, u32[]{:S(2)}) %copy-start) | copy-done | bytes 4194328
  5.2 0.0 copy-start.1
  5.2 1.5 %collective-permute-start = (f32[2,256,128]{2,1,0:T(8,128)S(1)}, f32[2,256,128]{2,1,0:T(8,128)S(1)}, u32[]{:S(2)}, u32[]{:S(2)}) collective-permute-start(f32[2,256,128]{2,1,0:T(8,128)S(1)} %get-tuple-element.54), channel_id=1, source_target_pairs={{0,4},{4,8},{8,12},{12,16},{16,20},{20,24},{24,28},{28,0},{1,5},{5... | collective-permute-start | bytes 786440 | tf_op jit(solution)/shard_map/ppermute | solution.py:278
  6.7 3.2 %collective-permute-start.1 = (f32[2,256,128]{2,1,0:T(8,128)S(1)}, f32[2,256,128]{2,1,0:T(8,128)S(1)}, u32[]{:S(2)}, u32[]{:S(2)}) collective-permute-start(f32[2,256,128]{2,1,0:T(8,128)S(1)} %get-tuple-element.55), channel_id=1, source_target_pairs={{0,28},{4,0},{8,4},{12,8},{16,12},{20,16},{24,20},{28,24},{1,29},{... | collective-permute-start | bytes 786440 | tf_op jit(solution)/shard_map/ppermute | solution.py:278
  10.0 0.0 copy-done.1
  10.0 11.0 %shard_map.47 = (bf16[16,256,256]{2,1,0:T(8,128)(2,1)S(1)}, bf16[16,256,256]{2,1,0:T(8,128)(2,1)S(1)}, bf16[16,128,128]{2,1,0:T(8,128)(2,1)S(1)}, bf16[16,128,12...) custom-call(f32[2,16,256,128]{3,2,1,0:T(8,128)S(1)} %copy-done.1), custom_call_target="tpu_custom_call" | custom-call | flops 9600000000 | bytes 4000000 | tf_op jit(solution)/shard_map/pallas_call | solution.py:493
  21.0 0.0 collective-permute-done.left
  21.0 0.0 collective-permute-done.1.right
  21.0 0.0 collective-permute-done.2.refs_1_
  21.0 0.1 collective-permute-start.4
  21.1 0.0 copy-start.2
  21.1 0.0 copy-start.3
  21.1 3.3 %shard_map.48 = (bf16[2,256,256]{2,1,0:T(8,128)(2,1)S(1)}, bf16[2,256,256]{2,1,0:T(8,128)(2,1)S(1)}, bf16[2,256,256]{2,1,0:T(8,128)(2,1)S(1)}, bf16[2,256,256]{2...) custom-call(f32[2,256,128]{2,1,0:T(8,128)S(1)} %collective-permute-d, ...), custom_call_target="tpu_custom_call" | custom-call | flops 2000000000 | bytes 4000000 | tf_op jit(solution)/shard_map/pallas_call | solution.py:493
  24.4 0.0 copy-start.4
  24.4 0.0 collective-permute-done.3.refs_2_
  24.4 0.0 collective-permute-done.4.refs_3_
  24.4 0.0 copy-done.2
  24.4 0.0 copy-done.3
  24.4 0.9 %shard_map.49.home = f32[64,2048]{1,0:T(8,128)S(1)} custom-call(f32[256,256]{1,0:T(8,128)S(1)} %copy-done.3, f32[64,2048]{1,0:T(8,128)S(1)} %copy-done.2, f32[64,2048]{1,0:T(8,128)S(1)} %collective-permute-done.2.refs_1_, f32[64,2048]{1,0:T(8,128)S(1)} %collective-permute-done.3.refs_2_, f32[64,2048]{1,0:T(8,128)S(1)} %collective-permute-done.4.refs_3_), custom_call_target="tpu_custom_call" | custom-call | flops 1000000000 | bytes 4000000 | tf_op jit(solution)/shard_map/pallas_call | solution.py:493
  25.3 2.8 %collective-permute-start.5 = (f32[64,512]{1,0:T(8,128)S(1)}, f32[64,512]{1,0:T(8,128)S(1)}, u32[]{:S(2)}, u32[]{:S(2)}) collective-permute-start(f32[64,512]{1,0:T(8,128)S(1)} %slice.4), channel_id=1, source_target_pairs={{0,28},{4,0},{8,4},{12,8},{16,12},{20,16},{24,20},{28,24},{1,29},{... | collective-permute-start | bytes 393224 | tf_op jit(solution)/shard_map/ppermute | solution.py:278
  28.2 0.0 copy-done.4
  28.2 2.8 %shard_map.50 = (f32[17,128,128]{2,1,0:T(8,128)S(1)}, f32[5,128,128]{2,1,0:T(8,128)S(1)}, f32[3,128,128]{2,1,0:T(8,128)S(1)}) custom-call(s32[2]{0:T(128)S(1)} %copy-done.4, bf16[16,128,128]{2,1,0:T(8,128)(2,1)S(1)} %get-tuple-element.62.q_high, bf16[16,128,128]{2,1,0:T(8,128)(2,1)S(1)} %get-tuple-element.63.q_low, ...), custom_call_target="tpu_custom_call" | custom-call | flops 4000000000 | bytes 4000000 | tf_op jit(solution)/shard_map/pallas_call | solution.py:493
  31.0 0.1 collective-permute-start.7
  31.0 0.5 %collective-permute-done.5.after = f32[64,512]{1,0:T(8,128)S(1)} collective-permute-done((f32[64,512]{1,0:T(8,128)S(1)}, f32[64,512]{1,0:T(8,128)S(1)}, u32[]{:S(2)}, u32[]{:S(2)}) %collective-permute-start.5) | collective-permute-done | bytes 131104 | tf_op jit(solution)/shard_map/ppermute | solution.py:278
  31.6 2.4 %shard_map.51 = (f32[64,2432]{1,0:T(8,128)S(1)}, f32[64,128]{1,0:T(8,128)S(1)}) custom-call(s32[2]{0:T(128)S(1)} %copy-done.4, f32[64,2048]{1,0:T(8,128)S(1)} %shard_map.49.home, f32[64,512]{1,0:T(8,128)S(1)} %collective-permute-done.5.after, bf16[2,256,256]{2,1,0:T(8,128)(2,1)S(1)} %get-tuple-element.68.left_high, ...), custom_call_target="tpu_custom_call" | custom-call | flops 3000000000 | bytes 4000000 | tf_op jit(solution)/shard_map/pallas_call | solution.py:493
  33.9 2.0 %shard_map.52 = (f32[17,64,128]{2,1,0:T(8,128)S(1)}, f32[5,64,128]{2,1,0:T(8,128)S(1)}, f32[64,256]{1,0:T(8,128)S(1)}, f32[64,128]{1,0:T(8,128)S(1)}) custom-call(s32[2]{0:T(128)S(1)} %copy-done.4, f32[64,2432]{1,0:T(8,128)S(1)} %get-tuple-element.80.line, f32[64,128]{1,0:T(8,128)S(1)} %get-tuple-element.81.state_in, ...), custom_call_target="tpu_custom_call" | custom-call | flops 3000000000 | bytes 4000000 | tf_op jit(solution)/shard_map/pallas_call | solution.py:493
  36.0 1.5 %collective-permute-start.6 = (f32[64,256]{1,0:T(8,128)S(1)}, f32[64,256]{1,0:T(8,128)S(1)}, u32[]{:S(2)}, u32[]{:S(2)}) collective-permute-start(f32[64,256]{1,0:T(8,128)S(1)} %get-tuple-element.82.mine), channel_id=1, source_target_pairs={{0,4},{4,0},{8,12},{12,8},{16,20},{20,16},{24,28},{28,24},{1,5},{5... | collective-permute-start | bytes 196616 | tf_op jit(solution)/shard_map/ppermute | solution.py:283
  37.4 0.6 %collective-permute-done.7.refs_1_ = f32[3,128,128]{2,1,0:T(8,128)S(1)} collective-permute-done((f32[3,128,128]{2,1,0:T(8,128)S(1)}, f32[3,128,128]{2,1,0:T(8,128)S(1)}, u32[]{:S(2)}, u32[]{:S(2)}) %collective-permute-start.7) | collective-permute-done | bytes 196640 | tf_op jit(solution)/shard_map/ppermute | solution.py:283
  38.0 0.3 shard_map.53
  38.3 0.1 collective-permute-start.9
  38.4 1.9 %collective-permute-done.6.other = f32[64,256]{1,0:T(8,128)S(1)} collective-permute-done((f32[64,256]{1,0:T(8,128)S(1)}, f32[64,256]{1,0:T(8,128)S(1)}, u32[]{:S(2)}, u32[]{:S(2)}) %collective-permute-start.6) | collective-permute-done | bytes 65568 | tf_op jit(solution)/shard_map/ppermute | solution.py:283
  40.3 0.2 shard_map.54
  40.5 0.4 collective-permute-start.8
  40.9 1.1 %shard_map.57.base = f32[64,2048]{1,0:T(8,128)S(1)} custom-call(s32[2]{0:T(128)S(1)} %copy-done.4, f32[64,128]{1,0:T(8,128)S(1)} %get-tuple-element.93.head, f32[5,64,128]{2,1,0:T(8,128)S(1)} %get-tuple-element.94.joins, f32[17,64,128]{2,1,0:T(8,128)S(1)} %get-tuple-element.95.y_local, bf16[16,128,128]{2,1,0:T(8,128)(2,1)S(1)} %get-tuple-element.96.q_high, ...), custom_call_target="tpu_custom_call" | custom-call | flops 2000000000 | bytes 4000000 | tf_op jit(solution)/shard_map/pallas_call | solution.py:493
  42.1 3.2 %collective-permute-done.9.refs_1_ = f32[3,128,128]{2,1,0:T(8,128)S(1)} collective-permute-done((f32[3,128,128]{2,1,0:T(8,128)S(1)}, f32[3,128,128]{2,1,0:T(8,128)S(1)}, u32[]{:S(2)}, u32[]{:S(2)}) %collective-permute-start.9) | collective-permute-done | bytes 196640 | tf_op jit(solution)/shard_map/ppermute | solution.py:283
  45.3 1.0 %shard_map.55 = (f32[3,128,128]{2,1,0:T(8,128)S(1)}, f32[3,128,128]{2,1,0:T(8,128)}, f32[3,128,128]{2,1,0:T(8,128)S(1)}) custom-call(f32[3,128,128]{2,1,0:T(8,128)S(1)} %get-tuple-element.86.refs_0_, f32[3,128,128]{2,1,0:T(8,128)S(1)} %collective-permute-done.9.refs_1_, f32[3,128,128]{2,1,0:T(8,128)S(1)} %get-tuple-element.87.refs_2_.refs_0_), custom_call_target="tpu_custom_call" | custom-call | flops 400000000 | bytes 4000000 | tf_op jit(solution)/shard_map/pallas_call | solution.py:493
  46.2 0.0 collective-permute-done.8.other
  46.3 0.3 shard_map.56
  46.5 2.7 %collective-permute-start.10 = (f32[64,256]{1,0:T(8,128)S(1)}, f32[64,256]{1,0:T(8,128)S(1)}, u32[]{:S(2)}, u32[]{:S(2)}) collective-permute-start(f32[64,256]{1,0:T(8,128)S(1)} %get-tuple-element.90), channel_id=1, source_target_pairs={{0,16},{4,20},{8,24},{12,28},{16,0},{20,4},{24,8},{28,12},{1,17},{... | collective-permute-start | bytes 196616 | tf_op jit(solution)/shard_map/ppermute | solution.py:283
  49.2 2.0 %shard_map.58 = (bf16[256,2048]{1,0:T(8,128)(2,1)S(1)}, bf16[256,2048]{1,0:T(8,128)(2,1)S(1)}) custom-call(s32[2]{0:T(128)S(1)} %copy-done.4, f32[5,128,128]{2,1,0:T(8,128)S(1)} %get-tuple-element.99.joins, f32[17,128,128]{2,1,0:T(8,128)S(1)} %get-tuple-element.100.y_local, bf16[16,128,128]{2,1,0:T(8,128)(2,1)S(1)} %get-tuple-element.96.q_high, ...), custom_call_target="tpu_custom_call" | custom-call | flops 3000000000 | bytes 4000000 | tf_op jit(solution)/shard_map/pallas_call | solution.py:493
  51.2 0.6 %collective-permute-done.10.half = f32[64,256]{1,0:T(8,128)S(1)} collective-permute-done((f32[64,256]{1,0:T(8,128)S(1)}, f32[64,256]{1,0:T(8,128)S(1)}, u32[]{:S(2)}, u32[]{:S(2)}) %collective-permute-start.10) | collective-permute-done | bytes 65568 | tf_op jit(solution)/shard_map/ppermute | solution.py:283
  51.7 1.4 %shard_map.59 = f32[64,2048]{1,0:T(8,128)} custom-call(f32[64,256]{1,0:T(8,128)S(1)} %collective-permute-done.10.half, f32[3,128,128]{2,1,0:T(8,128)S(1)} %get-tuple-element.91.inner, f32[64,256]{1,0:T(8,128)S(1)} %get-tuple-element.92.before, f32[64,2048]{1,0:T(8,128)S(1)} %shard_map.57.base, bf16[256,2048]{1,0:T(8,128)(2,1)S(1)} %get-tuple-element.101.high, ...), custom_call_target="tpu_custom_call" | custom-call | flops 1000000000 | bytes 4000000 | tf_op jit(solution)/shard_map/pallas_call | solution.py:493
  (2 shorter events, 0.1 us)
Async XLA Ops:
  0.0 24.4 %collective-permute-start.3 = (f32[64,2048]{1,0:T(8,128)}, f32[64,2048]{1,0:T(8,128)S(1)}, u32[]{:S(2)}, u32[]{:S(2)}) collective-permute-start(f32[64,2048]{1,0:T(8,128)} %refs_0_), channel_id=1, source_target_pairs={{0,1},{1,0},{2,3},{3,2},{4,5},{5,4},{6,7},{7,6},{8,9},{9,8},{10,11... | collective-permute-start | bytes 1572872 | tf_op jit(solution)/shard_map/ppermute | solution.py:283
  0.5 20.5 %collective-permute-start.2 = (f32[64,2048]{1,0:T(8,128)}, f32[64,2048]{1,0:T(8,128)S(1)}, u32[]{:S(2)}, u32[]{:S(2)}) collective-permute-start(f32[64,2048]{1,0:T(8,128)} %refs_0_), channel_id=1, source_target_pairs={{0,2},{1,3},{2,0},{3,1},{4,6},{5,7},{6,4},{7,5},{8,10},{9,11},{10,... | collective-permute-start | bytes 1572872 | tf_op jit(solution)/shard_map/ppermute | solution.py:283
  3.0 2.2 %copy-start = (f32[2,16,256,128]{3,2,1,0:T(8,128)S(1)}, f32[2,16,256,128]{3,2,1,0:T(8,128)}, u32[]{:S(2)}) copy-start(f32[2,16,256,128]{3,2,1,0:T(8,128)} %source.3) | copy-start | bytes 12582916
  5.2 4.8 %copy-start.1 = (f32[2,16,256,128]{3,2,1,0:T(8,128)S(1)}, f32[2,16,256,128]{3,2,1,0:T(8,128)}, u32[]{:S(2)}) copy-start(f32[2,16,256,128]{3,2,1,0:T(8,128)} %source.3) | copy-start | bytes 12582916
  5.2 15.8 %collective-permute-start = (f32[2,256,128]{2,1,0:T(8,128)S(1)}, f32[2,256,128]{2,1,0:T(8,128)S(1)}, u32[]{:S(2)}, u32[]{:S(2)}) collective-permute-start(f32[2,256,128]{2,1,0:T(8,128)S(1)} %get-tuple-element.54), channel_id=1, source_target_pairs={{0,4},{4,8},{8,12},{12,16},{16,20},{20,24},{24,28},{28,0},{1,5},{5... | collective-permute-start | bytes 786440 | tf_op jit(solution)/shard_map/ppermute | solution.py:278
  6.7 14.2 %collective-permute-start.1 = (f32[2,256,128]{2,1,0:T(8,128)S(1)}, f32[2,256,128]{2,1,0:T(8,128)S(1)}, u32[]{:S(2)}, u32[]{:S(2)}) collective-permute-start(f32[2,256,128]{2,1,0:T(8,128)S(1)} %get-tuple-element.55), channel_id=1, source_target_pairs={{0,28},{4,0},{8,4},{12,8},{16,12},{20,16},{24,20},{28,24},{1,29},{... | collective-permute-start | bytes 786440 | tf_op jit(solution)/shard_map/ppermute | solution.py:278
  21.0 3.4 %collective-permute-start.4 = (f32[64,2048]{1,0:T(8,128)S(1)}, f32[64,2048]{1,0:T(8,128)S(1)}, u32[]{:S(2)}, u32[]{:S(2)}) collective-permute-start(f32[64,2048]{1,0:T(8,128)S(1)} %collective-permute-done.2.refs_1_), channel_id=1, source_target_pairs={{0,1},{1,0},{2,3},{3,2},{4,5},{5,4},{6,7},{7,6},{8,9},{9,8},{10,11... | collective-permute-start | bytes 1572872 | tf_op jit(solution)/shard_map/ppermute | solution.py:283
  21.1 3.3 %copy-start.2 = (f32[64,2048]{1,0:T(8,128)S(1)}, f32[64,2048]{1,0:T(8,128)}, u32[]{:S(2)}) copy-start(f32[64,2048]{1,0:T(8,128)} %refs_0_) | copy-start | bytes 1572868
  21.1 3.3 %copy-start.3 = (f32[256,256]{1,0:T(8,128)S(1)}, f32[256,256]{1,0:T(8,128)}, u32[]{:S(2)}) copy-start(f32[256,256]{1,0:T(8,128)} %cauchy.1) | copy-start | bytes 786436
  24.4 3.8 %copy-start.4 = (s32[2]{0:T(128)S(1)}, s32[2]{0:T(128)}, u32[]{:S(2)}) copy-start(s32[2]{0:T(128)} %start.9) | copy-start | bytes 28
  25.3 6.2 %collective-permute-start.5 = (f32[64,512]{1,0:T(8,128)S(1)}, f32[64,512]{1,0:T(8,128)S(1)}, u32[]{:S(2)}, u32[]{:S(2)}) collective-permute-start(f32[64,512]{1,0:T(8,128)S(1)} %slice.4), channel_id=1, source_target_pairs={{0,28},{4,0},{8,4},{12,8},{16,12},{20,16},{24,20},{28,24},{1,29},{... | collective-permute-start | bytes 393224 | tf_op jit(solution)/shard_map/ppermute | solution.py:278
  31.0 7.1 %collective-permute-start.7 = (f32[3,128,128]{2,1,0:T(8,128)S(1)}, f32[3,128,128]{2,1,0:T(8,128)S(1)}, u32[]{:S(2)}, u32[]{:S(2)}) collective-permute-start(f32[3,128,128]{2,1,0:T(8,128)S(1)} %get-tuple-element.73.refs_0_), channel_id=1, source_target_pairs={{0,4},{4,0},{8,12},{12,8},{16,20},{20,16},{24,28},{28,24},{1,5},{5... | collective-permute-start | bytes 589832 | tf_op jit(solution)/shard_map/ppermute | solution.py:283
  36.0 4.3 %collective-permute-start.6 = (f32[64,256]{1,0:T(8,128)S(1)}, f32[64,256]{1,0:T(8,128)S(1)}, u32[]{:S(2)}, u32[]{:S(2)}) collective-permute-start(f32[64,256]{1,0:T(8,128)S(1)} %get-tuple-element.82.mine), channel_id=1, source_target_pairs={{0,4},{4,0},{8,12},{12,8},{16,20},{20,16},{24,28},{28,24},{1,5},{5... | collective-permute-start | bytes 196616 | tf_op jit(solution)/shard_map/ppermute | solution.py:283
  38.3 6.9 %collective-permute-start.9 = (f32[3,128,128]{2,1,0:T(8,128)S(1)}, f32[3,128,128]{2,1,0:T(8,128)S(1)}, u32[]{:S(2)}, u32[]{:S(2)}) collective-permute-start(f32[3,128,128]{2,1,0:T(8,128)S(1)} %get-tuple-element.86.refs_0_), channel_id=1, source_target_pairs={{0,8},{4,12},{8,0},{12,4},{16,24},{20,28},{24,16},{28,20},{1,9},{5... | collective-permute-start | bytes 589832 | tf_op jit(solution)/shard_map/ppermute | solution.py:283
  40.5 5.7 %collective-permute-start.8 = (f32[64,256]{1,0:T(8,128)S(1)}, f32[64,256]{1,0:T(8,128)S(1)}, u32[]{:S(2)}, u32[]{:S(2)}) collective-permute-start(f32[64,256]{1,0:T(8,128)S(1)} %get-tuple-element.85.mine), channel_id=1, source_target_pairs={{0,8},{4,12},{8,0},{12,4},{16,24},{20,28},{24,16},{28,20},{1,9},{5... | collective-permute-start | bytes 196616 | tf_op jit(solution)/shard_map/ppermute | solution.py:283
  46.5 5.2 %collective-permute-start.10 = (f32[64,256]{1,0:T(8,128)S(1)}, f32[64,256]{1,0:T(8,128)S(1)}, u32[]{:S(2)}, u32[]{:S(2)}) collective-permute-start(f32[64,256]{1,0:T(8,128)S(1)} %get-tuple-element.90), channel_id=1, source_target_pairs={{0,16},{4,20},{8,24},{12,28},{16,0},{20,4},{24,8},{28,12},{1,17},{... | collective-permute-start | bytes 196616 | tf_op jit(solution)/shard_map/ppermute | solution.py:283

commit v5 on v4

--- a/solution.py
+++ b/solution.py
@@ -166,14 +166,14 @@
     return runs
 
 
-def edges_kernel(source, last, first):
+def edges_kernel(source, kept, last, first):
     last[...] = source[:, source.shape[1] - 1]
     first[...] = source[0, :2]
 
 
 def reflect_kernel(sweeps, last_slot, source, *refs):
     count, double, spread = source.shape[1:]
-    found = [refs[i * 7 : i * 7 + 7] for i in range(len(sweeps))]
+    found = [refs[i * 8 : i * 8 + 8] for i in range(len(sweeps))]
     limit = last_slot - lax.axis_index("row") * count
     values = [source[sweep, b] for sweep in sweeps for b in range(count)]
     active = [b < count - 2 or b <= limit for _ in sweeps for b in range(count)]
@@ -182,11 +182,12 @@
         found[i // count][1][i % count] = low
     runs = runs_of(count, 1)[1:]
     state = [[None] * len(runs) for _ in found]
+    maps = [[None] * len(runs) for _ in found]
     for step in range(max(stop - at for at, stop in runs)):
         for j, (at, stop) in enumerate(runs):
             if at + step >= stop:
                 continue
-            for i, (k_high, k_low, q_high, q_low, maps, upto, beyond) in enumerate(found):
+            for i, (k_high, k_low, q_high, q_low, _, _, _, beyond) in enumerate(found):
                 b = at + step - 1
                 high, low = k_high[b, :spread, :], k_low[b, :spread, :]
                 if step == 0:
@@ -196,21 +197,23 @@
                 state[i][j] = both[:, spread:]
                 q_high[b], q_low[b] = split(both[:, :spread])
                 if b == count - 2 or (at + step + 1 == stop and b < count - 1):
-                    maps[j] = both[:, spread:]
+                    maps[i][j] = both[:, spread:]
                 if b == count - 1:
                     beyond[...] = both[:, spread:]
-    so_far = [[maps[j] for j in range(len(runs))] for _, _, _, _, maps, _, _ in found]
-    distance = 1
-    while distance < len(runs):
-        so_far = [
-            each[:distance]
-            + [times(each[j - distance], each[j]) for j in range(distance, len(runs))]
-            for each in so_far
-        ]
-        distance *= 2
-    for each, (_, _, _, _, _, upto, _) in zip(so_far, found):
-        for j, value in enumerate(each):
-            upto[j] = value
+    for each, (_, _, _, _, join_high, join_low, upto, _) in zip(maps, found):
+        spans = {(j, j + 1): value for j, value in enumerate(each)}
+        length = 2
+        while length <= len(runs):
+            half = 1 << ((length - 1).bit_length() - 1)
+            for j in range(len(runs) - length + 1):
+                spans[j, j + length] = times(spans[j, j + half], spans[j + half, j + length])
+            length += 1
+        for j in range(len(runs)):
+            upto[j] = spans[0, j + 1]
+            for stop in range(len(runs)):
+                block = spans.get((j, stop + 1), jnp.zeros((spread, spread), F32))
+                rows, columns = (slice(i * spread, (i + 1) * spread) for i in (j, stop))
+                join_high[rows, columns], join_low[rows, columns] = split(block)
 
 
 def reflect(refl_v, sweeps):
@@ -219,12 +222,13 @@
     shape = jax.ShapeDtypeStruct
     shapes = [shape((slots, double, double), BF16)] * 2
     shapes += [shape((slots, spread, spread), BF16)] * 2
-    shapes += [shape((runs, spread, spread), F32)] * 2 + [shape((spread, spread), F32)]
+    shapes += [shape((runs * spread, runs * spread), BF16)] * 2
+    shapes += [shape((runs, spread, spread), F32), shape((spread, spread), F32)]
     results = whole_call(
         functools.partial(reflect_kernel, sweeps, lax.axis_size("row") * slots - 3),
         shapes * len(sweeps), len(sweeps) * slots * 300_000_000, [], [refl_v], vmem=24,
     )
-    return [results[i * 7 : i * 7 + 7] for i in range(len(sweeps))]
+    return [results[i * 8 : i * 8 + 8] for i in range(len(sweeps))]
 
 
 def edge_kernel(
@@ -298,7 +302,7 @@
     return table + [(right, b) for b in range(extra)]
 
 
-def chain(aligned, k_high, k_low, runs, maps, slots, y_local, joins):
+def chain(aligned, k_high, k_low, runs, join_high, join_low, slots, y_local, joins):
     rows, spread = joins.shape[1:]
     carry = [jnp.zeros((rows, spread), F32)] * len(runs)
 
@@ -314,16 +318,14 @@
             if at + step < min(stop, slots):
                 advance(j, at + step)
     beyond = list(range(slots, runs[-1][1]))
-    joins[0] = jnp.zeros_like(carry[0])
-    so_far, ends = carry[0], list(carry)
-    for j in range(1, len(runs)):
-        joins[j] = so_far
-        so_far = times(so_far, maps[j - 1]) + ends[j]
-        if beyond:
-            advance(len(runs) - 1, beyond.pop(0))
+    added = apply(jnp.concatenate(carry[:-1], axis=1), join_high[...], join_low[...])
+    joins[0], joins[1] = jnp.zeros_like(carry[0]), carry[0]
+    entered = [added[:, j * spread : (j + 1) * spread] + carry[j + 1] for j in range(len(runs) - 1)]
+    for j, value in enumerate(entered[:-1]):
+        joins[j + 2] = value
     for slot in beyond:
         advance(len(runs) - 1, slot)
-    return so_far
+    return entered[-1]
 
 
 def terms(table, runs):
@@ -351,8 +353,8 @@
 
 
 def first_kernel(
-    count, start, home, after, left_high, left_low, k_high, k_low, right_high, right_low, maps,
-    q_high, q_low, q_right_high, q_right_low, line, state, y_local, joins,
+    count, start, home, after, left_high, left_low, k_high, k_low, right_high, right_low, join_high,
+    join_low, q_high, q_low, q_right_high, q_right_low, line, state, y_local, joins,
 ):
     spread = state.shape[1]
     offset = start[0]
@@ -360,7 +362,7 @@
     runs = runs_of(count, y_local.shape[0] - count)
     highs = slot_table((left_high, 0), k_high, right_high)
     lows = slot_table((left_low, 0), k_low, right_low)
-    state[...] = chain(aligned, highs, lows, runs, maps, count, y_local, joins)
+    state[...] = chain(aligned, highs, lows, runs, join_high, join_low, count, y_local, joins)
     q_highs = slot_table((None, 0), q_high, q_right_high)
     q_lows = slot_table((None, 0), q_low, q_right_low)
     settled(runs, joins, q_highs, q_lows, y_local, line)
@@ -371,15 +373,17 @@
 
 
 def second_kernel(
-    count, start, line, state_in, left_high, left_low, k_high, k_low, maps, y_local, joins, state,
-    head,
+    count, start, line, state_in, left_high, left_low, k_high, k_low, join_high, join_low, y_local,
+    joins, state, head,
 ):
     spread = head.shape[1]
     ahead = start[1] - start[0]
     aligned = rolled(line[...], ahead + spread)
     runs = runs_of(count, y_local.shape[0] - count)
     highs, lows = slot_table((left_high, 1), k_high), slot_table((left_low, 1), k_low)
-    state[:, spread:] = chain(aligned, highs, lows, runs, maps, count, y_local, joins)
+    state[:, spread:] = chain(
+        aligned, highs, lows, runs, join_high, join_low, count, y_local, joins
+    )
     state[:, :spread] = state_in[...]
     head[...] = pltpu.roll(
         line[:, : 2 * spread], lax.rem(4 * spread - ahead, 2 * spread), 1
@@ -401,7 +405,7 @@
 
 def response_kernel(
     count, start, q_high, q_low, q_right_high, q_right_low, reach, left_high, left_low, k_high,
-    k_low, maps, totals, y_local, joins, through_device, line,
+    k_low, join_high, join_low, totals, y_local, joins, through_device, line,
 ):
     spread = line.shape[0]
     entry = left_high[0, :spread, :spread].astype(F32) + left_low[0, :spread, :spread].astype(F32)
@@ -411,25 +415,30 @@
     aligned = rolled(line[...], start[1] - start[0] + spread)
     runs = runs_of(count, y_local.shape[0] - count)
     highs, lows = slot_table((left_high, 1), k_high), slot_table((left_low, 1), k_low)
-    through_device[1] = chain(aligned, highs, lows, runs, maps, count, y_local, joins)
+    through_device[1] = chain(
+        aligned, highs, lows, runs, join_high, join_low, count, y_local, joins
+    )
     through_device[0], through_device[2] = totals[0], totals[1]
 
 
-def home_kernel(
-    count, start, joins, y_local, q_high, q_low, reach, left_high, left_low, high, low, line
-):
-    spread, columns = line.shape[0], high.shape[1]
+def moved_home(start, line, high, low):
+    spread, columns = high.shape
+    high[...], low[...] = split(rolled(line[...], spread - start[1])[:, :columns])
+
+
+def home_first_kernel(count, start, joins, y_local, q_high, q_low, high, low, line):
     runs = runs_of(count, y_local.shape[0] - count)
     q_highs, q_lows = slot_table((None, 0), q_high), slot_table((None, 0), q_low)
-    for sweep in range(2):
-        at = slice(sweep * spread, (sweep + 1) * spread)
-        if sweep == 0:
-            settled(runs, joins, q_highs, q_lows, y_local, line)
-        else:
-            entry = left_high[1, :spread, :spread].astype(F32)
-            entry = entry + left_low[1, :spread, :spread].astype(F32)
-            reached(runs, entry, reach.at[1], q_highs, q_lows, line)
-        high[at], low[at] = split(rolled(line[...], spread - start[1])[:, :columns])
+    settled(runs, joins, q_highs, q_lows, y_local, line)
+    moved_home(start, line, high, low)
+
+
+def home_second_kernel(count, start, reach, q_high, q_low, left_high, left_low, high, low, line):
+    spread = line.shape[0]
+    entry = left_high[1, :spread, :spread].astype(F32) + left_low[1, :spread, :spread].astype(F32)
+    q_highs, q_lows = slot_table((None, 0), q_high), slot_table((None, 0), q_low)
+    reached(runs_of(count, 1), entry, reach.at[1], q_highs, q_lows, line)
+    moved_home(start, line, high, low)
 
 
 def is_upper(level):
@@ -446,9 +455,10 @@
 
 def join_maps_kernel(level, *refs):
     upper = is_upper(level)
-    mine, other, (high, both, inside) = refs[0], refs[1], refs[-3:]
-    inner = refs[2]
-    spread = both.shape[1]
+    mine, other, refs = refs[0], refs[1], list(refs[2:])
+    inner = refs.pop(0) if level else None
+    high, inside, *both = refs
+    spread = high.shape[1]
     low = [jnp.where(upper, other[i], mine[i]) for i in range(3)]
     for i in range(3):
         high[i] = jnp.where(upper, mine[i], other[i])
@@ -460,8 +470,9 @@
             times(low[2], later[2]),
         ]
 
-    for i, value in enumerate(joined(high)):
-        both[i] = value
+    if both:
+        for i, value in enumerate(joined(high)):
+            both[0][i] = value
     if level:
         for i, value in enumerate(joined(inner)):
             inside[i] = jnp.where(upper, value, inner[i])
@@ -483,19 +494,24 @@
         refs[1][...] = jnp.where(upper, low, 0.0)
 
 
-def final_kernel(levels, half, inner, before, base, high, low, out):
+def final_kernel(
+    levels, half, inner, before, base, high_first, high_second, low_first, low_second, out
+):
     enters = jnp.where(is_upper(levels - 1), half[...], 0.0)
     incoming = before[...] + through(enters, inner)
-    out[...] = base[...] + apply(incoming, high[...], low[...])
-
-
-def whole_call(kernel, shapes, flops, scalars, arrays, scratch=(), vmem=8):
+    high = jnp.concatenate([high_first[...], high_second[...]], axis=0)
+    low = jnp.concatenate([low_first[...], low_second[...]], axis=0)
+    out[...] = base[...] + apply(incoming, high, low)
+
+
+def whole_call(kernel, shapes, flops, scalars, arrays, scratch=(), vmem=8, aliases={}):
     return pl.pallas_call(
         kernel,
         out_shape=shapes,
         in_specs=[SMEM] * len(scalars) + [VMEM] * len(arrays),
         out_specs=jax.tree.map(lambda shape: VMEM, shapes),
         scratch_shapes=list(scratch),
+        input_output_aliases=aliases,
         compiler_params=pltpu.CompilerParams(vmem_limit_bytes=vmem << 20),
         cost_estimate=pl.CostEstimate(
             flops=flops, bytes_accessed=4_000_000, transcendentals=0
@@ -519,15 +535,18 @@
         pieces += [swapped(piece, "col", distance) for piece in pieces]
         if owners == [0]:
             pair = shape((2,) + refl_v.shape[2:])
-            left, right = whole_call(edges_kernel, [pair, pair], 10_000_000, [], [refl_v])
+            refl_v, left, right = whole_call(
+                edges_kernel, [shape(refl_v.shape), pair, pair], 10_000_000, [], [refl_v],
+                aliases={0: 0},
+            )
             left, right = shifted(left, 1), shifted(right, -1)
             if slots <= 16:
                 one, two = reflect(refl_v, (0, 1))
             else:
                 [one], [two] = reflect(refl_v, (0,)), reflect(refl_v, (1,))
-            high1, low1, qh1, ql1, maps1, upto1, beyond = one
-            high2, low2, qh2, ql2, maps2, upto2, _ = two
-            pieces[-1] = after_all(pieces[-1], beyond, left, right)
+            high1, low1, qh1, ql1, *joins1, upto1, beyond = one
+            high2, low2, qh2, ql2, *joins2, upto2, _ = two
+            pieces = list(lax.optimization_barrier((*pieces, beyond, left, right))[:2])
         owners += [owner ^ distance for owner in owners]
         distance //= 2
     k_pair = jax.ShapeDtypeStruct((2,) + (2 * spread, 2 * spread), BF16)
@@ -549,56 +568,61 @@
         functools.partial(response_kernel, slots),
         [shape((slots + 1,) + square), shape((runs,) + square), shape((3,) + square)],
         4_000_000_000, starts,
-        [qh1, ql1, qrh, qrl, after_all(reach, merged), lh, ll, high2, low2, maps2,
+        [qh1, ql1, qrh, qrl, after_all(reach, merged), lh, ll, high2, low2, *joins2,
          totals],
         [pltpu.VMEM((spread, columns + 3 * spread), F32)],
     )
     line, state1 = whole_call(
         functools.partial(first_kernel, slots),
         [shape((rows, columns + 3 * spread)), shape((rows, spread))], 3_000_000_000, starts,
-        [after_all(merged, maps), after, lh, ll, high1, low1, rh, rl, maps1, qh1, ql1, qrh, qrl],
+        [after_all(merged, maps), after, lh, ll, high1, low1, rh, rl, *joins1, qh1, ql1, qrh, qrl],
         [pltpu.VMEM((slots + 3, rows, spread), F32), pltpu.VMEM((runs, rows, spread), F32)],
     )
     states = shape((rows, 2 * spread))
-    y2, joins2, state, head2 = whole_call(
+    y2, entries2, state, head2 = whole_call(
         functools.partial(second_kernel, slots),
         [shape((slots + 1, rows, spread)), shape((runs, rows, spread)), states,
          shape((rows, spread))],
         3_000_000_000, starts,
-        [line, state1, lh, ll, high2, low2, maps2],
-    )
-    groups = []
+        [line, state1, lh, ll, high2, low2, *joins2],
+    )
+    home = jax.ShapeDtypeStruct((spread, columns), BF16)
+    home_line = pltpu.VMEM((spread, columns + spread), F32)
+    high_second, low_second = whole_call(
+        functools.partial(home_second_kernel, slots), [home, home], 3_000_000_000, starts,
+        [after_all(reach, state), qh2, ql2, lh, ll], [home_line],
+    )
+    groups, inside, enters = [], None, None
     for level in range(levels - 1):
-        other = swapped(maps, "row", 1 << level)
-        arrays = [maps, other if level else after_all(other, state)]
-        arrays += [inside] if level else []
-        high, maps, inside = whole_call(
-            functools.partial(join_maps_kernel, level), [shape((3,) + square)] * 3,
-            400_000_000, [], arrays,
+        other, state_other = swapped(maps, "row", 1 << level), swapped(state, "row", 1 << level)
+        if level == 0:
+            other = after_all(other, state)
+        if level == levels - 2:
+            base = whole_call(
+                functools.partial(base_kernel, slots), shape((rows, columns)), 2_000_000_000, starts,
+                [after_all(head2, state), entries2, y2, qh2, ql2],
+                [pltpu.VMEM((rows, columns + spread), F32)],
+            )
+            other = after_all(other, base)
+        high, inner, *maps = whole_call(
+            functools.partial(join_maps_kernel, level),
+            [shape((3,) + square)] * (2 if level == levels - 2 else 3), 400_000_000, [],
+            [maps, other] + ([inside] if level else []),
         )
-        groups.append((high, inside))
-
-    base = whole_call(
-        functools.partial(base_kernel, slots), shape((rows, columns)), 2_000_000_000, starts,
-        [head2, joins2, y2, qh2, ql2], [pltpu.VMEM((rows, columns + spread), F32)],
-    )
-    enters = None
-    for level in range(levels - 1):
-        arrays = [state, swapped(state, "row", 1 << level), groups[level][0]]
-        arrays += [groups[level - 1][1], enters] if level else []
+        maps = maps[0] if maps else None
+        arrays = [state, state_other, high] + ([inside, enters] if level else [])
         state, enters = whole_call(
             functools.partial(join_states_kernel, level), [states] * 2, 100_000_000, [], arrays,
         )
+        inside = inner
     half = swapped(state, "row", 1 << (levels - 1))
-    home = jax.ShapeDtypeStruct((2 * spread, columns), BF16)
-    home_high, home_low = whole_call(
-        functools.partial(home_kernel, slots), [home, home], 3_000_000_000, starts,
-        [after_all(joins_response, state), y_response, qh2, ql2, reach, lh, ll],
-        [pltpu.VMEM((spread, columns + spread), F32)],
+    high_first, low_first = whole_call(
+        functools.partial(home_first_kernel, slots), [home, home], 1_500_000_000, starts,
+        [after_all(joins_response, state), y_response, qh2, ql2], [home_line],
     )
     return whole_call(
         functools.partial(final_kernel, levels), shape((rows, columns)), 1_000_000_000, [],
-        [half, groups[-1][1], enters, base, home_high, home_low],
+        [half, inside, enters, base, high_first, high_second, low_first, low_second],
     )
 
 

time: 53.3 us -> 53.2 us (level)
  waiting for transfers between devices: 6.8 us -> 7.68 us
  starting transfers between devices: 15.3 us -> 14.6 us
    ppermute x8, starting transfers between devices: 7.71 us -> 6.79 us  [swapped(): lax.ppermute(array, axis, [(i, i ^ distance) for i in range(devices)])]
    ppermute x8, waiting for transfers between devices: 6.25 us -> 6.89 us  [swapped(): lax.ppermute(array, axis, [(i, i ^ distance) for i in range(devices)])]
    pallas_call x14 -> x15, Pallas kernels: 28.6 us -> 28.4 us  [whole_call(): pl.pallas_call(kernel, out_shape=shapes, in_specs=[SMEM] * len(scalars) +...]
    unnamed x10 -> x7, local copies, waits for them, and re-layouts: 2.21 us -> 2.2 us
  transfers between devices with their start and end apart: 11 -> 11, of which waited for: 5 -> 6; matrix products, arithmetic and copies ran while one was open for 0% -> 0% of each run, Pallas kernels for 49% -> 49%
where the time goes in v5:
time: 53.2 us; the launch traced here: 53.1 us
  Pallas kernels  28.4 us (53%)
  starting transfers between devices  14.6 us (27%)
  waiting for transfers between devices  7.68 us (14%)
  local copies, waits for them, and re-layouts  2.22 us (4%)
    pallas_call x15, Pallas kernels, whole_call(): pl.pallas_call(kernel, out_shape=shapes, in_specs=[SMEM] * len(scalars) +...  28.4 us
    ppermute x3, starting transfers between devices, shifted(): lax.ppermute(array, 'row', [(i, (i + by) % devices) for i in range(device...  7.83 us
    ppermute x8, waiting for transfers between devices, swapped(): lax.ppermute(array, axis, [(i, i ^ distance) for i in range(devices)])  6.89 us
    ppermute x8, starting transfers between devices, swapped(): lax.ppermute(array, axis, [(i, i ^ distance) for i in range(devices)])  6.79 us
    unnamed x7, local copies, waits for them, and re-layouts  2.2 us
  transfers between devices with their start and end apart: 11, of which 6 were waited for; matrix products, arithmetic and copies ran while one was open for 0% of the time, Pallas kernels for 49%

profile of v5, /device:TPU:0, one launch (start us, length us, event | category | flops | bytes accessed | tf_op | source)
XLA Modules:
  0.0 53.1 jit_solution(7879627591505875239)
XLA Ops:
  0.0 2.2 %copy.8.source = f32[2,16,256,128]{3,2,1,0:T(8,128)S(1)} copy(f32[2,16,256,128]{3,2,1,0:T(8,128)} %param.6) | data formatting | bytes 8388608
  2.2 0.0 copy-start
  2.2 3.0 %collective-permute-start.1 = (f32[2,256,128]{2,1,0:T(8,128)S(1)}, f32[2,256,128]{2,1,0:T(8,128)S(1)}, u32[]{:S(2)}, u32[]{:S(2)}) collective-permute-start(f32[2,256,128]{2,1,0:T(8,128)S(1)} %get-tuple-element.65), channel_id=1, source_target_pairs={{0,4},{4,8},{8,12},{12,16},{16,20},{20,24},{24,28},{28,0},{1,5},{5... | collective-permute-start | bytes 786440 | tf_op jit(solution)/shard_map/ppermute | solution.py:282
  5.2 3.1 %collective-permute-start.2 = (f32[2,256,128]{2,1,0:T(8,128)S(1)}, f32[2,256,128]{2,1,0:T(8,128)S(1)}, u32[]{:S(2)}, u32[]{:S(2)}) collective-permute-start(f32[2,256,128]{2,1,0:T(8,128)S(1)} %get-tuple-element.66), channel_id=1, source_target_pairs={{0,28},{4,0},{8,4},{12,8},{16,12},{20,16},{24,20},{28,24},{1,29},{... | collective-permute-start | bytes 786440 | tf_op jit(solution)/shard_map/ppermute | solution.py:282
  8.3 0.0 copy-done
  8.3 1.6 %collective-permute-start = (f32[64,2048]{1,0:T(8,128)S(1)}, f32[64,2048]{1,0:T(8,128)S(1)}, u32[]{:S(2)}, u32[]{:S(2)}) collective-permute-start(f32[64,2048]{1,0:T(8,128)S(1)} %copy-done), channel_id=1, source_target_pairs={{0,2},{1,3},{2,0},{3,1},{4,6},{5,7},{6,4},{7,5},{8,10},{9,11},{10,... | collective-permute-start | bytes 1572872 | tf_op jit(solution)/shard_map/ppermute | solution.py:287
  10.0 11.1 %shard_map.47 = (bf16[16,256,256]{2,1,0:T(8,128)(2,1)S(1)}, bf16[16,256,256]{2,1,0:T(8,128)(2,1)S(1)}, bf16[16,128,128]{2,1,0:T(8,128)(2,1)S(1)}, bf16[16,128,12...) custom-call(f32[2,16,256,128]{3,2,1,0:T(8,128)S(1)} %get-tuple-eleme, ...), custom_call_target="tpu_custom_call" | custom-call | flops 9600000000 | bytes 4000000 | tf_op jit(solution)/shard_map/pallas_call | solution.py:508
  21.1 0.0 collective-permute-done.1.left
  21.1 0.0 collective-permute-done.2.right
  21.1 0.6 %collective-permute-done.refs_1_ = f32[64,2048]{1,0:T(8,128)S(1)} collective-permute-done((f32[64,2048]{1,0:T(8,128)S(1)}, f32[64,2048]{1,0:T(8,128)S(1)}, u32[]{:S(2)}, u32[]{:S(2)}) %collective-permute-start) | collective-permute-done | bytes 524320 | tf_op jit(solution)/shard_map/ppermute | solution.py:287
  21.7 0.0 collective-permute-start.3
  21.7 0.5 collective-permute-start.4
  22.2 0.0 copy-start.1
  22.2 3.2 %shard_map.48 = (bf16[2,256,256]{2,1,0:T(8,128)(2,1)S(1)}, bf16[2,256,256]{2,1,0:T(8,128)(2,1)S(1)}, bf16[2,256,256]{2,1,0:T(8,128)(2,1)S(1)}, bf16[2,256,256]{2...) custom-call(f32[2,256,128]{2,1,0:T(8,128)S(1)} %collective-permute-d, ...), custom_call_target="tpu_custom_call" | custom-call | flops 2000000000 | bytes 4000000 | tf_op jit(solution)/shard_map/pallas_call | solution.py:508
  25.5 0.0 copy-start.2
  25.5 0.0 collective-permute-done.3.refs_2_
  25.5 0.0 collective-permute-done.4.refs_3_
  25.5 0.0 copy-done.1
  25.5 0.9 %shard_map.49.home = f32[64,2048]{1,0:T(8,128)S(1)} custom-call(f32[256,256]{1,0:T(8,128)S(1)} %copy-done.1, f32[64,2048]{1,0:T(8,128)S(1)} %copy-done, f32[64,2048]{1,0:T(8,128)S(1)} %collective-permute-done.refs_1_, f32[64,2048]{1,0:T(8,128)S(1)} %collective-permute-done.3.refs_2_, f32[64,2048]{1,0:T(8,128)S(1)} %collective-permute-done.4.refs_3_), custom_call_target="tpu_custom_call" | custom-call | flops 1000000000 | bytes 4000000 | tf_op jit(solution)/shard_map/pallas_call | solution.py:508
  26.4 1.7 %collective-permute-start.5 = (f32[64,512]{1,0:T(8,128)S(1)}, f32[64,512]{1,0:T(8,128)S(1)}, u32[]{:S(2)}, u32[]{:S(2)}) collective-permute-start(f32[64,512]{1,0:T(8,128)S(1)} %slice.4), channel_id=1, source_target_pairs={{0,28},{4,0},{8,4},{12,8},{16,12},{20,16},{24,20},{28,24},{1,29},{... | collective-permute-start | bytes 393224 | tf_op jit(solution)/shard_map/ppermute | solution.py:282
  28.2 0.0 copy-done.2
  28.2 2.5 %shard_map.50 = (f32[17,128,128]{2,1,0:T(8,128)S(1)}, f32[5,128,128]{2,1,0:T(8,128)S(1)}, f32[3,128,128]{2,1,0:T(8,128)S(1)}) custom-call(s32[2]{0:T(128)S(1)} %copy-done.2, bf16[16,128,128]{2,1,0:T(8,128)(2,1)S(1)} %get-tuple-element.73.q_high, bf16[16,128,128]{2,1,0:T(8,128)(2,1)S(1)} %get-tuple-element.74.q_low, ...), custom_call_target="tpu_custom_call" | custom-call | flops 4000000000 | bytes 4000000 | tf_op jit(solution)/shard_map/pallas_call | solution.py:508
  30.7 0.4 collective-permute-start.7
  31.1 0.8 %collective-permute-done.5.after = f32[64,512]{1,0:T(8,128)S(1)} collective-permute-done((f32[64,512]{1,0:T(8,128)S(1)}, f32[64,512]{1,0:T(8,128)S(1)}, u32[]{:S(2)}, u32[]{:S(2)}) %collective-permute-start.5) | collective-permute-done | bytes 131104 | tf_op jit(solution)/shard_map/ppermute | solution.py:282
  31.9 2.4 %shard_map.51 = (f32[64,2432]{1,0:T(8,128)S(1)}, f32[64,128]{1,0:T(8,128)S(1)}) custom-call(s32[2]{0:T(128)S(1)} %copy-done.2, f32[64,2048]{1,0:T(8,128)S(1)} %shard_map.49.home, f32[64,512]{1,0:T(8,128)S(1)} %collective-permute-done.5.after, bf16[2,256,256]{2,1,0:T(8,128)(2,1)S(1)} %get-tuple-element.79.left_high, ...), custom_call_target="tpu_custom_call" | custom-call | flops 3000000000 | bytes 4000000 | tf_op jit(solution)/shard_map/pallas_call | solution.py:508
  34.3 1.9 %shard_map.52 = (f32[17,64,128]{2,1,0:T(8,128)S(1)}, f32[5,64,128]{2,1,0:T(8,128)S(1)}, f32[64,256]{1,0:T(8,128)S(1)}, f32[64,128]{1,0:T(8,128)S(1)}) custom-call(s32[2]{0:T(128)S(1)} %copy-done.2, f32[64,2432]{1,0:T(8,128)S(1)} %get-tuple-element.93.line, f32[64,128]{1,0:T(8,128)S(1)} %get-tuple-element.94.state_in, ...), custom_call_target="tpu_custom_call" | custom-call | flops 3000000000 | bytes 4000000 | tf_op jit(solution)/shard_map/pallas_call | solution.py:508
  36.2 0.9 %collective-permute-start.6 = (f32[64,256]{1,0:T(8,128)S(1)}, f32[64,256]{1,0:T(8,128)S(1)}, u32[]{:S(2)}, u32[]{:S(2)}) collective-permute-start(f32[64,256]{1,0:T(8,128)S(1)} %get-tuple-element.95.mine), channel_id=1, source_target_pairs={{0,4},{4,0},{8,12},{12,8},{16,20},{20,16},{24,28},{28,24},{1,5},{5... | collective-permute-start | bytes 196616 | tf_op jit(solution)/shard_map/ppermute | solution.py:287
  37.0 1.4 %shard_map.59 = (bf16[128,2048]{1,0:T(8,128)(2,1)S(1)}, bf16[128,2048]{1,0:T(8,128)(2,1)S(1)}) custom-call(s32[2]{0:T(128)S(1)} %copy-done.2, f32[2,4,128,128]{3,2,1,0:T(8,128)S(1)} %get-tuple-element.117.reach, bf16[16,128,128]{2,1,0:T(8,128)(2,1)S(1)} %get-tuple-element.104.q_high, bf16[16,128,128]{2,1,0:T(8,128)(2,1)S(1)} %get-tuple-element.105.q_low, ...), custom_call_target="tpu_custom_call" | custom-call | flops 3000000000 | bytes 4000000 | tf_op jit(solution)/shard_map/pallas_call | solution.py:508
  38.4 0.0 collective-permute-done.7.refs_1_
  38.4 0.3 shard_map.53
  38.7 0.3 collective-permute-start.9
  39.0 1.4 %collective-permute-done.6.other = f32[64,256]{1,0:T(8,128)S(1)} collective-permute-done((f32[64,256]{1,0:T(8,128)S(1)}, f32[64,256]{1,0:T(8,128)S(1)}, u32[]{:S(2)}, u32[]{:S(2)}) %collective-permute-start.6) | collective-permute-done | bytes 65568 | tf_op jit(solution)/shard_map/ppermute | solution.py:287
  40.5 0.2 shard_map.54
  40.7 0.4 collective-permute-start.8
  41.1 1.1 %shard_map.55.base = f32[64,2048]{1,0:T(8,128)S(1)} custom-call(s32[2]{0:T(128)S(1)} %copy-done.2, f32[64,128]{1,0:T(8,128)S(1)} %get-tuple-element.101.head, f32[5,64,128]{2,1,0:T(8,128)S(1)} %get-tuple-element.102.joins, f32[17,64,128]{2,1,0:T(8,128)S(1)} %get-tuple-element.103.y_local, bf16[16,128,128]{2,1,0:T(8,128)(2,1)S(1)} %get-tuple-element.104.q_high, ...), custom_call_target="tpu_custom_call" | custom-call | flops 2000000000 | bytes 4000000 | tf_op jit(solution)/shard_map/pallas_call | solution.py:508
  42.3 3.2 %collective-permute-done.9.refs_1_ = f32[3,128,128]{2,1,0:T(8,128)S(1)} collective-permute-done((f32[3,128,128]{2,1,0:T(8,128)S(1)}, f32[3,128,128]{2,1,0:T(8,128)S(1)}, u32[]{:S(2)}, u32[]{:S(2)}) %collective-permute-start.9) | collective-permute-done | bytes 196640 | tf_op jit(solution)/shard_map/ppermute | solution.py:287
  45.5 0.3 shard_map.56
  45.8 0.4 collective-permute-done.8.other
  46.2 0.3 shard_map.57
  46.4 2.6 %collective-permute-start.10 = (f32[64,256]{1,0:T(8,128)S(1)}, f32[64,256]{1,0:T(8,128)S(1)}, u32[]{:S(2)}, u32[]{:S(2)}) collective-permute-start(f32[64,256]{1,0:T(8,128)S(1)} %get-tuple-element.110), channel_id=1, source_target_pairs={{0,16},{4,20},{8,24},{12,28},{16,0},{20,4},{24,8},{28,12},{1,17},{... | collective-permute-start | bytes 196616 | tf_op jit(solution)/shard_map/ppermute | solution.py:287
  49.1 1.4 %shard_map.58 = (bf16[128,2048]{1,0:T(8,128)(2,1)S(1)}, bf16[128,2048]{1,0:T(8,128)(2,1)S(1)}) custom-call(s32[2]{0:T(128)S(1)} %copy-done.2, f32[5,128,128]{2,1,0:T(8,128)S(1)} %get-tuple-element.114.joins, f32[17,128,128]{2,1,0:T(8,128)S(1)} %get-tuple-element.115.y_local, bf16[16,128,128]{2,1,0:T(8,128)(2,1)S(1)} %get-tuple-element.104.q_high, ...), custom_call_target="tpu_custom_call" | custom-call | flops 1500000000 | bytes 4000000 | tf_op jit(solution)/shard_map/pallas_call | solution.py:508
  50.5 1.2 %collective-permute-done.10.half = f32[64,256]{1,0:T(8,128)S(1)} collective-permute-done((f32[64,256]{1,0:T(8,128)S(1)}, f32[64,256]{1,0:T(8,128)S(1)}, u32[]{:S(2)}, u32[]{:S(2)}) %collective-permute-start.10) | collective-permute-done | bytes 65568 | tf_op jit(solution)/shard_map/ppermute | solution.py:287
  51.7 1.4 %shard_map.60 = f32[64,2048]{1,0:T(8,128)} custom-call(f32[64,256]{1,0:T(8,128)S(1)} %collective-permute-done.10.half, f32[3,128,128]{2,1,0:T(8,128)S(1)} %get-tuple-element.111.inner, f32[64,256]{1,0:T(8,128)S(1)} %get-tuple-element.112.before, f32[64,2048]{1,0:T(8,128)S(1)} %shard_map.55.base, bf16[128,2048]{1,0:T(8,128)(2,1)S(1)} %get-tuple-element.116.high_first, ...), custom_call_target="tpu_custom_call" | custom-call | flops 1000000000 | bytes 4000000 | tf_op jit(solution)/shard_map/pallas_call | solution.py:508
  (2 shorter events, 0.1 us)
Async XLA Ops:
  2.2 6.1 %copy-start = (f32[64,2048]{1,0:T(8,128)S(1)}, f32[64,2048]{1,0:T(8,128)}, u32[]{:S(2)}) copy-start(f32[64,2048]{1,0:T(8,128)} %refs_0_) | copy-start | bytes 1572868
  2.2 18.9 %collective-permute-start.1 = (f32[2,256,128]{2,1,0:T(8,128)S(1)}, f32[2,256,128]{2,1,0:T(8,128)S(1)}, u32[]{:S(2)}, u32[]{:S(2)}) collective-permute-start(f32[2,256,128]{2,1,0:T(8,128)S(1)} %get-tuple-element.65), channel_id=1, source_target_pairs={{0,4},{4,8},{8,12},{12,16},{16,20},{20,24},{24,28},{28,0},{1,5},{5... | collective-permute-start | bytes 786440 | tf_op jit(solution)/shard_map/ppermute | solution.py:282
  5.2 15.9 %collective-permute-start.2 = (f32[2,256,128]{2,1,0:T(8,128)S(1)}, f32[2,256,128]{2,1,0:T(8,128)S(1)}, u32[]{:S(2)}, u32[]{:S(2)}) collective-permute-start(f32[2,256,128]{2,1,0:T(8,128)S(1)} %get-tuple-element.66), channel_id=1, source_target_pairs={{0,28},{4,0},{8,4},{12,8},{16,12},{20,16},{24,20},{28,24},{1,29},{... | collective-permute-start | bytes 786440 | tf_op jit(solution)/shard_map/ppermute | solution.py:282
  8.3 13.4 %collective-permute-start = (f32[64,2048]{1,0:T(8,128)S(1)}, f32[64,2048]{1,0:T(8,128)S(1)}, u32[]{:S(2)}, u32[]{:S(2)}) collective-permute-start(f32[64,2048]{1,0:T(8,128)S(1)} %copy-done), channel_id=1, source_target_pairs={{0,2},{1,3},{2,0},{3,1},{4,6},{5,7},{6,4},{7,5},{8,10},{9,11},{10,... | collective-permute-start | bytes 1572872 | tf_op jit(solution)/shard_map/ppermute | solution.py:287
  21.7 3.8 %collective-permute-start.3 = (f32[64,2048]{1,0:T(8,128)S(1)}, f32[64,2048]{1,0:T(8,128)S(1)}, u32[]{:S(2)}, u32[]{:S(2)}) collective-permute-start(f32[64,2048]{1,0:T(8,128)S(1)} %copy-done), channel_id=1, source_target_pairs={{0,1},{1,0},{2,3},{3,2},{4,5},{5,4},{6,7},{7,6},{8,9},{9,8},{10,11... | collective-permute-start | bytes 1572872 | tf_op jit(solution)/shard_map/ppermute | solution.py:287
  21.7 3.8 %collective-permute-start.4 = (f32[64,2048]{1,0:T(8,128)S(1)}, f32[64,2048]{1,0:T(8,128)S(1)}, u32[]{:S(2)}, u32[]{:S(2)}) collective-permute-start(f32[64,2048]{1,0:T(8,128)S(1)} %collective-permute-done.refs_1_), channel_id=1, source_target_pairs={{0,1},{1,0},{2,3},{3,2},{4,5},{5,4},{6,7},{7,6},{8,9},{9,8},{10,11... | collective-permute-start | bytes 1572872 | tf_op jit(solution)/shard_map/ppermute | solution.py:287
  22.2 3.3 %copy-start.1 = (f32[256,256]{1,0:T(8,128)S(1)}, f32[256,256]{1,0:T(8,128)}, u32[]{:S(2)}) copy-start(f32[256,256]{1,0:T(8,128)} %cauchy.1) | copy-start | bytes 786436
  25.5 2.7 %copy-start.2 = (s32[2]{0:T(128)S(1)}, s32[2]{0:T(128)}, u32[]{:S(2)}) copy-start(s32[2]{0:T(128)} %start.11) | copy-start | bytes 28
  26.4 5.5 %collective-permute-start.5 = (f32[64,512]{1,0:T(8,128)S(1)}, f32[64,512]{1,0:T(8,128)S(1)}, u32[]{:S(2)}, u32[]{:S(2)}) collective-permute-start(f32[64,512]{1,0:T(8,128)S(1)} %slice.4), channel_id=1, source_target_pairs={{0,28},{4,0},{8,4},{12,8},{16,12},{20,16},{24,20},{28,24},{1,29},{... | collective-permute-start | bytes 393224 | tf_op jit(solution)/shard_map/ppermute | solution.py:282
  30.7 7.7 %collective-permute-start.7 = (f32[3,128,128]{2,1,0:T(8,128)S(1)}, f32[3,128,128]{2,1,0:T(8,128)S(1)}, u32[]{:S(2)}, u32[]{:S(2)}) collective-permute-start(f32[3,128,128]{2,1,0:T(8,128)S(1)} %get-tuple-element.85.refs_0_), channel_id=1, source_target_pairs={{0,4},{4,0},{8,12},{12,8},{16,20},{20,16},{24,28},{28,24},{1,5},{5... | collective-permute-start | bytes 589832 | tf_op jit(solution)/shard_map/ppermute | solution.py:287
  36.2 4.3 %collective-permute-start.6 = (f32[64,256]{1,0:T(8,128)S(1)}, f32[64,256]{1,0:T(8,128)S(1)}, u32[]{:S(2)}, u32[]{:S(2)}) collective-permute-start(f32[64,256]{1,0:T(8,128)S(1)} %get-tuple-element.95.mine), channel_id=1, source_target_pairs={{0,4},{4,0},{8,12},{12,8},{16,20},{20,16},{24,28},{28,24},{1,5},{5... | collective-permute-start | bytes 196616 | tf_op jit(solution)/shard_map/ppermute | solution.py:287
  38.7 6.7 %collective-permute-start.9 = (f32[3,128,128]{2,1,0:T(8,128)S(1)}, f32[3,128,128]{2,1,0:T(8,128)S(1)}, u32[]{:S(2)}, u32[]{:S(2)}) collective-permute-start(f32[3,128,128]{2,1,0:T(8,128)S(1)} %get-tuple-element.99.refs_0_), channel_id=1, source_target_pairs={{0,8},{4,12},{8,0},{12,4},{16,24},{20,28},{24,16},{28,20},{1,9},{5... | collective-permute-start | bytes 589832 | tf_op jit(solution)/shard_map/ppermute | solution.py:287
  40.7 5.5 %collective-permute-start.8 = (f32[64,256]{1,0:T(8,128)S(1)}, f32[64,256]{1,0:T(8,128)S(1)}, u32[]{:S(2)}, u32[]{:S(2)}) collective-permute-start(f32[64,256]{1,0:T(8,128)S(1)} %get-tuple-element.98.mine), channel_id=1, source_target_pairs={{0,8},{4,12},{8,0},{12,4},{16,24},{20,28},{24,16},{28,20},{1,9},{5... | collective-permute-start | bytes 196616 | tf_op jit(solution)/shard_map/ppermute | solution.py:287
  46.4 5.2 %collective-permute-start.10 = (f32[64,256]{1,0:T(8,128)S(1)}, f32[64,256]{1,0:T(8,128)S(1)}, u32[]{:S(2)}, u32[]{:S(2)}) collective-permute-start(f32[64,256]{1,0:T(8,128)S(1)} %get-tuple-element.110), channel_id=1, source_target_pairs={{0,16},{4,20},{8,24},{12,28},{16,0},{20,4},{24,8},{28,12},{1,17},{... | collective-permute-start | bytes 196616 | tf_op jit(solution)/shard_map/ppermute | solution.py:287

commit v6 on v5

--- a/solution.py
+++ b/solution.py
@@ -586,12 +586,6 @@
         3_000_000_000, starts,
         [line, state1, lh, ll, high2, low2, *joins2],
     )
-    home = jax.ShapeDtypeStruct((spread, columns), BF16)
-    home_line = pltpu.VMEM((spread, columns + spread), F32)
-    high_second, low_second = whole_call(
-        functools.partial(home_second_kernel, slots), [home, home], 3_000_000_000, starts,
-        [after_all(reach, state), qh2, ql2, lh, ll], [home_line],
-    )
     groups, inside, enters = [], None, None
     for level in range(levels - 1):
         other, state_other = swapped(maps, "row", 1 << level), swapped(state, "row", 1 << level)
@@ -610,6 +604,13 @@
             [maps, other] + ([inside] if level else []),
         )
         maps = maps[0] if maps else None
+        if level == 0:
+            home = jax.ShapeDtypeStruct((spread, columns), BF16)
+            home_line = pltpu.VMEM((spread, columns + spread), F32)
+            high_second, low_second = whole_call(
+                functools.partial(home_second_kernel, slots), [home, home], 3_000_000_000, starts,
+                [after_all(reach, high), qh2, ql2, lh, ll], [home_line],
+            )
         arrays = [state, state_other, high] + ([inside, enters] if level else [])
         state, enters = whole_call(
             functools.partial(join_states_kernel, level), [states] * 2, 100_000_000, [], arrays,

time: 53.2 us -> 52.1 us (0.979)
  starting transfers between devices: 14.6 us -> 13.8 us
    ppermute x8, starting transfers between devices: 6.79 us -> 6 us  [swapped(): lax.ppermute(array, axis, [(i, i ^ distance) for i in range(devices)])]
  transfers between devices with their start and end apart: 11 -> 11, of which waited for: 6 -> 7; matrix products, arithmetic and copies ran while one was open for 0% -> 0% of each run, Pallas kernels for 49% -> 50%
where the time goes in v6:
time: 52.1 us; the launch traced here: 51.9 us
  Pallas kernels  28.4 us (55%)
  starting transfers between devices  13.8 us (26%)
  waiting for transfers between devices  7.31 us (14%)
  local copies, waits for them, and re-layouts  2.22 us (4%)
    pallas_call x15, Pallas kernels, whole_call(): pl.pallas_call(kernel, out_shape=shapes, in_specs=[SMEM] * len(scalars) +...  28.4 us
    ppermute x3, starting transfers between devices, shifted(): lax.ppermute(array, 'row', [(i, (i + by) % devices) for i in range(device...  7.83 us
    ppermute x8, waiting for transfers between devices, swapped(): lax.ppermute(array, axis, [(i, i ^ distance) for i in range(devices)])  6.52 us
    ppermute x8, starting transfers between devices, swapped(): lax.ppermute(array, axis, [(i, i ^ distance) for i in range(devices)])  6 us
    unnamed x7, local copies, waits for them, and re-layouts  2.2 us
  transfers between devices with their start and end apart: 11, of which 7 were waited for; matrix products, arithmetic and copies ran while one was open for 0% of the time, Pallas kernels for 50%

profile of v6, /device:TPU:0, one launch (start us, length us, event | category | flops | bytes accessed | tf_op | source)
XLA Modules:
  0.0 51.9 jit_solution(1634321522629625591)
XLA Ops:
  0.0 2.2 %copy.8.source = f32[2,16,256,128]{3,2,1,0:T(8,128)S(1)} copy(f32[2,16,256,128]{3,2,1,0:T(8,128)} %param.6) | data formatting | bytes 8388608
  2.2 0.0 copy-start
  2.2 3.0 %collective-permute-start.1 = (f32[2,256,128]{2,1,0:T(8,128)S(1)}, f32[2,256,128]{2,1,0:T(8,128)S(1)}, u32[]{:S(2)}, u32[]{:S(2)}) collective-permute-start(f32[2,256,128]{2,1,0:T(8,128)S(1)} %get-tuple-element.65), channel_id=1, source_target_pairs={{0,4},{4,8},{8,12},{12,16},{16,20},{20,24},{24,28},{28,0},{1,5},{5... | collective-permute-start | bytes 786440 | tf_op jit(solution)/shard_map/ppermute | solution.py:282
  5.2 3.1 %collective-permute-start.2 = (f32[2,256,128]{2,1,0:T(8,128)S(1)}, f32[2,256,128]{2,1,0:T(8,128)S(1)}, u32[]{:S(2)}, u32[]{:S(2)}) collective-permute-start(f32[2,256,128]{2,1,0:T(8,128)S(1)} %get-tuple-element.66), channel_id=1, source_target_pairs={{0,28},{4,0},{8,4},{12,8},{16,12},{20,16},{24,20},{28,24},{1,29},{... | collective-permute-start | bytes 786440 | tf_op jit(solution)/shard_map/ppermute | solution.py:282
  8.3 0.0 copy-done
  8.3 1.6 %collective-permute-start = (f32[64,2048]{1,0:T(8,128)S(1)}, f32[64,2048]{1,0:T(8,128)S(1)}, u32[]{:S(2)}, u32[]{:S(2)}) collective-permute-start(f32[64,2048]{1,0:T(8,128)S(1)} %copy-done), channel_id=1, source_target_pairs={{0,2},{1,3},{2,0},{3,1},{4,6},{5,7},{6,4},{7,5},{8,10},{9,11},{10,... | collective-permute-start | bytes 1572872 | tf_op jit(solution)/shard_map/ppermute | solution.py:287
  10.0 11.1 %shard_map.47 = (bf16[16,256,256]{2,1,0:T(8,128)(2,1)S(1)}, bf16[16,256,256]{2,1,0:T(8,128)(2,1)S(1)}, bf16[16,128,128]{2,1,0:T(8,128)(2,1)S(1)}, bf16[16,128,12...) custom-call(f32[2,16,256,128]{3,2,1,0:T(8,128)S(1)} %get-tuple-eleme, ...), custom_call_target="tpu_custom_call" | custom-call | flops 9600000000 | bytes 4000000 | tf_op jit(solution)/shard_map/pallas_call | solution.py:508
  21.1 0.0 collective-permute-done.1.left
  21.1 0.0 collective-permute-done.2.right
  21.1 0.6 %collective-permute-done.refs_1_ = f32[64,2048]{1,0:T(8,128)S(1)} collective-permute-done((f32[64,2048]{1,0:T(8,128)S(1)}, f32[64,2048]{1,0:T(8,128)S(1)}, u32[]{:S(2)}, u32[]{:S(2)}) %collective-permute-start) | collective-permute-done | bytes 524320 | tf_op jit(solution)/shard_map/ppermute | solution.py:287
  21.7 0.0 collective-permute-start.3
  21.7 0.5 collective-permute-start.4
  22.2 0.0 copy-start.1
  22.2 3.2 %shard_map.48 = (bf16[2,256,256]{2,1,0:T(8,128)(2,1)S(1)}, bf16[2,256,256]{2,1,0:T(8,128)(2,1)S(1)}, bf16[2,256,256]{2,1,0:T(8,128)(2,1)S(1)}, bf16[2,256,256]{2...) custom-call(f32[2,256,128]{2,1,0:T(8,128)S(1)} %collective-permute-d, ...), custom_call_target="tpu_custom_call" | custom-call | flops 2000000000 | bytes 4000000 | tf_op jit(solution)/shard_map/pallas_call | solution.py:508
  25.5 0.0 copy-start.2
  25.5 0.0 collective-permute-done.3.refs_2_
  25.5 0.0 collective-permute-done.4.refs_3_
  25.5 0.0 copy-done.1
  25.5 0.9 %shard_map.49.home = f32[64,2048]{1,0:T(8,128)S(1)} custom-call(f32[256,256]{1,0:T(8,128)S(1)} %copy-done.1, f32[64,2048]{1,0:T(8,128)S(1)} %copy-done, f32[64,2048]{1,0:T(8,128)S(1)} %collective-permute-done.refs_1_, f32[64,2048]{1,0:T(8,128)S(1)} %collective-permute-done.3.refs_2_, f32[64,2048]{1,0:T(8,128)S(1)} %collective-permute-done.4.refs_3_), custom_call_target="tpu_custom_call" | custom-call | flops 1000000000 | bytes 4000000 | tf_op jit(solution)/shard_map/pallas_call | solution.py:508
  26.4 1.7 %collective-permute-start.5 = (f32[64,512]{1,0:T(8,128)S(1)}, f32[64,512]{1,0:T(8,128)S(1)}, u32[]{:S(2)}, u32[]{:S(2)}) collective-permute-start(f32[64,512]{1,0:T(8,128)S(1)} %slice.4), channel_id=1, source_target_pairs={{0,28},{4,0},{8,4},{12,8},{16,12},{20,16},{24,20},{28,24},{1,29},{... | collective-permute-start | bytes 393224 | tf_op jit(solution)/shard_map/ppermute | solution.py:282
  28.2 0.0 copy-done.2
  28.2 2.5 %shard_map.50 = (f32[17,128,128]{2,1,0:T(8,128)S(1)}, f32[5,128,128]{2,1,0:T(8,128)S(1)}, f32[3,128,128]{2,1,0:T(8,128)S(1)}) custom-call(s32[2]{0:T(128)S(1)} %copy-done.2, bf16[16,128,128]{2,1,0:T(8,128)(2,1)S(1)} %get-tuple-element.73.q_high, bf16[16,128,128]{2,1,0:T(8,128)(2,1)S(1)} %get-tuple-element.74.q_low, ...), custom_call_target="tpu_custom_call" | custom-call | flops 4000000000 | bytes 4000000 | tf_op jit(solution)/shard_map/pallas_call | solution.py:508
  30.7 0.4 collective-permute-start.7
  31.1 0.8 %collective-permute-done.5.after = f32[64,512]{1,0:T(8,128)S(1)} collective-permute-done((f32[64,512]{1,0:T(8,128)S(1)}, f32[64,512]{1,0:T(8,128)S(1)}, u32[]{:S(2)}, u32[]{:S(2)}) %collective-permute-start.5) | collective-permute-done | bytes 131104 | tf_op jit(solution)/shard_map/ppermute | solution.py:282
  31.9 2.4 %shard_map.51 = (f32[64,2432]{1,0:T(8,128)S(1)}, f32[64,128]{1,0:T(8,128)S(1)}) custom-call(s32[2]{0:T(128)S(1)} %copy-done.2, f32[64,2048]{1,0:T(8,128)S(1)} %shard_map.49.home, f32[64,512]{1,0:T(8,128)S(1)} %collective-permute-done.5.after, bf16[2,256,256]{2,1,0:T(8,128)(2,1)S(1)} %get-tuple-element.79.left_high, ...), custom_call_target="tpu_custom_call" | custom-call | flops 3000000000 | bytes 4000000 | tf_op jit(solution)/shard_map/pallas_call | solution.py:508
  34.3 1.9 %shard_map.52 = (f32[17,64,128]{2,1,0:T(8,128)S(1)}, f32[5,64,128]{2,1,0:T(8,128)S(1)}, f32[64,256]{1,0:T(8,128)S(1)}, f32[64,128]{1,0:T(8,128)S(1)}) custom-call(s32[2]{0:T(128)S(1)} %copy-done.2, f32[64,2432]{1,0:T(8,128)S(1)} %get-tuple-element.93.line, f32[64,128]{1,0:T(8,128)S(1)} %get-tuple-element.94.state_in, ...), custom_call_target="tpu_custom_call" | custom-call | flops 3000000000 | bytes 4000000 | tf_op jit(solution)/shard_map/pallas_call | solution.py:508
  36.2 0.9 %collective-permute-start.6 = (f32[64,256]{1,0:T(8,128)S(1)}, f32[64,256]{1,0:T(8,128)S(1)}, u32[]{:S(2)}, u32[]{:S(2)}) collective-permute-start(f32[64,256]{1,0:T(8,128)S(1)} %get-tuple-element.95.mine), channel_id=1, source_target_pairs={{0,4},{4,0},{8,12},{12,8},{16,20},{20,16},{24,28},{28,24},{1,5},{5... | collective-permute-start | bytes 196616 | tf_op jit(solution)/shard_map/ppermute | solution.py:287
  37.0 0.3 collective-permute-done.7.refs_1_
  37.3 0.3 shard_map.53
  37.6 0.1 collective-permute-start.9
  37.7 2.8 %collective-permute-done.6.other = f32[64,256]{1,0:T(8,128)S(1)} collective-permute-done((f32[64,256]{1,0:T(8,128)S(1)}, f32[64,256]{1,0:T(8,128)S(1)}, u32[]{:S(2)}, u32[]{:S(2)}) %collective-permute-start.6) | collective-permute-done | bytes 65568 | tf_op jit(solution)/shard_map/ppermute | solution.py:287
  40.5 0.2 shard_map.54
  40.7 0.1 collective-permute-start.8
  40.8 1.4 %shard_map.59 = (bf16[128,2048]{1,0:T(8,128)(2,1)S(1)}, bf16[128,2048]{1,0:T(8,128)(2,1)S(1)}) custom-call(s32[2]{0:T(128)S(1)} %copy-done.2, f32[2,4,128,128]{3,2,1,0:T(8,128)S(1)} %get-tuple-element.117.reach, bf16[16,128,128]{2,1,0:T(8,128)(2,1)S(1)} %get-tuple-element.104.q_high, bf16[16,128,128]{2,1,0:T(8,128)(2,1)S(1)} %get-tuple-element.105.q_low, ...), custom_call_target="tpu_custom_call" | custom-call | flops 3000000000 | bytes 4000000 | tf_op jit(solution)/shard_map/pallas_call | solution.py:508
  42.1 1.1 %shard_map.55.base = f32[64,2048]{1,0:T(8,128)S(1)} custom-call(s32[2]{0:T(128)S(1)} %copy-done.2, f32[64,128]{1,0:T(8,128)S(1)} %get-tuple-element.101.head, f32[5,64,128]{2,1,0:T(8,128)S(1)} %get-tuple-element.102.joins, f32[17,64,128]{2,1,0:T(8,128)S(1)} %get-tuple-element.103.y_local, bf16[16,128,128]{2,1,0:T(8,128)(2,1)S(1)} %get-tuple-element.104.q_high, ...), custom_call_target="tpu_custom_call" | custom-call | flops 2000000000 | bytes 4000000 | tf_op jit(solution)/shard_map/pallas_call | solution.py:508
  43.3 0.8 %collective-permute-done.9.refs_1_ = f32[3,128,128]{2,1,0:T(8,128)S(1)} collective-permute-done((f32[3,128,128]{2,1,0:T(8,128)S(1)}, f32[3,128,128]{2,1,0:T(8,128)S(1)}, u32[]{:S(2)}, u32[]{:S(2)}) %collective-permute-start.9) | collective-permute-done | bytes 196640 | tf_op jit(solution)/shard_map/ppermute | solution.py:287
  44.1 0.3 shard_map.56
  44.4 0.6 %collective-permute-done.8.other = f32[64,256]{1,0:T(8,128)S(1)} collective-permute-done((f32[64,256]{1,0:T(8,128)S(1)}, f32[64,256]{1,0:T(8,128)S(1)}, u32[]{:S(2)}, u32[]{:S(2)}) %collective-permute-start.8) | collective-permute-done | bytes 65568 | tf_op jit(solution)/shard_map/ppermute | solution.py:287
  45.0 0.3 shard_map.57
  45.3 2.4 %collective-permute-start.10 = (f32[64,256]{1,0:T(8,128)S(1)}, f32[64,256]{1,0:T(8,128)S(1)}, u32[]{:S(2)}, u32[]{:S(2)}) collective-permute-start(f32[64,256]{1,0:T(8,128)S(1)} %get-tuple-element.110), channel_id=1, source_target_pairs={{0,16},{4,20},{8,24},{12,28},{16,0},{20,4},{24,8},{28,12},{1,17},{... | collective-permute-start | bytes 196616 | tf_op jit(solution)/shard_map/ppermute | solution.py:287
  47.7 1.4 %shard_map.58 = (bf16[128,2048]{1,0:T(8,128)(2,1)S(1)}, bf16[128,2048]{1,0:T(8,128)(2,1)S(1)}) custom-call(s32[2]{0:T(128)S(1)} %copy-done.2, f32[5,128,128]{2,1,0:T(8,128)S(1)} %get-tuple-element.114.joins, f32[17,128,128]{2,1,0:T(8,128)S(1)} %get-tuple-element.115.y_local, bf16[16,128,128]{2,1,0:T(8,128)(2,1)S(1)} %get-tuple-element.104.q_high, ...), custom_call_target="tpu_custom_call" | custom-call | flops 1500000000 | bytes 4000000 | tf_op jit(solution)/shard_map/pallas_call | solution.py:508
  49.1 1.4 %collective-permute-done.10.half = f32[64,256]{1,0:T(8,128)S(1)} collective-permute-done((f32[64,256]{1,0:T(8,128)S(1)}, f32[64,256]{1,0:T(8,128)S(1)}, u32[]{:S(2)}, u32[]{:S(2)}) %collective-permute-start.10) | collective-permute-done | bytes 65568 | tf_op jit(solution)/shard_map/ppermute | solution.py:287
  50.5 1.4 %shard_map.60 = f32[64,2048]{1,0:T(8,128)} custom-call(f32[64,256]{1,0:T(8,128)S(1)} %collective-permute-done.10.half, f32[3,128,128]{2,1,0:T(8,128)S(1)} %get-tuple-element.111.inner, f32[64,256]{1,0:T(8,128)S(1)} %get-tuple-element.112.before, f32[64,2048]{1,0:T(8,128)S(1)} %shard_map.55.base, bf16[128,2048]{1,0:T(8,128)(2,1)S(1)} %get-tuple-element.116.high_first, ...), custom_call_target="tpu_custom_call" | custom-call | flops 1000000000 | bytes 4000000 | tf_op jit(solution)/shard_map/pallas_call | solution.py:508
  (2 shorter events, 0.1 us)
Async XLA Ops:
  2.2 6.1 %copy-start = (f32[64,2048]{1,0:T(8,128)S(1)}, f32[64,2048]{1,0:T(8,128)}, u32[]{:S(2)}) copy-start(f32[64,2048]{1,0:T(8,128)} %refs_0_) | copy-start | bytes 1572868
  2.2 18.9 %collective-permute-start.1 = (f32[2,256,128]{2,1,0:T(8,128)S(1)}, f32[2,256,128]{2,1,0:T(8,128)S(1)}, u32[]{:S(2)}, u32[]{:S(2)}) collective-permute-start(f32[2,256,128]{2,1,0:T(8,128)S(1)} %get-tuple-element.65), channel_id=1, source_target_pairs={{0,4},{4,8},{8,12},{12,16},{16,20},{20,24},{24,28},{28,0},{1,5},{5... | collective-permute-start | bytes 786440 | tf_op jit(solution)/shard_map/ppermute | solution.py:282
  5.2 15.9 %collective-permute-start.2 = (f32[2,256,128]{2,1,0:T(8,128)S(1)}, f32[2,256,128]{2,1,0:T(8,128)S(1)}, u32[]{:S(2)}, u32[]{:S(2)}) collective-permute-start(f32[2,256,128]{2,1,0:T(8,128)S(1)} %get-tuple-element.66), channel_id=1, source_target_pairs={{0,28},{4,0},{8,4},{12,8},{16,12},{20,16},{24,20},{28,24},{1,29},{... | collective-permute-start | bytes 786440 | tf_op jit(solution)/shard_map/ppermute | solution.py:282
  8.3 13.4 %collective-permute-start = (f32[64,2048]{1,0:T(8,128)S(1)}, f32[64,2048]{1,0:T(8,128)S(1)}, u32[]{:S(2)}, u32[]{:S(2)}) collective-permute-start(f32[64,2048]{1,0:T(8,128)S(1)} %copy-done), channel_id=1, source_target_pairs={{0,2},{1,3},{2,0},{3,1},{4,6},{5,7},{6,4},{7,5},{8,10},{9,11},{10,... | collective-permute-start | bytes 1572872 | tf_op jit(solution)/shard_map/ppermute | solution.py:287
  21.7 3.8 %collective-permute-start.3 = (f32[64,2048]{1,0:T(8,128)S(1)}, f32[64,2048]{1,0:T(8,128)S(1)}, u32[]{:S(2)}, u32[]{:S(2)}) collective-permute-start(f32[64,2048]{1,0:T(8,128)S(1)} %copy-done), channel_id=1, source_target_pairs={{0,1},{1,0},{2,3},{3,2},{4,5},{5,4},{6,7},{7,6},{8,9},{9,8},{10,11... | collective-permute-start | bytes 1572872 | tf_op jit(solution)/shard_map/ppermute | solution.py:287
  21.7 3.8 %collective-permute-start.4 = (f32[64,2048]{1,0:T(8,128)S(1)}, f32[64,2048]{1,0:T(8,128)S(1)}, u32[]{:S(2)}, u32[]{:S(2)}) collective-permute-start(f32[64,2048]{1,0:T(8,128)S(1)} %collective-permute-done.refs_1_), channel_id=1, source_target_pairs={{0,1},{1,0},{2,3},{3,2},{4,5},{5,4},{6,7},{7,6},{8,9},{9,8},{10,11... | collective-permute-start | bytes 1572872 | tf_op jit(solution)/shard_map/ppermute | solution.py:287
  22.2 3.3 %copy-start.1 = (f32[256,256]{1,0:T(8,128)S(1)}, f32[256,256]{1,0:T(8,128)}, u32[]{:S(2)}) copy-start(f32[256,256]{1,0:T(8,128)} %cauchy.1) | copy-start | bytes 786436
  25.5 2.7 %copy-start.2 = (s32[2]{0:T(128)S(1)}, s32[2]{0:T(128)}, u32[]{:S(2)}) copy-start(s32[2]{0:T(128)} %start.11) | copy-start | bytes 28
  26.4 5.5 %collective-permute-start.5 = (f32[64,512]{1,0:T(8,128)S(1)}, f32[64,512]{1,0:T(8,128)S(1)}, u32[]{:S(2)}, u32[]{:S(2)}) collective-permute-start(f32[64,512]{1,0:T(8,128)S(1)} %slice.4), channel_id=1, source_target_pairs={{0,28},{4,0},{8,4},{12,8},{16,12},{20,16},{24,20},{28,24},{1,29},{... | collective-permute-start | bytes 393224 | tf_op jit(solution)/shard_map/ppermute | solution.py:282
  30.7 6.6 %collective-permute-start.7 = (f32[3,128,128]{2,1,0:T(8,128)S(1)}, f32[3,128,128]{2,1,0:T(8,128)S(1)}, u32[]{:S(2)}, u32[]{:S(2)}) collective-permute-start(f32[3,128,128]{2,1,0:T(8,128)S(1)} %get-tuple-element.85.refs_0_), channel_id=1, source_target_pairs={{0,4},{4,0},{8,12},{12,8},{16,20},{20,16},{24,28},{28,24},{1,5},{5... | collective-permute-start | bytes 589832 | tf_op jit(solution)/shard_map/ppermute | solution.py:287
  36.2 4.3 %collective-permute-start.6 = (f32[64,256]{1,0:T(8,128)S(1)}, f32[64,256]{1,0:T(8,128)S(1)}, u32[]{:S(2)}, u32[]{:S(2)}) collective-permute-start(f32[64,256]{1,0:T(8,128)S(1)} %get-tuple-element.95.mine), channel_id=1, source_target_pairs={{0,4},{4,0},{8,12},{12,8},{16,20},{20,16},{24,28},{28,24},{1,5},{5... | collective-permute-start | bytes 196616 | tf_op jit(solution)/shard_map/ppermute | solution.py:287
  37.6 6.5 %collective-permute-start.9 = (f32[3,128,128]{2,1,0:T(8,128)S(1)}, f32[3,128,128]{2,1,0:T(8,128)S(1)}, u32[]{:S(2)}, u32[]{:S(2)}) collective-permute-start(f32[3,128,128]{2,1,0:T(8,128)S(1)} %get-tuple-element.99.refs_0_), channel_id=1, source_target_pairs={{0,8},{4,12},{8,0},{12,4},{16,24},{20,28},{24,16},{28,20},{1,9},{5... | collective-permute-start | bytes 589832 | tf_op jit(solution)/shard_map/ppermute | solution.py:287
  40.7 4.3 %collective-permute-start.8 = (f32[64,256]{1,0:T(8,128)S(1)}, f32[64,256]{1,0:T(8,128)S(1)}, u32[]{:S(2)}, u32[]{:S(2)}) collective-permute-start(f32[64,256]{1,0:T(8,128)S(1)} %get-tuple-element.98.mine), channel_id=1, source_target_pairs={{0,8},{4,12},{8,0},{12,4},{16,24},{20,28},{24,16},{28,20},{1,9},{5... | collective-permute-start | bytes 196616 | tf_op jit(solution)/shard_map/ppermute | solution.py:287
  45.3 5.2 %collective-permute-start.10 = (f32[64,256]{1,0:T(8,128)S(1)}, f32[64,256]{1,0:T(8,128)S(1)}, u32[]{:S(2)}, u32[]{:S(2)}) collective-permute-start(f32[64,256]{1,0:T(8,128)S(1)} %get-tuple-element.110), channel_id=1, source_target_pairs={{0,16},{4,20},{8,24},{12,28},{16,0},{20,4},{24,8},{28,12},{1,17},{... | collective-permute-start | bytes 196616 | tf_op jit(solution)/shard_map/ppermute | solution.py:287
